TPU v7x, 32 devices: a whole 2x2x4 slice. The times are simulated.
32 devices in a mesh: groups: 2 (over y), cols: 4 (over z), rows: 2 (over x), layers: 2 (over core).
Axes of the slice: x: 2, y: 2, z: 4, core: 2. Of those that a mesh axis runs over, the one named last changes fastest.
Arguments:
- state_field: float32 [32, 128, 256], P(('groups', 'layers'), 'cols', 'rows'), parts along dimension 0, may hold values from -6 to 6
- conductivity: float32 [32, 128, 256], P(('groups', 'layers'), 'cols', 'rows'), parts along dimension 0, may hold values from 0.3 to 3
- storage: float32 [32, 128, 256], P(('groups', 'layers'), 'cols', 'rows'), parts along dimension 0, may hold values from 0.05 to 0.5
- gauge_owner: int32 [131072], P(('groups', 'cols', 'rows', 'layers')), parts along dimension 0, may hold values from 0 to 7, as said below
- gauge_cell: int32 [131072], P(('groups', 'cols', 'rows', 'layers')), parts along dimension 0, may hold values from 0 to 32767
- gauge_value: float32 [131072], P(('groups', 'cols', 'rows', 'layers')), parts along dimension 0, may hold values from -6 to 6
- gauge_weight: float32 [131072], P(('groups', 'cols', 'rows', 'layers')), parts along dimension 0, may hold values from 0.5 to 2
- pilot_index: int32 [128, 256], P('cols', 'rows'), may hold values from 0 to 4095, as said below
Outputs:
- adjoint: float32 [32, 128, 256], P(('groups', 'layers'), 'cols', 'rows'), parts along dimension 0
- pilot_gradient: float32 [8192], P(('groups', 'cols', 'rows')), parts along dimension 0
There are 2 independent parts, one for each index of `groups`. A program takes and returns all parts, laid end to end along the dimension named above; an argument that names none is the same for every part. Nothing has to cross between parts.
Inputs may be any that keep to these rules, and one draw needn't show every extreme that they name: `gauge_owner`: within the 4096 rows of one device no owner is named by more than 2048 rows; in every draw, for each layer half, one owner is named by exactly 2048 rows of every device of that half. `pilot_index`: aligned blocks of 4 x 2 cell columns share one pilot point and every pilot point covers exactly one such block; pilot p belongs to owner p // 512; the block of 32 x 128 columns of one device holds exactly 512 // (4 * 2) pilot points of each owner.
All inputs are finite; a program needn't handle non-finite values.
Results may differ from a plain program's by a relative error of at most 0.0001.
Values sent between devices are 32-bit elements; how exact they have to be, the bound alone decides.
No kernel may reach another device: no remote copies, remote signals or barrier semaphores. Data moves between devices by JAX's collectives and lax.ppermute only.
A program may use at most 64 MiB of HBM per device.

v0:
```python
import jax
import jax.numpy as jnp
from jax import lax
from jax.sharding import PartitionSpec as P

ITERS = 8


def with_halo(block, sides, width):
    for axis, dim in sides:
        count = lax.axis_size(axis)
        forward = [(i, i + 1) for i in range(count - 1)]
        backward = [(target, source) for source, target in forward]
        low = lax.ppermute(
            lax.slice_in_dim(block, block.shape[dim] - width, None, axis=dim), axis, forward
        )
        high = lax.ppermute(lax.slice_in_dim(block, 0, width, axis=dim), axis, backward)
        block = jnp.concatenate([low, block, high], axis=dim)
    return block


def neighbours(padded):
    return [
        padded[2:, 1:-1, 1:-1],
        padded[:-2, 1:-1, 1:-1],
        padded[1:-1, 2:, 1:-1],
        padded[1:-1, :-2, 1:-1],
        padded[1:-1, 1:-1, 2:],
        padded[1:-1, 1:-1, :-2],
    ]


def on_device(
    state_field,
    conductivity,
    storage,
    gauge_owner,
    gauge_cell,
    gauge_value,
    gauge_weight,
    pilot_index,
):
    fixed = with_halo(
        jnp.stack([conductivity, state_field]), (("cols", 2), ("rows", 3), ("layers", 1)), 1
    )
    face_weights = [0.5 * (conductivity + other) for other in neighbours(fixed[0])]
    state_sides = neighbours(fixed[1])
    diagonal = storage
    for weight_one in face_weights:
        diagonal = diagonal + weight_one

    def squares(field):
        return lax.psum(jnp.sum(field * field), ("cols", "rows", "layers"))

    peer_count = lax.axis_size("cols") * lax.axis_size("rows")
    gauge_count = gauge_owner.shape[0]
    capacity = 4 * gauge_count // peer_count
    one_hot = (gauge_owner[:, None] == jnp.arange(peer_count, dtype=jnp.int32)[None, :]).astype(
        jnp.int32
    )
    earlier = jnp.cumsum(one_hot, axis=0) - one_hot
    ranking = jnp.sum(earlier * one_hot, axis=1)
    position = gauge_owner * capacity + ranking
    payload = (
        jnp.zeros((2, peer_count * capacity), jnp.float32)
        .at[:, position]
        .set(jnp.stack([gauge_value, gauge_weight]))
    )
    targets = (
        jnp.zeros((1, peer_count * capacity), jnp.int32).at[:, position].set(gauge_cell[None, :])
    )
    got_payload, got_targets = (
        lax.all_to_all(
            payload.reshape(2, peer_count, capacity),
            ("cols", "rows"),
            split_axis=1,
            concat_axis=1,
            tiled=True,
        ),
        lax.all_to_all(
            targets.reshape(1, peer_count, capacity),
            ("cols", "rows"),
            split_axis=1,
            concat_axis=1,
            tiled=True,
        ),
    )
    got_payload = got_payload.reshape(2, -1)
    received_cells = got_targets.reshape(-1)
    flat_state = state_field.reshape(-1)
    misfit = got_payload[1] * (flat_state[received_cells] - got_payload[0])
    source_term = (
        jnp.zeros_like(flat_state).at[received_cells].add(misfit).reshape(state_field.shape)
    )
    adjoint = jnp.zeros_like(source_term)
    residual = source_term
    direction = source_term
    norm_now = squares(residual)
    for iteration in range(ITERS):
        padded = with_halo(direction, (("cols", 1), ("rows", 2), ("layers", 0)), 1)
        result = diagonal * direction
        for operate_weight_one, operate_other in zip(face_weights, neighbours(padded)):
            result = result - operate_weight_one * operate_other
        step_length = norm_now / lax.psum(jnp.sum(direction * result), ("cols", "rows", "layers"))
        adjoint = adjoint + step_length * direction
        residual = residual - step_length * result
        norm_next = squares(residual)
        direction = residual + norm_next / norm_now * direction
        norm_now = norm_next
    adjoint_padded = with_halo(adjoint, (("cols", 1), ("rows", 2), ("layers", 0)), 1)
    total = jnp.zeros_like(adjoint)
    for adjoint_side, state_side in zip(neighbours(adjoint_padded), state_sides):
        total = total + (adjoint - adjoint_side) * (state_field - state_side)
    cell_gradient = -0.5 * conductivity * total
    column_sums = jnp.sum(cell_gradient, axis=0)
    width_x = column_sums.shape[0]
    width_y = column_sums.shape[1]
    blocks = width_x * width_y // 8
    dense = (
        jnp.zeros((blocks * peer_count,), jnp.float32)
        .at[pilot_index.reshape(-1)]
        .add(column_sums.reshape(-1))
    )
    owned = lax.psum_scatter(dense, ("cols", "rows"), scatter_dimension=0, tiled=True)
    pilot_gradient = lax.psum(owned, "layers")
    return (adjoint, pilot_gradient)


def solution(mesh):
    return jax.shard_map(
        on_device,
        mesh=mesh,
        in_specs=(
            P(("groups", "layers"), "cols", "rows"),
            P(("groups", "layers"), "cols", "rows"),
            P(("groups", "layers"), "cols", "rows"),
            P(("groups", "cols", "rows", "layers")),
            P(("groups", "cols", "rows", "layers")),
            P(("groups", "cols", "rows", "layers")),
            P(("groups", "cols", "rows", "layers")),
            P("cols", "rows"),
        ),
        out_specs=(P(("groups", "layers"), "cols", "rows"), P(("groups", "cols", "rows"))),
        check_vma=False,
    )
```

profile of v0, /device:TPU:0, one launch (start us, length us, event | category | flops | bytes accessed | tf_op | source)
XLA Modules:
  0.0 1013.7 jit_solution(14229054544719391086)
XLA Ops:
  1.5 4.9 collective-permute-start
  12.9 16.3 %scatter_custom_fusion = s32[16384]{0:T(1024)} fusion(s32[4096]{0:T(1024)S(1)} %compare_select_fusion.2, s32[4096]{0:T(1024)} %param.12, s32[]{:T(128)} %constant.9.clone.1), kind=kCustom, calls=%fused_computation.416 | custom fusion | bytes 66048 | tf_op jit(solution)/shard_map/scatter | solution.py:70
  29.2 6.9 all-to-all-start
  37.2 3.9 collective-permute-start.2
  45.3 14.6 %scatter_custom_fusion.1 = f32[2,16384]{0,1:T(8,128)} fusion(s32[4096]{0:T(1024)S(1)} %compare_select_fusion.2, f32[4096,2]{1,0:T(8,128)} %copy.12, f32[]{:T(128)} %constant.8.clone.1), kind=kCustom, calls=%fused_computation.5 | custom fusion | bytes 131584 | tf_op jit(solution)/shard_map/scatter | solution.py:67
  59.9 5.8 copy.13
  68.6 6.6 all-to-all-start.1
  75.3 90.5 %gather_fusion = f32[16384]{0:T(1024)S(1)} fusion(f32[32768]{0:T(1024)S(1)} %bitcast.45, s32[16384]{0:T(1024)S(1)} %broadcast_clamp_fusion), kind=kCustom, calls=%fused_computation | custom fusion | bytes 196608 | tf_op jit(solution)/shard_map/gather | solution.py:91
  166.0 109.3 %scatter_custom_fusion.2 = f32[32768]{0:T(1024)S(1)} fusion(s32[16384]{0:T(1024)S(1)} %bitcast.62, f32[16384]{0:T(1024)S(1)} %subtract_multiply_fusion, f32[]{:T(128)} %constant.8.clone.1), kind=kCustom, calls=%fused_computation.366 | custom fusion | flops 16384 | bytes 131076 | tf_op jit(solution)/shard_map/scatter-add | solution.py:93
  275.4 3.9 collective-permute-start.6
  280.9 3.8 collective-permute-done.7
  284.8 3.8 collective-permute-start.8
  291.5 4.4 collective-permute-done.9
  302.2 30.8 %all-reduce.1 = (f32[]{:T(128)}, f32[]{:T(128)}) all-reduce(f32[]{:T(128)} %multiply_reduce_fusion.14, f32[]{:T(128)} %get-tuple-element.26), channel_id=1, replica_groups=mesh['groups'=2,'cols'=4,'rows'=2,'layers'=2] {'cols','rows','layers'}, use_global_device_ids=true, to_apply=%region_7.8 | all-reduce | flops 2 | bytes 16 | tf_op jit(solution)/shard_map/psum | solution.py:53
  335.0 30.1 %psum.121 = f32[]{:T(128)} all-reduce(f32[]{:T(128)} %multiply_reduce_fusion.12), channel_id=1, replica_groups=mesh['groups'=2,'cols'=4,'rows'=2,'layers'=2] {'cols','rows','layers'}, use_global_device_ids=true, to_apply=%region_11.12 | all-reduce | flops 1 | bytes 8 | tf_op jit(solution)/shard_map/psum | solution.py:53
  369.1 4.2 collective-permute-done.13
  377.5 4.4 collective-permute-done.15
  383.3 3.0 collective-permute-start.17
  388.1 30.4 %psum.122 = f32[]{:T(128)} all-reduce(f32[]{:T(128)} %get-tuple-element.24), channel_id=1, replica_groups=mesh['groups'=2,'cols'=4,'rows'=2,'layers'=2] {'cols','rows','layers'}, use_global_device_ids=true, to_apply=%region_13.14 | all-reduce | flops 1 | bytes 8 | tf_op jit(solution)/shard_map/psum | solution.py:104
  420.5 30.1 %psum.123 = f32[]{:T(128)} all-reduce(f32[]{:T(128)} %get-tuple-element.22), channel_id=1, replica_groups=mesh['groups'=2,'cols'=4,'rows'=2,'layers'=2] {'cols','rows','layers'}, use_global_device_ids=true, to_apply=%region_15.16 | all-reduce | flops 1 | bytes 8 | tf_op jit(solution)/shard_map/psum | solution.py:53
  454.6 4.2 collective-permute-done.19
  463.1 4.4 collective-permute-done.21
  468.9 3.0 collective-permute-start.23
  473.7 30.4 %psum.124 = f32[]{:T(128)} all-reduce(f32[]{:T(128)} %get-tuple-element.20), channel_id=1, replica_groups=mesh['groups'=2,'cols'=4,'rows'=2,'layers'=2] {'cols','rows','layers'}, use_global_device_ids=true, to_apply=%region_17.18 | all-reduce | flops 1 | bytes 8 | tf_op jit(solution)/shard_map/psum | solution.py:104
  506.1 30.3 %psum.125 = f32[]{:T(128)} all-reduce(f32[]{:T(128)} %get-tuple-element.18), channel_id=1, replica_groups=mesh['groups'=2,'cols'=4,'rows'=2,'layers'=2] {'cols','rows','layers'}, use_global_device_ids=true, to_apply=%region_19.20 | all-reduce | flops 1 | bytes 8 | tf_op jit(solution)/shard_map/psum | solution.py:53
  540.4 4.2 collective-permute-done.25
  548.8 4.4 collective-permute-done.27
  559.4 30.4 %psum.126 = f32[]{:T(128)} all-reduce(f32[]{:T(128)} %get-tuple-element.16), channel_id=1, replica_groups=mesh['groups'=2,'cols'=4,'rows'=2,'layers'=2] {'cols','rows','layers'}, use_global_device_ids=true, to_apply=%region_21.22 | all-reduce | flops 1 | bytes 8 | tf_op jit(solution)/shard_map/psum | solution.py:104
  591.8 30.1 %psum.127 = f32[]{:T(128)} all-reduce(f32[]{:T(128)} %get-tuple-element.14), channel_id=1, replica_groups=mesh['groups'=2,'cols'=4,'rows'=2,'layers'=2] {'cols','rows','layers'}, use_global_device_ids=true, to_apply=%region_23.24 | all-reduce | flops 1 | bytes 8 | tf_op jit(solution)/shard_map/psum | solution.py:53
  625.9 4.2 collective-permute-done.31
  634.5 4.4 collective-permute-done.33
  645.1 30.4 %psum.128 = f32[]{:T(128)} all-reduce(f32[]{:T(128)} %get-tuple-element.12), channel_id=1, replica_groups=mesh['groups'=2,'cols'=4,'rows'=2,'layers'=2] {'cols','rows','layers'}, use_global_device_ids=true, to_apply=%region_25.26 | all-reduce | flops 1 | bytes 8 | tf_op jit(solution)/shard_map/psum | solution.py:104
  677.5 30.1 %psum.129 = f32[]{:T(128)} all-reduce(f32[]{:T(128)} %get-tuple-element.10), channel_id=1, replica_groups=mesh['groups'=2,'cols'=4,'rows'=2,'layers'=2] {'cols','rows','layers'}, use_global_device_ids=true, to_apply=%region_27.28 | all-reduce | flops 1 | bytes 8 | tf_op jit(solution)/shard_map/psum | solution.py:53
  711.6 4.2 collective-permute-done.37
  720.1 4.4 collective-permute-done.39
  730.7 30.4 %psum.130 = f32[]{:T(128)} all-reduce(f32[]{:T(128)} %get-tuple-element.8), channel_id=1, replica_groups=mesh['groups'=2,'cols'=4,'rows'=2,'layers'=2] {'cols','rows','layers'}, use_global_device_ids=true, to_apply=%region_29.30 | all-reduce | flops 1 | bytes 8 | tf_op jit(solution)/shard_map/psum | solution.py:104
  763.1 30.1 %psum.131 = f32[]{:T(128)} all-reduce(f32[]{:T(128)} %get-tuple-element.6), channel_id=1, replica_groups=mesh['groups'=2,'cols'=4,'rows'=2,'layers'=2] {'cols','rows','layers'}, use_global_device_ids=true, to_apply=%region_31.32 | all-reduce | flops 1 | bytes 8 | tf_op jit(solution)/shard_map/psum | solution.py:53
  797.2 4.2 collective-permute-done.43
  805.6 4.4 collective-permute-done.45
  816.2 30.4 %psum.132 = f32[]{:T(128)} all-reduce(f32[]{:T(128)} %get-tuple-element.4), channel_id=1, replica_groups=mesh['groups'=2,'cols'=4,'rows'=2,'layers'=2] {'cols','rows','layers'}, use_global_device_ids=true, to_apply=%region_33.34 | all-reduce | flops 1 | bytes 8 | tf_op jit(solution)/shard_map/psum | solution.py:104
  848.6 30.1 %psum.133 = f32[]{:T(128)} all-reduce(f32[]{:T(128)} %multiply_reduce_fusion), channel_id=1, replica_groups=mesh['groups'=2,'cols'=4,'rows'=2,'layers'=2] {'cols','rows','layers'}, use_global_device_ids=true, to_apply=%region_35.36 | all-reduce | flops 1 | bytes 8 | tf_op jit(solution)/shard_map/psum | solution.py:53
  882.7 4.2 collective-permute-done.49
  891.2 4.4 collective-permute-done.51
  901.8 30.4 %psum.134 = f32[]{:T(128)} all-reduce(f32[]{:T(128)} %fusion.27), channel_id=1, replica_groups=mesh['groups'=2,'cols'=4,'rows'=2,'layers'=2] {'cols','rows','layers'}, use_global_device_ids=true, to_apply=%region_37.38 | all-reduce | flops 1 | bytes 8 | tf_op jit(solution)/shard_map/psum | solution.py:104
  936.3 4.2 collective-permute-done.55
  944.8 4.4 collective-permute-done.57
  955.4 22.3 %scatter_custom_fusion.3 = f32[4096]{0:T(1024)S(1)} fusion(s32[4096]{0:T(1024)S(1)} %bitcast.69, f32[4096]{0:T(1024)S(1)} %bitcast.66, f32[]{:T(128)} %constant.8.clone.1), kind=kCustom, calls=%fused_computation.420 | custom fusion | flops 4096 | bytes 16388 | tf_op jit(solution)/shard_map/scatter-add | solution.py:122
  977.6 33.0 %all-reduce = f32[4096]{0:T(1024)S(1)} all-reduce(f32[4096]{0:T(1024)S(1)} %scatter_custom_fusion.3), channel_id=2, replica_groups=mesh['groups'=2,'cols'=4,'rows'=2,'layers'=2] {'cols','rows'}, use_global_device_ids=true, to_apply=%region_40.41.clone | all-reduce | flops 4096 | bytes 32768
  (194 shorter events, 131.6 us)
Async XLA Ops:
  1.5 34.6 %collective-permute-start = (f32[2,8,1,128]{3,2,1,0:T(1,128)S(1)}, f32[2,8,1,128]{3,2,1,0:T(1,128)S(1)}, u32[]{:S(2)}, u32[]{:S(2)}) collective-permute-start(f32[2,8,1,128]{3,2,1,0:T(1,128)S(1)} %get-tuple-element.58), channel_id=1, source_target_pairs={{0,4},{4,8},{8,12},{1,5},{5,9},{9,13},{2,6},{6,10},{10,14},{3,7},{... | collective-permute-start | bytes 24584 | tf_op jit(solution)/shard_map/ppermute | solution.py:14
  6.4 29.7 %collective-permute-start.1 = (f32[2,8,1,128]{3,2,1,0:T(1,128)S(1)}, f32[2,8,1,128]{3,2,1,0:T(1,128)S(1)}, u32[]{:S(2)}, u32[]{:S(2)}) collective-permute-start(f32[2,8,1,128]{3,2,1,0:T(1,128)S(1)} %get-tuple-element.59), channel_id=1, source_target_pairs={{4,0},{8,4},{12,8},{5,1},{9,5},{13,9},{6,2},{10,6},{14,10},{7,3},{... | collective-permute-start | bytes 24584 | tf_op jit(solution)/shard_map/ppermute | solution.py:17
  29.2 39.4 %all-to-all-start = ((s32[1,8,2048]{2,0,1:T(1,128)}), s32[1,8,2048]{2,0,1:T(1,128)S(1)}, u32[]{:S(2)}, u32[]{:S(2)}) async-start(s32[1,8,2048]{2,0,1:T(1,128)} %bitcast.2), calls=%async_computation | async-start | bytes 131072 | tf_op jit(solution)/shard_map/all_to_all | solution.py:80
  37.2 28.5 %collective-permute-start.2 = (f32[2,8,34,1]{3,2,1,0:T(8,128)S(1)}, f32[2,8,34,1]{3,2,1,0:T(8,128)S(1)}, u32[]{:S(2)}, u32[]{:S(2)}) collective-permute-start(f32[2,8,34,1]{3,2,1,0:T(8,128)S(1)} %get-tuple-element.56), channel_id=1, source_target_pairs={{0,2},{1,3},{4,6},{5,7},{8,10},{9,11},{12,14},{13,15},{16,18},{17,... | collective-permute-start | bytes 6536 | tf_op jit(solution)/shard_map/ppermute | solution.py:14
  41.2 24.6 %collective-permute-start.3 = (f32[2,8,34,1]{3,2,1,0:T(8,128)S(1)}, f32[2,8,34,1]{3,2,1,0:T(8,128)S(1)}, u32[]{:S(2)}, u32[]{:S(2)}) collective-permute-start(f32[2,8,34,1]{3,2,1,0:T(8,128)S(1)} %get-tuple-element.57), channel_id=1, source_target_pairs={{2,0},{3,1},{6,4},{7,5},{10,8},{11,9},{14,12},{15,13},{18,16},{19,... | collective-permute-start | bytes 6536 | tf_op jit(solution)/shard_map/ppermute | solution.py:17
  66.0 214.6 %collective-permute-start.4 = (f32[2,1,34,130]{3,2,1,0:T(8,128)S(1)}, f32[2,1,34,130]{3,2,1,0:T(8,128)S(1)}, u32[]{:S(2)}, u32[]{:S(2)}) collective-permute-start(f32[2,1,34,130]{3,2,1,0:T(8,128)S(1)} %get-tuple-element.34), channel_id=1, source_target_pairs={{0,1},{2,3},{4,5},{6,7},{8,9},{10,11},{12,13},{14,15},{16,17},{18,... | collective-permute-start | bytes 106088 | tf_op jit(solution)/shard_map/ppermute | solution.py:14
  67.3 213.3 %collective-permute-start.5 = (f32[2,1,34,130]{3,2,1,0:T(8,128)S(1)}, f32[2,1,34,130]{3,2,1,0:T(8,128)S(1)}, u32[]{:S(2)}, u32[]{:S(2)}) collective-permute-start(f32[2,1,34,130]{3,2,1,0:T(8,128)S(1)} %get-tuple-element.35), channel_id=1, source_target_pairs={{1,0},{3,2},{5,4},{7,6},{9,8},{11,10},{13,12},{15,14},{17,16},{19,... | collective-permute-start | bytes 106088 | tf_op jit(solution)/shard_map/ppermute | solution.py:17
  68.6 97.3 %all-to-all-start.1 = ((f32[2,8,2048]{2,0,1:T(2,128)}), f32[2,8,2048]{2,0,1:T(2,128)S(1)}, u32[]{:S(2)}, u32[]{:S(2)}) async-start(f32[2,8,2048]{2,0,1:T(2,128)} %copy.13), calls=%async_computation.1 | async-start | bytes 262144 | tf_op jit(solution)/shard_map/all_to_all | solution.py:73
  275.4 5.6 collective-permute-start.6
  279.2 5.5 collective-permute-start.7
  284.8 6.6 collective-permute-start.8
  288.6 7.2 collective-permute-start.9
  296.0 5.0 collective-permute-start.10
  367.8 5.5 collective-permute-start.13
  373.4 4.1 collective-permute-start.14
  374.7 7.2 collective-permute-start.15
  382.0 4.3 collective-permute-start.16
  383.3 3.9 collective-permute-start.17
  453.3 5.5 collective-permute-start.19
  458.9 4.1 collective-permute-start.20
  460.3 7.2 collective-permute-start.21
  467.6 4.3 collective-permute-start.22
  468.9 3.9 collective-permute-start.23
  539.0 5.5 collective-permute-start.25
  544.7 4.1 collective-permute-start.26
  546.0 7.2 collective-permute-start.27
  553.3 4.3 collective-permute-start.28
  624.6 5.5 collective-permute-start.31
  630.3 4.2 collective-permute-start.32
  631.7 7.2 collective-permute-start.33
  639.0 4.3 collective-permute-start.34
  710.3 5.5 collective-permute-start.37
  715.9 4.1 collective-permute-start.38
  717.2 7.2 collective-permute-start.39
  724.6 4.3 collective-permute-start.40
  795.9 5.5 collective-permute-start.43
  801.5 4.1 collective-permute-start.44
  802.8 7.2 collective-permute-start.45
  810.1 4.3 collective-permute-start.46
  881.4 5.5 collective-permute-start.49
  887.0 4.1 collective-permute-start.50
  888.4 7.2 collective-permute-start.51
  895.7 4.3 collective-permute-start.52
  935.0 5.5 collective-permute-start.55
  940.6 4.1 collective-permute-start.56
  941.9 7.2 collective-permute-start.57
  949.3 5.6 collective-permute-start.58
  950.6 4.3 collective-permute-start.59
  (20 other events, 1037.8 us)
where the time goes:
time: 1020 us; the launch traced here: 1010 us
  blocking collectives  491 us (48%)
  other arithmetic  154 us (15%)
  local copies, waits for them, and re-layouts  132 us (13%)
  starting transfers between devices  118 us (12%)
  waiting for transfers between devices  96.7 us (9%)
  between operations  22.4 us (2%)
    psum x8, blocking collectives, squares(): return lax.psum(jnp.sum(field * field), ('cols', 'rows', 'layers'))  242 us
    psum x7, blocking collectives, on_device(): lax.psum(jnp.sum(direction * result), ('cols', 'rows', 'layers'))  213 us
    scatter-add x1, other arithmetic, on_device(): jnp.zeros_like(flat_state).at[received_cells].add(misfit)  109 us
    gather x1, local copies, waits for them, and re-layouts, on_device(): misfit = got_payload[1] * (flat_state[received_cells] - got_payload[0])  90.5 us
    ppermute x30, waiting for transfers between devices, with_halo(): lax.ppermute(lax.slice_in_dim(block, 0, width, axis=dim), axis, backward)  76.9 us
    ppermute x30, starting transfers between devices, with_halo(): lax.ppermute(lax.slice_in_dim(block, block.shape[dim] - width, None, axis...  65.9 us
    ppermute x30, starting transfers between devices, with_halo(): lax.ppermute(lax.slice_in_dim(block, 0, width, axis=dim), axis, backward)  38.8 us
    unnamed x1, blocking collectives  33 us
  transfers between devices with their start and end apart: 62, of which 35 were waited for; matrix products, arithmetic and copies ran while one was open for 24% of the time, Pallas kernels for 0%

commit v1 on v0

v1 whole, which is shorter than its diff:
```python
import functools

import jax
import jax.numpy as jnp
from jax import lax
from jax.experimental import pallas as pl
from jax.experimental.pallas import tpu as pltpu
from jax.sharding import PartitionSpec as P

ITERS = 8
HALO = 8
LANES = 128
LANE_BITS = 7
GRID_AXES = ("cols", "rows", "layers")
PEER_AXES = ("cols", "rows")
NT = (((1,), (1,)), ((), ()))
EXACT = lax.Precision.HIGHEST
VMEM_BYTES = 50 * 1024 * 1024


def kernel_call(body, out_shape, scratch=()):
    return functools.partial(
        pl.pallas_call,
        body,
        out_shape=out_shape,
        scratch_shapes=list(scratch),
        compiler_params=pltpu.CompilerParams(vmem_limit_bytes=VMEM_BYTES),
    )


VMEM = pl.BlockSpec(memory_space=pltpu.VMEM)
SMEM = pl.BlockSpec(memory_space=pltpu.SMEM)


def pieces_of(x):
    first = x.astype(jnp.bfloat16).astype(jnp.float32)
    rest = x - first
    second = rest.astype(jnp.bfloat16).astype(jnp.float32)
    return first, second, rest - second


def row_iota(rows, lanes=LANES):
    return lax.broadcasted_iota(jnp.int32, (rows, lanes), 0)


def lane_iota(rows, lanes=LANES):
    return lax.broadcasted_iota(jnp.int32, (rows, lanes), 1)


def picked(mask, row):
    return jnp.where(mask, row, jnp.zeros_like(row)).astype(jnp.bfloat16)


def mm(a, b, dims=(((1,), (0,)), ((), ())), precision=None):
    return lax.dot_general(a, b, dims, precision=precision, preferred_element_type=jnp.float32)


def route_body(peers, capacity, owner_ref, cell_ref, value_ref, weight_ref, out_ref):
    rows = owner_ref.shape[0]
    owner = owner_ref[...]
    ra, ca = row_iota(LANES, 2 * LANES), lane_iota(LANES, 2 * LANES)
    earlier_lane = jnp.where((ra < ca) | (ca >= LANES), 1.0, 0.0).astype(jnp.bfloat16)
    earlier_row = jnp.where(row_iota(rows, rows) > lane_iota(rows, rows), 1.0, 0.0).astype(
        jnp.bfloat16
    )

    def rank_of(peer, rank):
        hit = owner == peer
        counts = mm(jnp.where(hit, 1.0, 0.0).astype(jnp.bfloat16), earlier_lane)
        before = mm(earlier_row, counts[:, LANES:].astype(jnp.bfloat16))
        return rank + jnp.where(hit, counts[:, :LANES] + before, 0.0)

    rank = jnp.zeros((rows, LANES), jnp.float32)
    if peers <= 16:
        for peer in range(peers):
            rank = rank_of(peer, rank)
    else:
        rank = lax.fori_loop(0, peers, rank_of, rank)
    position = owner * capacity + rank.astype(jnp.int32)
    slot_row = lax.shift_right_logical(position, LANE_BITS)
    slot_lane = position & (LANES - 1)
    cell = cell_ref[...]
    columns = [
        lax.shift_right_logical(cell, LANE_BITS).astype(jnp.float32),
        (cell & (LANES - 1)).astype(jnp.float32),
        *pieces_of(value_ref[...]),
        *pieces_of(weight_ref[...]),
    ]
    slot_rows = peers * capacity // LANES
    rows_at, lanes_at = row_iota(slot_rows), row_iota(LANES)
    total = jnp.zeros((slot_rows, len(columns) * LANES), jnp.float32)
    step = 8
    for start in range(0, rows, step):
        left, right = [], [[] for _ in columns]
        for r in range(start, start + step):
            left.append(
                jnp.where(rows_at == slot_row[r : r + 1], 1.0, 0.0).astype(jnp.bfloat16)
            )
            lane_hit = lanes_at == slot_lane[r : r + 1]
            for q, column in enumerate(columns):
                right[q].append(picked(lane_hit, column[r : r + 1]))
        right = jnp.concatenate([jnp.concatenate(q, axis=1) for q in right], axis=0)
        total = total + mm(jnp.concatenate(left, axis=1), right, NT)
    part = [total[:, q * LANES : (q + 1) * LANES] for q in range(len(columns))]
    fields = [
        part[0] * LANES + part[1],
        part[2] + part[3] + part[4],
        part[5] + part[6] + part[7],
    ]
    each = capacity // LANES
    for peer in range(peers):
        for q, field in enumerate(fields):
            out_ref[peer, q * each : (q + 1) * each, :] = field[peer * each : (peer + 1) * each]


def source_body(got_ref, state_ref, out_ref, acc_ref):
    peers, each = got_ref.shape[0], got_ref.shape[1] // 3
    cells = state_ref.shape[0]
    state_t = jnp.concatenate(
        [p.astype(jnp.bfloat16) for p in pieces_of(jnp.transpose(state_ref[...]))], axis=0
    )
    acc_ref[...] = jnp.zeros_like(acc_ref)
    rows_at, lanes_at = row_iota(cells), row_iota(LANES)

    def one_peer(peer, carry):
        cell = got_ref[peer, 0:each, :].astype(jnp.int32)
        value = got_ref[peer, each : 2 * each, :]
        weight = got_ref[peer, 2 * each : 3 * each, :]
        high = lax.shift_right_logical(cell, LANE_BITS)
        low = cell & (LANES - 1)
        row_hits = jnp.concatenate(
            [
                jnp.where(rows_at == high[r : r + 1], 1.0, 0.0).astype(jnp.bfloat16)
                for r in range(each)
            ],
            axis=1,
        )
        heads = mm(state_t, row_hits)
        right = [[], [], []]
        for r in range(each):
            lane_hit = lanes_at == low[r : r + 1]
            here = heads[:, r * LANES : (r + 1) * LANES]
            head = here[:LANES] + here[LANES : 2 * LANES] + here[2 * LANES :]
            head = jnp.sum(jnp.where(lane_hit, head, 0.0), axis=0, keepdims=True)
            misfit = weight[r : r + 1] * (head - value[r : r + 1])
            for q, piece in enumerate(pieces_of(misfit)):
                right[q].append(picked(lane_hit, piece))
        right = jnp.concatenate([jnp.concatenate(q, axis=1) for q in right], axis=0)
        acc_ref[...] += mm(row_hits, right, NT)
        return carry

    lax.fori_loop(0, peers, one_peer, 0)
    out_ref[...] = (
        acc_ref[:, :LANES] + acc_ref[:, LANES : 2 * LANES] + acc_ref[:, 2 * LANES :]
    )


def all_sum(x):
    while x.ndim > 2:
        x = jnp.sum(x, axis=0)
    return jnp.sum(jnp.sum(x, axis=0, keepdims=True), axis=1, keepdims=True)


def safe_ratio(a, b):
    return jnp.where(b > 0.0, a / jnp.where(b > 0.0, b, 1.0), 0.0)


def local_body(source_ref, conductivity_ref, storage_ref, out_ref):
    c = conductivity_ref[...]

    def up(x, axis):
        if axis == 0:
            return jnp.concatenate([x[1:], x[:1]], axis=0)
        return pltpu.roll(x, x.shape[axis] - 1, axis)

    def down(x, axis):
        if axis == 0:
            return jnp.concatenate([x[-1:], x[:-1]], axis=0)
        return pltpu.roll(x, 1, axis)

    faces = [0.5 * (c + up(c, axis)) for axis in range(3)]
    diagonal = storage_ref[...]
    for axis, face in enumerate(faces):
        diagonal = diagonal + face + down(face, axis)

    now, last = source_ref[...], None
    norm_last = None
    lanes = lane_iota(1)
    out = jnp.zeros((1, LANES), jnp.float32)
    for k in range(ITERS):
        image = diagonal * now
        for axis, face in enumerate(faces):
            image = image - face * up(now, axis) - down(face * now, axis)
        norm = all_sum(now * now)
        alpha = safe_ratio(all_sum(now * image), norm)
        beta = norm if k == 0 else safe_ratio(norm, norm_last)
        out = jnp.where(lanes == k, alpha, out)
        out = jnp.where(lanes == ITERS + k, beta, out)
        if k < ITERS - 1:
            following = image - alpha * now
            if k:
                following = following - beta * last
            now, last, norm_last = following, now, norm
    out_ref[...] = jnp.broadcast_to(out, out_ref.shape)


def common_coefficients(got):
    lanes = lane_iota(got.shape[0])
    used = lanes < ITERS
    alpha = jnp.where(used, got, 0.0)
    beta = jnp.where(used, pltpu.roll(got, LANES - ITERS, 1), 0.0)
    weight = jnp.where(used, beta, 1.0)
    for shift in (1, 2, 4):
        weight = weight * jnp.where(lanes >= shift, pltpu.roll(weight, shift, 1), 1.0)
    weight = jnp.where(used, weight, 0.0)
    beta_next = jnp.where(lanes < ITERS - 1, pltpu.roll(beta, LANES - 1, 1), 0.0)
    now = jnp.where(lanes == 0, 1.0, 0.0)
    last = jnp.zeros_like(now)
    alphas, gammas = [], []
    norm_last = None
    for k in range(ITERS):
        image = (
            jnp.where((lanes >= 1) & used, pltpu.roll(now, 1, 1), 0.0)
            + alpha * now
            + beta_next * pltpu.roll(now, LANES - 1, 1)
        )
        norm = all_sum(weight * now * now)
        a = safe_ratio(all_sum(weight * now * image), norm)
        alphas.append(a)
        g = None
        if k:
            g = safe_ratio(norm, norm_last)
            gammas.append(g)
        following = image - a * now
        if k:
            following = following - g * last
        now, last, norm_last = following, now, norm
    return alphas, gammas


def unpack(layer, field, own, other, low, high, sides, padded, strip):
    nz, nx = own.shape[-3], own.shape[-2]
    place = jnp.where(
        lane_iota(2 * HALO)
        == jnp.where(
            row_iota(2 * HALO) < HALO, row_iota(2 * HALO), row_iota(2 * HALO) + LANES - 2 * HALO
        ),
        1.0,
        0.0,
    )
    spread = mm(jnp.transpose(sides[field]), place, precision=EXACT)
    strip[...] = spread.reshape(strip.shape)
    for i in range(nz):
        j = jnp.where(layer == 0, i, nz - 1 - i)
        for half, block in ((0, own), (1, other)):
            to = half * nz + i
            padded[to, HALO : HALO + nx, :LANES] = block[field, j]
            padded[to, :HALO, :LANES] = low[field, half * nz + j]
            padded[to, HALO + nx :, :LANES] = high[field, half * nz + j]
            padded[to, :, LANES:] = strip[half * nz + j]


def basis_body(
    peers,
    layer_ref,
    f_own, f_other, f_low, f_high, f_sides,
    b_own, b_other, b_low, b_high, b_sides,
    got_ref, pilot_ref,
    own_ref, send_ref,
    c_pad, s_pad, h_pad, diag, wx, wy, wz, basis, strip, grads,
):
    layer = layer_ref[0]
    nz, nx = f_own.shape[1], f_own.shape[2]
    planes, width = c_pad.shape[0], c_pad.shape[1]
    for field, target in ((0, c_pad), (1, s_pad), (2, h_pad)):
        unpack(layer, field, f_own, f_other, f_low, f_high, f_sides, target, strip)
    unpack(layer, 0, b_own, b_other, b_low, b_high, b_sides, basis.at[0], strip)

    def right(x):
        return pltpu.roll(x, x.shape[1] - 1, 1)

    def left(x):
        return pltpu.roll(x, 1, 1)

    def fore(x):
        return pltpu.roll(x, x.shape[0] - 1, 0)

    def back(x):
        return pltpu.roll(x, 1, 0)

    def joined(a, b):
        return jnp.where((a > 0.0) & (b > 0.0), 0.5 * (a + b), 0.0)

    for z in range(planes):
        c = c_pad[z]
        cf, cr = fore(c), right(c)
        total = cf + back(c) + cr + left(c)
        wx[z] = joined(c, cf)
        wy[z] = joined(c, cr)
        if z + 1 < planes:
            wz[z] = joined(c, c_pad[z + 1])
            total = total + c_pad[z + 1]
        if z:
            total = total + c_pad[z - 1]
        diag[z] = s_pad[z] + 3.0 * c + 0.5 * total

    alphas, gammas = common_coefficients(got_ref[...])
    betas = [None] + [jnp.sqrt(g) for g in gammas] + [jnp.sqrt(gammas[-1])]
    scales = [None] + [safe_ratio(jnp.ones_like(b), b) for b in betas[1:]]
    for k in range(ITERS):
        for z in range(nz + ITERS - 1 - k):
            v = basis[k, z]
            wxz, wyz = wx[z], wy[z]
            image = (diag[z] - alphas[k]) * v - wz[z] * basis[k, z + 1]
            if z:
                image = image - wz[z - 1] * basis[k, z - 1]
            image = image - wxz * fore(v) - back(wxz * v) - wyz * right(v) - left(wyz * v)
            if k:
                image = image - betas[k] * basis[k - 1, z]
            basis[k + 1, z] = image * scales[k + 1]

    inner = slice(HALO, HALO + nx)
    for z in range(nz):
        c = -0.5 * c_pad[z, inner, :LANES]
        h = h_pad[z, inner, :LANES]
        wide = h_pad[z, inner, :]
        grads[0, z] = c * (h - h_pad[z, HALO + 1 : HALO + nx + 1, :LANES])
        grads[1, z] = c * (h - h_pad[z, HALO - 1 : HALO + nx - 1, :LANES])
        grads[2, z] = c * (h - right(wide)[:, :LANES])
        grads[3, z] = c * (h - left(wide)[:, :LANES])
        grads[4, z] = c * (h - h_pad[z + 1, inner, :LANES])
        grads[5, z] = c * (h - h_pad[z - 1, inner, :LANES]) if z else c * h

    dots = {}
    for i in range(ITERS + 1):
        for j in range(i + 1):
            acc = basis[i, 0, inner, :LANES] * basis[j, 0, inner, :LANES]
            for z in range(1, nz):
                acc = acc + basis[i, z, inner, :LANES] * basis[j, z, inner, :LANES]
            dots[i, j] = dots[j, i] = all_sum(acc)
    lanes = lane_iota(1)
    entries = jnp.zeros((1, LANES), jnp.float32)
    place = 0
    for i in range(ITERS):
        for j in range(i + 1):
            entry = betas[j + 1] * dots[i, j + 1] + alphas[j] * dots[i, j]
            if j:
                entry = entry + betas[j] * dots[i, j - 1]
            entries = jnp.where(lanes == place, entry, entries)
            place += 1
    for i in range(ITERS):
        entries = jnp.where(lanes == place, dots[i, 0], entries)
        place += 1

    sums = []
    for k in range(ITERS):
        acc = jnp.zeros((nx, LANES), jnp.float32)
        for z in range(nz):
            u = basis[k, z, inner, :LANES]
            wide = basis[k, z, inner, :]
            acc = acc + (u - basis[k, z, HALO + 1 : HALO + nx + 1, :LANES]) * grads[0, z]
            acc = acc + (u - basis[k, z, HALO - 1 : HALO + nx - 1, :LANES]) * grads[1, z]
            acc = acc + (u - right(wide)[:, :LANES]) * grads[2, z]
            acc = acc + (u - left(wide)[:, :LANES]) * grads[3, z]
            acc = acc + (u - basis[k, z + 1, inner, :LANES]) * grads[4, z]
            if z:
                acc = acc + (u - basis[k, z - 1, inner, :LANES]) * grads[5, z]
            else:
                acc = acc + u * grads[5, z]
            own_ref[k, jnp.where(layer == 0, z, nz - 1 - z)] = u
        sums.append(acc)
    blocks_x = nx // 4
    four = jnp.where(lax.shift_right_logical(lane_iota(blocks_x, nx), 2) == row_iota(blocks_x, nx), 1.0, 0.0)
    sums = mm(four, jnp.concatenate(sums, axis=1), precision=EXACT)
    pilots = nx * LANES // 8
    each = pilots // LANES
    pilot_rows = peers * each
    pilot = [pilot_ref[4 * r : 4 * r + 1, :] for r in range(blocks_x)]
    lane_hits = jnp.concatenate(
        [jnp.where(row_iota(LANES) == (p & (LANES - 1)), 1.0, 0.0).astype(jnp.bfloat16) for p in pilot],
        axis=1,
    )
    rows_at = row_iota(pilot_rows)
    row_hit = [rows_at == lax.shift_right_logical(p, LANE_BITS) for p in pilot]
    copies = send_ref.shape[0] // peers
    for k in range(ITERS):
        part = pieces_of(sums[:, k * LANES : (k + 1) * LANES])
        values = jnp.concatenate(
            [
                jnp.concatenate(
                    [picked(row_hit[r], p[r : r + 1]) for r in range(blocks_x)], axis=1
                )
                for p in part
            ],
            axis=0,
        )
        dense = mm(values, lane_hits, NT)
        dense = dense[:pilot_rows] + dense[pilot_rows : 2 * pilot_rows] + dense[2 * pilot_rows :]
        for peer in range(peers):
            for copy in range(copies):
                send_ref[peer * copies + copy, k * each : (k + 1) * each, :] = dense[
                    peer * each : (peer + 1) * each
                ]
    tail = send_ref.shape[1] - ITERS * each
    send_ref[:, ITERS * each :, :] = jnp.broadcast_to(
        entries[None], (send_ref.shape[0], tail, LANES)
    )


def solve_body(got_ref, own_ref, adjoint_ref, pilot_ref):
    total = got_ref[0]
    for i in range(1, got_ref.shape[0]):
        total = total + got_ref[i]
    each = pilot_ref.shape[0]
    entries = total[ITERS * each : ITERS * each + 1, :]
    scalar = [entries[0, i] for i in range(ITERS * (ITERS + 1) // 2 + ITERS)]
    matrix, place = {}, 0
    for i in range(ITERS):
        for j in range(i + 1):
            matrix[i, j] = scalar[place]
            place += 1
    rhs = scalar[place:]
    lower, scaled, inverse = {}, {}, []
    for i in range(ITERS):
        for j in range(i + 1):
            s = matrix[i, j]
            for k in range(j):
                s = s - scaled[i, k] * lower[j, k]
            scaled[i, j] = s
            if j < i:
                lower[i, j] = s * inverse[j]
        inverse.append(jnp.where(scaled[i, i] > 0.0, 1.0 / scaled[i, i], 0.0))
    y = []
    for i in range(ITERS):
        s = rhs[i]
        for k in range(i):
            s = s - lower[i, k] * y[k]
        y.append(s)
    x = [None] * ITERS
    for i in reversed(range(ITERS)):
        s = y[i] * inverse[i]
        for k in range(i + 1, ITERS):
            s = s - lower[k, i] * x[k]
        x[i] = s
    pilot = x[0] * total[:each]
    for k in range(1, ITERS):
        pilot = pilot + x[k] * total[k * each : (k + 1) * each]
    pilot_ref[...] = pilot
    for z in range(own_ref.shape[1]):
        acc = x[0] * own_ref[0, z]
        for k in range(1, ITERS):
            acc = acc + x[k] * own_ref[k, z]
        adjoint_ref[z] = acc


def surroundings(block):
    layer_count, row_count, col_count = (lax.axis_size(a) for a in ("layers", "rows", "cols"))
    other = lax.ppermute(block, "layers", [(0, 1), (1, 0)])
    forward = [(i, i + 1) for i in range(col_count - 1)]
    backward = [(b, a) for a, b in forward]
    low_edge = jnp.concatenate([block[:, :, :HALO], other[:, :, :HALO]], axis=1)
    high_edge = jnp.concatenate([block[:, :, -HALO:], other[:, :, -HALO:]], axis=1)
    low = lax.ppermute(high_edge, "cols", forward)
    high = lax.ppermute(low_edge, "cols", backward)
    both = jnp.concatenate([low, jnp.concatenate([block, other], axis=1), high], axis=2)

    def packed(edge):
        return jnp.transpose(edge, (0, 3, 1, 2)).reshape(edge.shape[0], HALO, -1)

    if row_count == 2:
        row = lax.axis_index("rows")
        edge = packed(jnp.where(row == 0, both[..., -HALO:], both[..., :HALO]))
        got = lax.ppermute(edge, "rows", [(0, 1), (1, 0)])
        sides = jnp.concatenate(
            [jnp.where(row == 0, got, 0.0), jnp.where(row == 0, 0.0, got)], axis=1
        )
    else:
        forward = [(i, i + 1) for i in range(row_count - 1)]
        backward = [(b, a) for a, b in forward]
        from_left = lax.ppermute(packed(both[..., -HALO:]), "rows", forward)
        from_right = lax.ppermute(packed(both[..., :HALO]), "rows", backward)
        sides = jnp.concatenate([from_right, from_left], axis=1)
    return block, other, low, high, sides


def on_device(
    state_field,
    conductivity,
    storage,
    gauge_owner,
    gauge_cell,
    gauge_value,
    gauge_weight,
    pilot_index,
):
    nz, nx, ny = state_field.shape
    peers = lax.axis_size("cols") * lax.axis_size("rows")
    devices = peers * lax.axis_size("layers")
    gauges = gauge_owner.shape[0]
    capacity = 4 * gauges // peers
    f32 = jnp.float32

    def shape(*dims):
        return jax.ShapeDtypeStruct(dims, f32)

    fixed = surroundings(jnp.stack([conductivity, storage, state_field]))

    def flat(x):
        return x.reshape(gauges // LANES, LANES)

    payload = kernel_call(
        functools.partial(route_body, peers, capacity),
        shape(peers, 3 * capacity // LANES, LANES),
    )(in_specs=[VMEM] * 4, out_specs=VMEM)(
        flat(gauge_owner), flat(gauge_cell), flat(gauge_value), flat(gauge_weight)
    )
    got = lax.all_to_all(payload, PEER_AXES, 0, 0, tiled=True)
    source = kernel_call(
        source_body, shape(nz * nx, LANES), [pltpu.VMEM((nz * nx, 3 * LANES), f32)]
    )(in_specs=[VMEM] * 2, out_specs=VMEM)(got, state_field.reshape(nz * nx, ny))
    source = source.reshape(nz, nx, ny)
    around = surroundings(source[None])

    local = kernel_call(local_body, shape(devices, LANES))(in_specs=[VMEM] * 3, out_specs=VMEM)(
        source, conductivity, storage
    )
    measures = lax.all_to_all(local, GRID_AXES, 0, 0, tiled=True)

    each = nx * ny // 8 // LANES
    send_rows = (ITERS * each + 8) // 8 * 8
    planes, width = 2 * nz, nx + 2 * HALO
    padded = pltpu.VMEM((planes, width, 2 * LANES), f32)
    layer = lax.axis_index("layers").astype(jnp.int32).reshape(1)
    own, send = kernel_call(
        functools.partial(basis_body, peers),
        (shape(ITERS, nz, nx, LANES), shape(devices, send_rows, LANES)),
        [padded] * 7
        + [
            pltpu.VMEM((ITERS + 1, planes, width, 2 * LANES), f32),
            pltpu.VMEM((planes, width, LANES), f32),
            pltpu.VMEM((6, nz, nx, LANES), f32),
        ],
    )(in_specs=[SMEM] + [VMEM] * 12, out_specs=(VMEM, VMEM))(
        layer, *fixed, *around, measures, pilot_index
    )
    parts = lax.all_to_all(send, GRID_AXES, 0, 0, tiled=True)
    adjoint, pilot = kernel_call(solve_body, (shape(nz, nx, ny), shape(each, LANES)))(
        in_specs=[VMEM] * 2, out_specs=(VMEM, VMEM)
    )(parts, own)
    return adjoint, pilot.reshape(-1)


def solution(mesh):
    return jax.shard_map(
        on_device,
        mesh=mesh,
        in_specs=(
            P(("groups", "layers"), "cols", "rows"),
            P(("groups", "layers"), "cols", "rows"),
            P(("groups", "layers"), "cols", "rows"),
            P(("groups", "cols", "rows", "layers")),
            P(("groups", "cols", "rows", "layers")),
            P(("groups", "cols", "rows", "layers")),
            P(("groups", "cols", "rows", "layers")),
            P("cols", "rows"),
        ),
        out_specs=(P(("groups", "layers"), "cols", "rows"), P(("groups", "cols", "rows"))),
        check_vma=False,
    )
```

time: 1020 us -> 90.8 us (0.09)
  blocking collectives: 491 us -> 15.7 us
  other arithmetic: 154 us -> 1.78 us
  local copies, waits for them, and re-layouts: 132 us -> 3.44 us
  starting transfers between devices: 118 us -> 22.9 us
  waiting for transfers between devices: 96.7 us -> 17.1 us
  Pallas kernels: 0 us -> 28.3 us
  between operations: 22.4 us -> 0.93 us
    psum x16 -> x0, blocking collectives: 458 us -> none  [the longest x8 242 us: squares(): return lax.psum(jnp.sum(field * field), ('cols', 'rows', 'layers'))]
    scatter-add x2 -> x0, other arithmetic: 132 us -> none  [the longest x1 109 us: on_device(): jnp.zeros_like(flat_state).at[received_cells].add(misfit)]
    ppermute x60 -> x8, starting transfers between devices: 105 us -> 12.2 us  [the longest x2 7.32 us: surroundings(): low = lax.ppermute(high_edge, 'cols', forward)]
    gather x1 -> x0, local copies, waits for them, and re-layouts: 90.5 us -> none  [on_device(): misfit = got_payload[1] * (flat_state[received_cells] - got_payload[0])]
    ppermute x60 -> x8, waiting for transfers between devices: 96.7 us -> 10.3 us  [the longest x2 3.8 us: surroundings(): got = lax.ppermute(edge, 'rows', [(0, 1), (1, 0)])]
    unnamed x1 -> x0, blocking collectives: 33 us -> none
    scatter x2 -> x0, local copies, waits for them, and re-layouts: 30.9 us -> none  [the longest x1 16.3 us: on_device(): jnp.zeros((1, peer_count * capacity), jnp.int32).at[:, position]]
    pallas_call x0 -> x5, Pallas kernels: none -> 28.3 us  [the longest x1 10.3 us: on_device(): kernel_call(source_body, shape(nz * nx, LANES), [pltpu.VMEM((nz * nx, 3 *...]
  transfers between devices with their start and end apart: 62 -> 10, of which waited for: 35 -> 4; matrix products, arithmetic and copies ran while one was open for 24% -> 3% of each run, Pallas kernels for 0% -> 14%
where the time goes in v1:
time: 90.8 us; the launch traced here: 90.1 us
  Pallas kernels  28.3 us (31%)
  starting transfers between devices  22.9 us (25%)
  waiting for transfers between devices  17.1 us (19%)
  blocking collectives  15.7 us (17%)
  local copies, waits for them, and re-layouts  3.44 us (4%)
  other arithmetic  1.78 us (2%)
  between operations  0.93 us (1%)
    all_to_all x1, blocking collectives, on_device(): parts = lax.all_to_all(send, GRID_AXES, 0, 0, tiled=True)  15.7 us
    pallas_call x1, Pallas kernels, on_device(): kernel_call(source_body, shape(nz * nx, LANES), [pltpu.VMEM((nz * nx, 3 *...  10.3 us
    pallas_call x1, Pallas kernels, on_device(): kernel_call(functools.partial(basis_body, peers), (shape(ITERS, nz, nx, L...  9.66 us
    ppermute x2, starting transfers between devices, surroundings(): low = lax.ppermute(high_edge, 'cols', forward)  7.32 us
    all_to_all x1, starting transfers between devices, on_device(): got = lax.all_to_all(payload, PEER_AXES, 0, 0, tiled=True)  7.25 us
    all_to_all x1, waiting for transfers between devices, on_device(): got = lax.all_to_all(payload, PEER_AXES, 0, 0, tiled=True)  6.78 us
    pallas_call x1, Pallas kernels, on_device(): kernel_call(functools.partial(route_body, peers, capacity), shape(peers,...  4.4 us
    ppermute x2, waiting for transfers between devices, surroundings(): got = lax.ppermute(edge, 'rows', [(0, 1), (1, 0)])  3.8 us
  transfers between devices with their start and end apart: 10, of which 4 were waited for; matrix products, arithmetic and copies ran while one was open for 3% of the time, Pallas kernels for 14%

profile of v1, /device:TPU:0, one launch (start us, length us, event | category | flops | bytes accessed | tf_op | source)
XLA Modules:
  0.0 90.1 jit_solution(10608461744615597486)
XLA Ops:
  0.6 0.0 copy-start.2
  0.6 0.0 copy-start.1
  0.7 0.0 copy-start
  0.7 0.0 copy-start.4
  0.7 0.8 copy-done.4
  1.4 0.0 copy-start.5
  1.4 0.7 copy-done.5
  2.2 0.0 copy-start.6
  2.2 0.7 copy-done.6
  2.9 0.0 copy-start.7
  2.9 0.7 copy-done.7
  3.6 4.4 %shard_map.95 = f32[8,48,128]{2,1,0:T(8,128)} custom-call(s32[32,128]{1,0:T(8,128)S(1)} %bitcast.35, s32[32,128]{1,0:T(8,128)S(1)} %bitcast.36, f32[32,128]{1,0:T(8,128)S(1)} %bitcast.37, f32[32,128]{1,0:T(8,128)S(1)} %bitcast.38), custom_call_target="tpu_custom_call" | custom-call | tf_op jit(solution)/shard_map/pallas_call | solution.py:511
  8.0 7.2 %all-to-all-start = ((f32[8,48,128]{2,1,0:T(8,128)}), f32[8,48,128]{2,1,0:T(8,128)S(1)}, u32[]{:S(2)}, u32[]{:S(2)}) async-start(f32[8,48,128]{2,1,0:T(8,128)} %shard_map.95), calls=%async_computation | async-start | bytes 393216 | tf_op jit(solution)/shard_map/all_to_all | solution.py:517
  15.2 1.1 %pad_maximum_fusion.1.f_own = f32[3,8,32,128]{3,2,1,0:T(8,128)S(1)} fusion(f32[1,8,32,128]{3,2,1,0:T(8,128)} %bitcast.27, f32[1,8,32,128]{3,2,1,0:T(8,128)} %bitcast.30, f32[1,8,32,128]{3,2,1,0:T(8,128)} %bitcast.32), kind=kLoop, calls=%fused_computation.3 | loop fusion | flops 196608 | bytes 786432 | tf_op jit(solution)/shard_map/stack | solution.py:506
  16.3 0.1 collective-permute-start
  16.4 6.8 %all-to-all-done.got_ref = f32[8,48,128]{2,1,0:T(8,128)S(1)} async-done(((f32[8,48,128]{2,1,0:T(8,128)}), f32[8,48,128]{2,1,0:T(8,128)S(1)}, u32[]{:S(2)}, u32[]{:S(2)}) %all-to-all-start) | async-done | bytes 196640 | tf_op jit(solution)/shard_map/all_to_all | solution.py:517
  23.2 0.0 copy-done
  23.2 10.3 %shard_map.96 = f32[256,128]{1,0:T(8,128)S(1)} custom-call(f32[8,48,128]{2,1,0:T(8,128)S(1)} %all-to-all-done.got_ref, f32[256,128]{1,0:T(8,128)S(1)} %bitcast.28), custom_call_target="tpu_custom_call" | custom-call | tf_op jit(solution)/shard_map/pallas_call | solution.py:518
  33.5 0.1 collective-permute-start.4
  33.5 0.0 copy-done.2
  33.6 0.0 copy-done.1
  33.6 2.7 %shard_map.97 = f32[16,128]{1,0:T(8,128)} custom-call(f32[8,32,128]{2,1,0:T(8,128)S(1)} %bitcast.23, f32[8,32,128]{2,1,0:T(8,128)S(1)} %copy-done.2, f32[8,32,128]{2,1,0:T(8,128)S(1)} %copy-done.1), custom_call_target="tpu_custom_call" | custom-call | tf_op jit(solution)/shard_map/pallas_call | solution.py:524
  36.3 3.5 %all-to-all-start.1 = ((f32[16,1,128]{2,1,0:T(1,128)}), f32[16,1,128]{2,1,0:T(1,128)S(1)}, u32[]{:S(2)}, u32[]{:S(2)}) async-start(f32[16,1,128]{2,1,0:T(1,128)} %bitcast.16), calls=%async_computation.1 | async-start | bytes 16384 | tf_op jit(solution)/shard_map/all_to_all | solution.py:527
  39.8 0.0 collective-permute-done.f_other
  39.8 0.0 collective-permute-done.4.b_other
  39.9 3.7 %collective-permute-start.5 = (f32[1,16,8,128]{3,2,1,0:T(8,128)S(1)}, f32[1,16,8,128]{3,2,1,0:T(8,128)S(1)}, u32[]{:S(2)}, u32[]{:S(2)}) collective-permute-start(f32[1,16,8,128]{3,2,1,0:T(8,128)S(1)} %pad_maximum_fusion.6), channel_id=1, source_target_pairs={{0,4},{4,8},{8,12},{1,5},{5,9},{9,13},{2,6},{6,10},{10,14},{3,7},{... | collective-permute-start | bytes 196616 | tf_op jit(solution)/shard_map/ppermute | solution.py:463
  43.6 1.3 %collective-permute-start.6 = (f32[1,16,8,128]{3,2,1,0:T(8,128)S(1)}, f32[1,16,8,128]{3,2,1,0:T(8,128)S(1)}, u32[]{:S(2)}, u32[]{:S(2)}) collective-permute-start(f32[1,16,8,128]{3,2,1,0:T(8,128)S(1)} %pad_maximum_fusion.7), channel_id=1, source_target_pairs={{4,0},{8,4},{12,8},{5,1},{9,5},{13,9},{6,2},{10,6},{14,10},{7,3},{... | collective-permute-start | bytes 196616 | tf_op jit(solution)/shard_map/ppermute | solution.py:464
  45.0 1.3 %collective-permute-start.2 = (f32[3,16,8,128]{3,2,1,0:T(8,128)S(1)}, f32[3,16,8,128]{3,2,1,0:T(8,128)S(1)}, u32[]{:S(2)}, u32[]{:S(2)}) collective-permute-start(f32[3,16,8,128]{3,2,1,0:T(8,128)S(1)} %pad_maximum_fusion.4), channel_id=1, source_target_pairs={{4,0},{8,4},{12,8},{5,1},{9,5},{13,9},{6,2},{10,6},{14,10},{7,3},{... | collective-permute-start | bytes 589832 | tf_op jit(solution)/shard_map/ppermute | solution.py:464
  46.3 0.0 collective-permute-done.5.b_low
  46.3 3.5 %collective-permute-done.6.b_high = f32[1,16,8,128]{3,2,1,0:T(8,128)S(1)} collective-permute-done((f32[1,16,8,128]{3,2,1,0:T(8,128)S(1)}, f32[1,16,8,128]{3,2,1,0:T(8,128)S(1)}, u32[]{:S(2)}, u32[]{:S(2)}) %collective-permute-start.6) | collective-permute-done | bytes 65568 | tf_op jit(solution)/shard_map/ppermute | solution.py:464
  49.8 0.2 slice_select_fusion.1
  50.0 0.1 copy.16
  50.1 1.5 %collective-permute-start.7 = (f32[1,8,768]{2,1,0:T(8,128)S(1)}, f32[1,8,768]{2,1,0:T(8,128)S(1)}, u32[]{:S(2)}, u32[]{:S(2)}) collective-permute-start(f32[1,8,768]{2,1,0:T(8,128)S(1)} %copy.16), channel_id=1, source_target_pairs={{0,2},{2,0},{1,3},{3,1},{4,6},{6,4},{5,7},{7,5},{8,10},{10,8},{9,1... | collective-permute-start | bytes 73736 | tf_op jit(solution)/shard_map/ppermute | solution.py:473
  51.7 3.6 %collective-permute-start.1 = (f32[3,16,8,128]{3,2,1,0:T(8,128)S(1)}, f32[3,16,8,128]{3,2,1,0:T(8,128)S(1)}, u32[]{:S(2)}, u32[]{:S(2)}) collective-permute-start(f32[3,16,8,128]{3,2,1,0:T(8,128)S(1)} %pad_maximum_fusion.3), channel_id=1, source_target_pairs={{0,4},{4,8},{8,12},{1,5},{5,9},{9,13},{2,6},{6,10},{10,14},{3,7},{... | collective-permute-start | bytes 589832 | tf_op jit(solution)/shard_map/ppermute | solution.py:463
  55.3 0.0 collective-permute-done.7
  55.3 0.0 collective-permute-done.2.f_high
  55.3 2.9 %collective-permute-done.1.f_low = f32[3,16,8,128]{3,2,1,0:T(8,128)S(1)} collective-permute-done((f32[3,16,8,128]{3,2,1,0:T(8,128)S(1)}, f32[3,16,8,128]{3,2,1,0:T(8,128)S(1)}, u32[]{:S(2)}, u32[]{:S(2)}) %collective-permute-start.1) | collective-permute-done | bytes 196640 | tf_op jit(solution)/shard_map/ppermute | solution.py:463
  58.2 0.1 pad_maximum_fusion
  58.3 0.4 slice_select_fusion
  58.7 0.0 copy-start.3
  58.7 0.3 copy.15
  59.0 0.6 collective-permute-start.3
  59.6 3.8 %collective-permute-done.3 = f32[3,8,768]{2,1,0:T(8,128)S(1)} collective-permute-done((f32[3,8,768]{2,1,0:T(8,128)S(1)}, f32[3,8,768]{2,1,0:T(8,128)S(1)}, u32[]{:S(2)}, u32[]{:S(2)}) %collective-permute-start.3) | collective-permute-done | bytes 73760 | tf_op jit(solution)/shard_map/ppermute | solution.py:473
  63.5 0.0 all-to-all-done.1
  63.5 0.0 copy-done.3
  63.5 9.7 %shard_map.98 = (f32[8,8,32,128]{3,2,1,0:T(8,128)S(1)}, f32[16,40,128]{2,1,0:T(8,128)S(1)}) custom-call(s32[1]{0:T(128)} %bitcast.layer_ref, f32[3,8,32,128]{3,2,1,0:T(8,128)S(1)} %pad_maximum_fusion.1.f_own, f32[3,8,32,128]{3,2,1,0:T(8,128)S(1)} %collective-permute-done.f_other, f32[3,16,8,128]{3,2,1,0:T(8,128)S(1)} %collective-permute-done.1.f_low, ...), custom_call_target="tpu_custom_call" | custom-call | tf_op jit(solution)/shard_map/pallas_call | solution.py:534
  73.1 15.7 %all_to_all.21.got_ref = f32[16,40,128]{2,1,0:T(8,128)S(1)} all-to-all(f32[16,40,128]{2,1,0:T(8,128)S(1)} %get-tuple-element.6), channel_id=1, replica_groups=mesh['groups'=2,'cols'=4,'rows'=2,'layers'=2] {'cols','rows','layers'}, dimensions={0} | all-to-all | bytes 655360 | tf_op jit(solution)/shard_map/all_to_all | solution.py:546
  88.8 1.2 %shard_map.99 = (f32[8,32,128]{2,1,0:T(8,128)}, f32[4,128]{1,0:T(4,128)}) custom-call(f32[16,40,128]{2,1,0:T(8,128)S(1)} %all_to_all.21.got_ref, f32[8,8,32,128]{3,2,1,0:T(8,128)S(1)} %get-tuple-element.7.own_ref), custom_call_target="tpu_custom_call" | custom-call | tf_op jit(solution)/shard_map/pallas_call | solution.py:547
  (13 shorter events, 0.2 us)
Async XLA Ops:
  0.6 32.9 %copy-start.2 = (f32[8,32,128]{2,1,0:T(8,128)S(1)}, f32[8,32,128]{2,1,0:T(8,128)}, u32[]{:S(2)}) copy-start(f32[8,32,128]{2,1,0:T(8,128)} %conductivity_ref.1) | copy-start | bytes 393220
  0.6 32.9 %copy-start.1 = (f32[8,32,128]{2,1,0:T(8,128)S(1)}, f32[8,32,128]{2,1,0:T(8,128)}, u32[]{:S(2)}) copy-start(f32[8,32,128]{2,1,0:T(8,128)} %storage_ref.1) | copy-start | bytes 393220
  0.7 22.5 %copy-start = (f32[8,32,128]{2,1,0:T(8,128)S(1)}, f32[8,32,128]{2,1,0:T(8,128)}, u32[]{:S(2)}) copy-start(f32[8,32,128]{2,1,0:T(8,128)} %param.8) | copy-start | bytes 393220
  0.7 0.8 copy-start.4
  1.4 0.7 copy-start.5
  2.2 0.7 copy-start.6
  2.9 0.7 copy-start.7
  8.0 15.2 %all-to-all-start = ((f32[8,48,128]{2,1,0:T(8,128)}), f32[8,48,128]{2,1,0:T(8,128)S(1)}, u32[]{:S(2)}, u32[]{:S(2)}) async-start(f32[8,48,128]{2,1,0:T(8,128)} %shard_map.95), calls=%async_computation | async-start | bytes 393216 | tf_op jit(solution)/shard_map/all_to_all | solution.py:517
  16.3 23.5 %collective-permute-start = (f32[3,8,32,128]{3,2,1,0:T(8,128)S(1)}, f32[3,8,32,128]{3,2,1,0:T(8,128)S(1)}, u32[]{:S(2)}, u32[]{:S(2)}) collective-permute-start(f32[3,8,32,128]{3,2,1,0:T(8,128)S(1)} %pad_maximum_fusion.1.f_own), channel_id=1, source_target_pairs={{0,1},{1,0},{2,3},{3,2},{4,5},{5,4},{6,7},{7,6},{8,9},{9,8},{10,11... | collective-permute-start | bytes 1179656 | tf_op jit(solution)/shard_map/ppermute | solution.py:458
  33.5 6.4 %collective-permute-start.4 = (f32[1,8,32,128]{3,2,1,0:T(8,128)S(1)}, f32[1,8,32,128]{3,2,1,0:T(8,128)S(1)}, u32[]{:S(2)}, u32[]{:S(2)}) collective-permute-start(f32[1,8,32,128]{3,2,1,0:T(8,128)S(1)} %bitcast.22), channel_id=1, source_target_pairs={{0,1},{1,0},{2,3},{3,2},{4,5},{5,4},{6,7},{7,6},{8,9},{9,8},{10,11... | collective-permute-start | bytes 393224 | tf_op jit(solution)/shard_map/ppermute | solution.py:458
  36.3 27.1 %all-to-all-start.1 = ((f32[16,1,128]{2,1,0:T(1,128)}), f32[16,1,128]{2,1,0:T(1,128)S(1)}, u32[]{:S(2)}, u32[]{:S(2)}) async-start(f32[16,1,128]{2,1,0:T(1,128)} %bitcast.16), calls=%async_computation.1 | async-start | bytes 16384 | tf_op jit(solution)/shard_map/all_to_all | solution.py:527
  39.9 6.4 %collective-permute-start.5 = (f32[1,16,8,128]{3,2,1,0:T(8,128)S(1)}, f32[1,16,8,128]{3,2,1,0:T(8,128)S(1)}, u32[]{:S(2)}, u32[]{:S(2)}) collective-permute-start(f32[1,16,8,128]{3,2,1,0:T(8,128)S(1)} %pad_maximum_fusion.6), channel_id=1, source_target_pairs={{0,4},{4,8},{8,12},{1,5},{5,9},{9,13},{2,6},{6,10},{10,14},{3,7},{... | collective-permute-start | bytes 196616 | tf_op jit(solution)/shard_map/ppermute | solution.py:463
  43.6 6.2 %collective-permute-start.6 = (f32[1,16,8,128]{3,2,1,0:T(8,128)S(1)}, f32[1,16,8,128]{3,2,1,0:T(8,128)S(1)}, u32[]{:S(2)}, u32[]{:S(2)}) collective-permute-start(f32[1,16,8,128]{3,2,1,0:T(8,128)S(1)} %pad_maximum_fusion.7), channel_id=1, source_target_pairs={{4,0},{8,4},{12,8},{5,1},{9,5},{13,9},{6,2},{10,6},{14,10},{7,3},{... | collective-permute-start | bytes 196616 | tf_op jit(solution)/shard_map/ppermute | solution.py:464
  45.0 10.3 %collective-permute-start.2 = (f32[3,16,8,128]{3,2,1,0:T(8,128)S(1)}, f32[3,16,8,128]{3,2,1,0:T(8,128)S(1)}, u32[]{:S(2)}, u32[]{:S(2)}) collective-permute-start(f32[3,16,8,128]{3,2,1,0:T(8,128)S(1)} %pad_maximum_fusion.4), channel_id=1, source_target_pairs={{4,0},{8,4},{12,8},{5,1},{9,5},{13,9},{6,2},{10,6},{14,10},{7,3},{... | collective-permute-start | bytes 589832 | tf_op jit(solution)/shard_map/ppermute | solution.py:464
  50.1 5.1 %collective-permute-start.7 = (f32[1,8,768]{2,1,0:T(8,128)S(1)}, f32[1,8,768]{2,1,0:T(8,128)S(1)}, u32[]{:S(2)}, u32[]{:S(2)}) collective-permute-start(f32[1,8,768]{2,1,0:T(8,128)S(1)} %copy.16), channel_id=1, source_target_pairs={{0,2},{2,0},{1,3},{3,1},{4,6},{6,4},{5,7},{7,5},{8,10},{10,8},{9,1... | collective-permute-start | bytes 73736 | tf_op jit(solution)/shard_map/ppermute | solution.py:473
  51.7 6.6 %collective-permute-start.1 = (f32[3,16,8,128]{3,2,1,0:T(8,128)S(1)}, f32[3,16,8,128]{3,2,1,0:T(8,128)S(1)}, u32[]{:S(2)}, u32[]{:S(2)}) collective-permute-start(f32[3,16,8,128]{3,2,1,0:T(8,128)S(1)} %pad_maximum_fusion.3), channel_id=1, source_target_pairs={{0,4},{4,8},{8,12},{1,5},{5,9},{9,13},{2,6},{6,10},{10,14},{3,7},{... | collective-permute-start | bytes 589832 | tf_op jit(solution)/shard_map/ppermute | solution.py:463
  58.7 4.8 %copy-start.3 = (s32[32,128]{1,0:T(8,128)S(1)}, s32[32,128]{1,0:T(8,128)}, u32[]{:S(2)}) copy-start(s32[32,128]{1,0:T(8,128)} %pilot_ref.1) | copy-start | bytes 49156
  59.0 4.4 %collective-permute-start.3 = (f32[3,8,768]{2,1,0:T(8,128)S(1)}, f32[3,8,768]{2,1,0:T(8,128)S(1)}, u32[]{:S(2)}, u32[]{:S(2)}) collective-permute-start(f32[3,8,768]{2,1,0:T(8,128)S(1)} %copy.15), channel_id=1, source_target_pairs={{0,2},{2,0},{1,3},{3,1},{4,6},{6,4},{5,7},{7,5},{8,10},{10,8},{9,1... | collective-permute-start | bytes 221192 | tf_op jit(solution)/shard_map/ppermute | solution.py:473

commit v2 on v1

v2 whole, which is shorter than its diff:
```python
import functools

import jax
import jax.numpy as jnp
from jax import lax
from jax.experimental import pallas as pl
from jax.experimental.pallas import tpu as pltpu
from jax.sharding import PartitionSpec as P

ITERS = 8
HALO = 8
FACTS = 64
SLOTS = 96
LANES = 128
LANE_BITS = 7
GRID_AXES = ("cols", "rows", "layers")
PEER_AXES = ("cols", "rows")
NT = (((1,), (1,)), ((), ()))
EXACT = lax.Precision.HIGHEST
VMEM_BYTES = 50 * 1024 * 1024


def kernel_call(body, out_shape, scratch=(), weight=1):
    return functools.partial(
        pl.pallas_call,
        body,
        out_shape=out_shape,
        scratch_shapes=list(scratch),
        compiler_params=pltpu.CompilerParams(vmem_limit_bytes=VMEM_BYTES),
        cost_estimate=pl.CostEstimate(
            flops=0, bytes_accessed=weight * 3_000_000, transcendentals=0
        ),
    )


VMEM = pl.BlockSpec(memory_space=pltpu.VMEM)
SMEM = pl.BlockSpec(memory_space=pltpu.SMEM)
ANY = pl.BlockSpec(memory_space=pl.ANY)


def pieces_of(x):
    first = x.astype(jnp.bfloat16).astype(jnp.float32)
    rest = x - first
    second = rest.astype(jnp.bfloat16).astype(jnp.float32)
    return first, second, rest - second


def row_iota(rows, lanes=LANES):
    return lax.broadcasted_iota(jnp.int32, (rows, lanes), 0)


def lane_iota(rows, lanes=LANES):
    return lax.broadcasted_iota(jnp.int32, (rows, lanes), 1)


def picked(mask, row):
    return jnp.where(mask, row, jnp.zeros_like(row)).astype(jnp.bfloat16)


def mm(a, b, dims=(((1,), (0,)), ((), ())), precision=None):
    return lax.dot_general(a, b, dims, precision=precision, preferred_element_type=jnp.float32)


def ranks(owner, peers):
    rows = owner.shape[0]
    ra, ca = row_iota(LANES, 2 * LANES), lane_iota(LANES, 2 * LANES)
    earlier_lane = jnp.where((ra < ca) | (ca >= LANES), 1.0, 0.0).astype(jnp.bfloat16)
    earlier_row = jnp.where(row_iota(rows, rows) > lane_iota(rows, rows), 1.0, 0.0).astype(
        jnp.bfloat16
    )

    def one(peer, rank):
        hit = owner == peer
        counts = mm(jnp.where(hit, 1.0, 0.0).astype(jnp.bfloat16), earlier_lane)
        before = mm(earlier_row, counts[:, LANES:].astype(jnp.bfloat16))
        return rank + jnp.where(hit, counts[:, :LANES] + before, 0.0)

    rank = jnp.zeros((rows, LANES), jnp.float32)
    if peers <= 16:
        for peer in range(peers):
            rank = one(peer, rank)
    else:
        rank = lax.fori_loop(0, peers, one, rank)
    return rank.astype(jnp.int32)


def route_body(
    peers, capacity, owner_hbm, cell_hbm, value_hbm, weight_hbm, out_ref,
    owner_ref, cell_ref, value_ref, weight_ref, sems,
):
    copies = [
        pltpu.make_async_copy(source, target, sems.at[i])
        for i, (source, target) in enumerate(
            (
                (owner_hbm, owner_ref),
                (cell_hbm, cell_ref),
                (value_hbm, value_ref),
                (weight_hbm, weight_ref),
            )
        )
    ]
    for copy in copies:
        copy.start()
    for copy in copies:
        copy.wait()
    rows = owner_ref.shape[0]
    owner = owner_ref[...]
    position = owner * capacity + ranks(owner, peers)
    slot_row = lax.shift_right_logical(position, LANE_BITS)
    slot_lane = position & (LANES - 1)
    cell = cell_ref[...]
    columns = [
        lax.shift_right_logical(cell, LANE_BITS).astype(jnp.float32),
        (cell & (LANES - 1)).astype(jnp.float32),
        *pieces_of(value_ref[...]),
        *pieces_of(weight_ref[...]),
    ]
    slot_rows = peers * capacity // LANES
    rows_at, lanes_at = row_iota(slot_rows), row_iota(LANES)
    total = jnp.zeros((slot_rows, len(columns) * LANES), jnp.float32)
    step = 8
    for start in range(0, rows, step):
        left, right = [], [[] for _ in columns]
        for r in range(start, start + step):
            left.append(
                jnp.where(rows_at == slot_row[r : r + 1], 1.0, 0.0).astype(jnp.bfloat16)
            )
            lane_hit = lanes_at == slot_lane[r : r + 1]
            for q, column in enumerate(columns):
                right[q].append(picked(lane_hit, column[r : r + 1]))
        right = jnp.concatenate([jnp.concatenate(q, axis=1) for q in right], axis=0)
        total = total + mm(jnp.concatenate(left, axis=1), right, NT)
    part = [total[:, q * LANES : (q + 1) * LANES] for q in range(len(columns))]
    fields = [
        part[0] * LANES + part[1],
        part[2] + part[3] + part[4],
        part[5] + part[6] + part[7],
    ]
    each = capacity // LANES

    for peer in range(peers):
        for q, field in enumerate(fields):
            out_ref[peer, q * each : (q + 1) * each, :] = field[peer * each : (peer + 1) * each]


def pilot_body(pilot_ref, spot_ref, slots_ref):
    peers = slots_ref.shape[0]
    blocks_x = pilot_ref.shape[0] // 4
    pilots = pilot_ref.shape[0] * pilot_ref.shape[1] // 8
    pilot = jnp.concatenate([pilot_ref[4 * r : 4 * r + 1, :] for r in range(blocks_x)], axis=0)
    owner = lax.div(pilot, jnp.int32(pilots))
    slot = pilot - owner * pilots
    first = (lane_iota(blocks_x) & 1) == 0
    owner = jnp.where(first, owner, -1)
    rank = ranks(owner, peers)
    spot_ref[...] = jnp.where(first, owner * LANES + rank, -1)
    left, high, low = [], [], []
    peer_at, lanes_at = row_iota(peers), row_iota(LANES)
    for r in range(blocks_x):
        left.append(jnp.where(peer_at == owner[r : r + 1], 1.0, 0.0).astype(jnp.bfloat16))
        hit = lanes_at == rank[r : r + 1]
        number = slot[r : r + 1]
        high.append(picked(hit, lax.shift_right_logical(number, LANE_BITS).astype(jnp.float32)))
        low.append(picked(hit, (number & (LANES - 1)).astype(jnp.float32)))
    left = jnp.concatenate(left, axis=1)
    slots_ref[...] = mm(left, jnp.concatenate(high, axis=1), NT) * LANES + mm(
        left, jnp.concatenate(low, axis=1), NT
    )


def source_body(
    each, got_ref, conductivity_ref, storage_ref, state_ref, out_ref, up_ref, down_ref, acc_ref
):
    peers = got_ref.shape[0]
    nz, nx = conductivity_ref.shape[0], conductivity_ref.shape[1]
    cells = nz * nx
    state_t = jnp.concatenate(
        [p.astype(jnp.bfloat16) for p in pieces_of(jnp.transpose(state_ref[...].reshape(cells, LANES)))], axis=0
    )
    acc_ref[...] = jnp.zeros_like(acc_ref)
    rows_at, lanes_at = row_iota(cells), row_iota(LANES)

    def one_peer(peer, carry):
        cell = got_ref[peer, 0:each, :].astype(jnp.int32)
        value = got_ref[peer, each : 2 * each, :]
        weight = got_ref[peer, 2 * each : 3 * each, :]
        high = lax.shift_right_logical(cell, LANE_BITS)
        low = cell & (LANES - 1)
        row_hits = jnp.concatenate(
            [
                jnp.where(rows_at == high[r : r + 1], 1.0, 0.0).astype(jnp.bfloat16)
                for r in range(each)
            ],
            axis=1,
        )
        heads = mm(state_t, row_hits)
        right = [[], [], []]
        for r in range(each):
            lane_hit = lanes_at == low[r : r + 1]
            here = heads[:, r * LANES : (r + 1) * LANES]
            head = here[:LANES] + here[LANES : 2 * LANES] + here[2 * LANES :]
            head = jnp.sum(jnp.where(lane_hit, head, 0.0), axis=0, keepdims=True)
            misfit = weight[r : r + 1] * (head - value[r : r + 1])
            for q, piece in enumerate(pieces_of(misfit)):
                right[q].append(picked(lane_hit, piece))
        right = jnp.concatenate([jnp.concatenate(q, axis=1) for q in right], axis=0)
        acc_ref[...] += mm(row_hits, right, NT)
        return carry

    lax.fori_loop(0, peers, one_peer, 0)
    total = acc_ref[:, :LANES] + acc_ref[:, LANES : 2 * LANES] + acc_ref[:, 2 * LANES :]
    out_ref[...] = total.reshape(nz, nx, LANES)
    for f, field in enumerate((conductivity_ref, storage_ref, state_ref, out_ref)):
        up_ref[f] = field[:, nx - HALO :, :]
        down_ref[f] = field[:, :HALO, :]


def all_sum(x):
    while x.ndim > 2:
        x = jnp.sum(x, axis=0)
    return jnp.sum(jnp.sum(x, axis=0, keepdims=True), axis=1, keepdims=True)


def safe_ratio(a, b):
    return jnp.where(b > 0.0, a / jnp.where(b > 0.0, b, 1.0), 0.0)


def pack_body(low_side, where_ref, *refs):
    *fields, low_ref, high_ref, out_ref = refs
    nz, nx = fields[0].shape[0], fields[0].shape[1]
    lanes = lane_iota(2 * (nx + 2 * HALO))
    tall = jnp.zeros(lanes.shape, jnp.float32)
    for pair in range(2):
        for z in range(nz):
            at = (pair * nz + z) * HALO
            x = jnp.concatenate(
                [
                    part
                    for f in (2 * pair, 2 * pair + 1)
                    for part in (low_ref[f, z], fields[f][z], high_ref[f, z])
                ],
                axis=0,
            )
            if low_side is None:
                shift = (at + jnp.where(where_ref[1] == 0, HALO, 0)) & (LANES - 1)
            else:
                shift = at if low_side else (at + HALO) & (LANES - 1)
            x = pltpu.roll(x, shift, 1)
            tall = jnp.where((lanes >= at) & (lanes < at + HALO), x, tall)
    rest = LANES - tall.shape[0]
    tall = jnp.concatenate([tall, jnp.zeros((rest, LANES), jnp.float32)], axis=0)
    out_ref[...] = jnp.transpose(tall).reshape(out_ref.shape)


def unpack(layer, f, own, other, edges, beside, padded):
    nz, nx = own.shape[0], own.shape[1]
    tall = nx + 2 * HALO
    at = lane_iota(tall)
    rows = slice((f % 2) * tall, (f % 2 + 1) * tall)
    for half, block in ((0, own), (1, other)):
        low, high = edges[2 * half], edges[2 * half + 1]
        for i in range(nz):
            j = jnp.where(layer == 0, i, nz - 1 - i)
            to = half * nz + i
            padded[to, HALO : HALO + nx, :LANES] = block[j]
            padded[to, :HALO, :LANES] = low[f, j]
            padded[to, HALO + nx :, :LANES] = high[f, j]
            strip = jnp.zeros((tall, LANES), jnp.float32)
            for tiles, first in beside[half]:
                shift = (2 * LANES + first - (f // 2 * nz + j) * HALO) & (LANES - 1)
                strip = jnp.where(
                    (at >= first) & (at < first + HALO), pltpu.roll(tiles[rows], shift, 1), strip
                )
            padded[to, :, LANES:] = strip


def basis_body(peers, side_count, where_ref, *refs):
    own, other = refs[:4], refs[4:8]
    edges = refs[8:12]
    sides = (refs[12 : 12 + side_count], refs[12 + side_count : 12 + 2 * side_count])
    refs = refs[12 + 2 * side_count :]
    spot_ref, slots_ref, own_ref, send_ref = refs[:4]
    c_pad, s_pad, h_pad, diag, wx, wy, wz, image, basis, grads = refs[4:]
    layer, row = where_ref[0], where_ref[1]
    nz, nx = own[0].shape[0], own[0].shape[1]
    planes, width = c_pad.shape[0], c_pad.shape[1]
    high_side, low_side = 0, LANES - HALO
    if side_count == 1:
        firsts = [jnp.where(row == 0, high_side, low_side)]
    else:
        firsts = [low_side, high_side]
    beside = [
        [
            (jnp.transpose(side[...].reshape(LANES, LANES)), first)
            for side, first in zip(half, firsts)
        ]
        for half in sides
    ]
    for f, target in enumerate((c_pad, s_pad, h_pad, basis.at[0])):
        unpack(layer, f, own[f], other[f], edges, beside, target)
    def right(x):
        return pltpu.roll(x, x.shape[1] - 1, 1)

    def left(x):
        return pltpu.roll(x, 1, 1)

    def fore(x):
        return pltpu.roll(x, x.shape[0] - 1, 0)

    def back(x):
        return pltpu.roll(x, 1, 0)

    def joined(a, b):
        return jnp.where((a > 0.0) & (b > 0.0), 0.5 * (a + b), 0.0)

    for z in range(planes):
        c = c_pad[z]
        cf, cr = fore(c), right(c)
        total = cf + back(c) + cr + left(c)
        wx[z] = joined(c, cf)
        wy[z] = joined(c, cr)
        if z + 1 < planes:
            wz[z] = joined(c, c_pad[z + 1])
            total = total + c_pad[z + 1]
        if z:
            total = total + c_pad[z - 1]
        diag[z] = s_pad[z] + 3.0 * c + 0.5 * total

    alphas, gammas, norms = [], [], []

    def member(k, z, rows=slice(None), lanes=slice(None)):
        u = image[z, rows, lanes] - alphas[k - 1] * basis[k - 1, z, rows, lanes]
        if k > 1:
            u = u - gammas[k - 1] * basis[k - 2, z, rows, lanes]
        basis[k, z, rows, lanes] = u

    def folded(x):
        x = x[:, :LANES] + x[:, LANES:]
        return sum(x[r : r + 8] for r in range(8, width, 8)) + x[:8]

    for k in range(ITERS):
        if k:
            member(k, 0)
        norm = jnp.zeros((8, LANES), jnp.float32)
        energy = jnp.zeros((8, LANES), jnp.float32)
        for z in range(nz + ITERS - 1 - k):
            if k:
                member(k, z + 1)
            v = basis[k, z]
            wxz, wyz = wx[z], wy[z]
            av = diag[z] * v - wz[z] * basis[k, z + 1]
            if z:
                av = av - wz[z - 1] * basis[k, z - 1]
            av = av - wxz * fore(v) - back(wxz * v) - wyz * right(v) - left(wyz * v)
            image[z] = av
            norm = norm + folded(v * v)
            energy = energy + folded(v * av)
        norm = all_sum(norm)
        alphas.append(safe_ratio(all_sum(energy), norm))
        gammas.append(safe_ratio(norm, norms[-1]) if k else jnp.zeros_like(norm))
        norms.append(norm)
    inner = slice(HALO, HALO + nx)
    for z in range(nz):
        member(ITERS, z, inner, slice(LANES))

    for z in range(nz):
        c = -0.5 * c_pad[z, inner, :LANES]
        h = h_pad[z, inner, :LANES]
        wide = h_pad[z, inner, :]
        grads[0, z] = c * (h - h_pad[z, HALO + 1 : HALO + nx + 1, :LANES])
        grads[1, z] = c * (h - h_pad[z, HALO - 1 : HALO + nx - 1, :LANES])
        grads[2, z] = c * (h - right(wide)[:, :LANES])
        grads[3, z] = c * (h - left(wide)[:, :LANES])
        grads[4, z] = c * (h - h_pad[z + 1, inner, :LANES])
        grads[5, z] = c * (h - h_pad[z - 1, inner, :LANES]) if z else c * h

    dots = {}
    for i in range(ITERS + 1):
        for j in range(i + 1):
            acc = basis[i, 0, inner, :LANES] * basis[j, 0, inner, :LANES]
            for z in range(1, nz):
                acc = acc + basis[i, z, inner, :LANES] * basis[j, z, inner, :LANES]
            dots[i, j] = dots[j, i] = all_sum(acc)

    def operator(i, j):
        entry = dots[i, j + 1] + alphas[j] * dots[i, j]
        return entry + gammas[j] * dots[i, j - 1] if j else entry

    lanes = lane_iota(1)
    facts = []
    for j in range(ITERS):
        row_facts = [0.5 * (operator(j, m) + operator(m, j)) for m in range(ITERS)]
        row_facts += [alphas[j], gammas[j], norms[j], dots[j, 0]]
        entries = jnp.zeros((1, LANES), jnp.float32)
        for place, entry in enumerate(row_facts):
            entries = jnp.where(lanes == FACTS + place, entry, entries)
        facts.append(entries)

    sums = []
    for k in range(ITERS):
        acc = jnp.zeros((nx, LANES), jnp.float32)
        for z in range(nz):
            u = basis[k, z, inner, :LANES]
            wide = basis[k, z, inner, :]
            acc = acc + (u - basis[k, z, HALO + 1 : HALO + nx + 1, :LANES]) * grads[0, z]
            acc = acc + (u - basis[k, z, HALO - 1 : HALO + nx - 1, :LANES]) * grads[1, z]
            acc = acc + (u - right(wide)[:, :LANES]) * grads[2, z]
            acc = acc + (u - left(wide)[:, :LANES]) * grads[3, z]
            acc = acc + (u - basis[k, z + 1, inner, :LANES]) * grads[4, z]
            if z:
                acc = acc + (u - basis[k, z - 1, inner, :LANES]) * grads[5, z]
            else:
                acc = acc + u * grads[5, z]
            own_ref[k, jnp.where(layer == 0, z, nz - 1 - z)] = u
        sums.append(acc)
    blocks_x = nx // 4
    four = jnp.where(
        lax.shift_right_logical(lane_iota(blocks_x, nx), 2) == row_iota(blocks_x, nx), 1.0, 0.0
    )
    sums = mm(four, jnp.concatenate(sums, axis=1), precision=EXACT)
    spot = [spot_ref[r : r + 1, :] for r in range(blocks_x)]
    lane_hits = jnp.concatenate(
        [
            jnp.where(row_iota(LANES) == (p & (LANES - 1)), 1.0, 0.0).astype(jnp.bfloat16)
            for p in spot
        ],
        axis=1,
    )
    peer_at = row_iota(peers)
    row_hit = [(p >= 0) & (peer_at == lax.shift_right_arithmetic(p, LANE_BITS)) for p in spot]
    values = []
    for k in range(ITERS):
        pair = sums[:, k * LANES : (k + 1) * LANES]
        pair = pair + pltpu.roll(pair, LANES - 1, 1)
        for p in pieces_of(pair):
            values.append(
                jnp.concatenate(
                    [picked(row_hit[r], p[r : r + 1]) for r in range(blocks_x)], axis=1
                )
            )
    dense = mm(jnp.concatenate(values, axis=0), lane_hits, NT)
    copies = send_ref.shape[0] // peers
    for k in range(ITERS):
        at = 3 * k * peers
        rows = dense[at : at + peers] + dense[at + peers : at + 2 * peers]
        rows = rows + dense[at + 2 * peers : at + 3 * peers]
        rows = jnp.where(lane_iota(peers) < FACTS, rows, facts[k])
        if k < 2:
            slots = pltpu.roll(slots_ref[...], (1 - k) * (LANES - SLOTS) + FACTS, 1)
            rows = jnp.where(lane_iota(peers) < SLOTS, rows, slots)
        for peer in range(peers):
            for copy in range(copies):
                send_ref[peer * copies + copy, k : k + 1, :] = rows[peer : peer + 1]


def solve_body(copies, where_ref, got_ref, own_ref, adjoint_ref, pilot_ref):
    senders = got_ref.shape[0]
    peers = senders // copies
    groups = senders * ITERS // LANES
    got = got_ref[...].reshape(groups, LANES, LANES)
    turned = [jnp.transpose(got[g])[FACTS:SLOTS] for g in range(groups)]

    def fact(place):
        return jnp.concatenate([t[place : place + 1] for t in turned], axis=0)

    alpha, gamma, weight, rhs = (fact(ITERS + place) for place in range(4))
    at = lane_iota(groups) & (ITERS - 1)
    gamma_next = jnp.where(at < ITERS - 1, pltpu.roll(gamma, LANES - 1, 1), 0.0)

    now = jnp.where(at == 0, 1.0, 0.0)
    last, norm_last = None, None
    common = []
    for k in range(ITERS):
        common.append(now)
        if k == ITERS - 1:
            break
        image = jnp.where(at > 0, pltpu.roll(now, 1, 1), 0.0) + alpha * now
        image = image + gamma_next * pltpu.roll(now, LANES - 1, 1)
        norm = all_sum(weight * now * now)
        following = image - safe_ratio(all_sum(weight * now * image), norm) * now
        if k:
            following = following - safe_ratio(norm, norm_last) * last
        now, last, norm_last = following, now, norm

    lanes = lane_iota(ITERS)
    ra, ca = row_iota(LANES), lane_iota(LANES)
    same = lax.shift_right_logical(ra, 3) == lax.shift_right_logical(ca, 3)
    spread = jnp.concatenate(
        [jnp.where(same & ((ra & (ITERS - 1)) == m), 1.0, 0.0) for m in range(ITERS)], axis=1
    )
    system = jnp.zeros((ITERS, LANES), jnp.float32)
    stacked = []
    for g in range(groups):
        t = jnp.concatenate([c[g : g + 1] for c in common], axis=0)
        stacked.append(t)
        wide = mm(t, spread, precision=EXACT)
        image = jnp.zeros((ITERS, LANES), jnp.float32)
        for m in range(ITERS):
            image = image + turned[g][m : m + 1] * wide[:, m * LANES : (m + 1) * LANES]
        right = jnp.concatenate(
            [image, rhs[g : g + 1], jnp.zeros((LANES - ITERS - 1, LANES), jnp.float32)], axis=0
        )
        system = system + mm(t, right, NT, precision=EXACT)
    rows = row_iota(ITERS)
    for p in range(ITERS):
        pivot_row = system[p : p + 1]
        pivot = jnp.sum(jnp.where(lanes == p, system, 0.0), axis=1, keepdims=True)
        inverse = jnp.sum(jnp.where(rows[:, :1] == p, pivot, 0.0), axis=0, keepdims=True)
        inverse = jnp.where(inverse > 0.0, 1.0 / jnp.where(inverse > 0.0, inverse, 1.0), 0.0)
        pivot_row = pivot_row * inverse
        system = jnp.where(rows == p, pivot_row, system - pivot * pivot_row)
    answer = jnp.sum(jnp.where(lanes == ITERS, system, 0.0), axis=1, keepdims=True)

    weights = [jnp.sum(answer * t, axis=0, keepdims=True) for t in stacked]
    me = where_ref[3]
    mine = []
    for k in range(ITERS):
        w = jnp.zeros((1, 1), jnp.float32)
        for g in range(groups):
            hit = lane_iota(1) == me * ITERS + k - g * LANES
            w = w + jnp.sum(jnp.where(hit, weights[g], 0.0), axis=1, keepdims=True)
        mine.append(w)
    for z in range(own_ref.shape[1]):
        acc = mine[0] * own_ref[0, z]
        for k in range(1, ITERS):
            acc = acc + mine[k] * own_ref[k, z]
        adjoint_ref[z] = acc

    per_group = LANES // ITERS // copies
    sender = lax.div(lane_iota(per_group), jnp.int32(ITERS * copies))
    values = jnp.concatenate(
        [
            mm(jnp.where(sender == row_iota(per_group), weights[g], 0.0), got[g], precision=EXACT)
            for g in range(groups)
        ],
        axis=0,
    )
    rows_at, lanes_at = row_iota(pilot_ref.shape[0]), row_iota(LANES)
    held = lane_iota(peers) < pilot_ref.shape[0] * LANES // peers
    pieces = pieces_of(jnp.where(held, values, 0.0))
    left, right = [[], [], []], []
    room = LANES - SLOTS
    for s in range(peers):
        slot = jnp.where(
            lane_iota(1) < room,
            pltpu.roll(got_ref[s * copies, 0:1, :], room, 1),
            pltpu.roll(got_ref[s * copies, 1:2, :], 2 * room, 1),
        ).astype(jnp.int32)
        hit = rows_at == lax.shift_right_logical(slot, LANE_BITS)
        for q, piece in enumerate(pieces):
            left[q].append(picked(hit, piece[s : s + 1]))
        right.append(
            jnp.where(lanes_at == (slot & (LANES - 1)), 1.0, 0.0).astype(jnp.bfloat16)
        )
    right = jnp.concatenate(right, axis=1)
    pilot_ref[...] = sum(mm(jnp.concatenate(q, axis=1), right, NT) for q in left)


def tied(*values):
    return lax.optimization_barrier(values)


def neighbour_pairs(axis):
    forward = [(i, i + 1) for i in range(lax.axis_size(axis) - 1)]
    return forward, [(b, a) for a, b in forward]


def swapped(x):
    return lax.ppermute(x, "layers", [(0, 1), (1, 0)])


def on_device(
    state_field,
    conductivity,
    storage,
    gauge_owner,
    gauge_cell,
    gauge_value,
    gauge_weight,
    pilot_index,
):
    nz, nx, ny = state_field.shape
    peers = lax.axis_size("cols") * lax.axis_size("rows")
    devices = peers * lax.axis_size("layers")
    gauges = gauge_owner.shape[0]
    capacity = 4 * gauges // peers
    f32 = jnp.float32
    row_count = lax.axis_size("rows")

    def shape(*dims, dtype=f32):
        return jax.ShapeDtypeStruct(dims, dtype)

    def flat(x):
        return x.reshape(gauges // LANES, LANES)

    where = jnp.stack(
        [lax.axis_index(a) for a in ("layers", "rows", "cols", GRID_AXES)]
    ).astype(jnp.int32)

    obs = pltpu.VMEM((gauges // LANES, LANES), f32)
    obs_int = pltpu.VMEM((gauges // LANES, LANES), jnp.int32)
    payload = kernel_call(
        functools.partial(route_body, peers, capacity),
        shape(peers, 3 * capacity // LANES, LANES),
        [obs_int, obs_int, obs, obs, pltpu.SemaphoreType.DMA((4,))],
        weight=5,
    )(in_specs=[ANY] * 4, out_specs=VMEM)(
        flat(gauge_owner), flat(gauge_cell), flat(gauge_value), flat(gauge_weight)
    )
    payload, pilot_index = tied(payload, pilot_index)
    got = lax.all_to_all(payload, PEER_AXES, 0, 0, tiled=True)
    spot, slots = kernel_call(
        pilot_body, (shape(nx // 4, LANES, dtype=jnp.int32), shape(peers, LANES))
    )(in_specs=[VMEM], out_specs=(VMEM, VMEM))(pilot_index)

    fixed = (conductivity, storage, state_field)
    got, spot, *fixed = tied(got, spot, *fixed)
    fixed_other = [swapped(x) for x in fixed]
    edge = shape(4, nz, HALO, LANES)
    source, up, down = kernel_call(
        functools.partial(source_body, capacity // LANES),
        (shape(nz, nx, LANES), edge, edge),
        [pltpu.VMEM((nz * nx, 3 * LANES), f32)],
        weight=10,
    )(in_specs=[VMEM] * 4, out_specs=(VMEM,) * 3)(got, *fixed)
    forward, backward = neighbour_pairs("cols")
    low = lax.ppermute(up, "cols", forward)
    high = lax.ppermute(down, "cols", backward)
    other = swapped(source)

    mine = (*fixed, source)

    def packed(low_side):
        return kernel_call(
            functools.partial(pack_body, low_side), shape(2 * nz, HALO, LANES)
        )(in_specs=[SMEM] + [VMEM] * 6, out_specs=VMEM)(where, *mine, low, high)

    if row_count == 2:
        sides = [lax.ppermute(packed(None), "rows", [(0, 1), (1, 0)])]
    else:
        forward, backward = neighbour_pairs("rows")
        sides = [
            lax.ppermute(packed(False), "rows", forward),
            lax.ppermute(packed(True), "rows", backward),
        ]
    edges = [low, high, swapped(low), swapped(high)]
    sides = sides + [swapped(x) for x in sides]

    each = nx * ny // 8 // LANES
    planes, width = 2 * nz, nx + 2 * HALO
    padded = pltpu.VMEM((planes, width, 2 * LANES), f32)
    own, send = kernel_call(
        functools.partial(basis_body, peers, len(sides) // 2),
        (shape(ITERS, nz, nx, LANES), shape(devices, ITERS, LANES)),
        [padded] * 8
        + [
            pltpu.VMEM((ITERS + 1, planes, width, 2 * LANES), f32),
            pltpu.VMEM((6, nz, nx, LANES), f32),
        ],
        weight=10,
    )(in_specs=[SMEM] + [VMEM] * (14 + len(sides)), out_specs=(VMEM, VMEM))(
        where, *mine, *fixed_other, other, *edges, *sides, spot, slots
    )
    parts = lax.all_to_all(send, GRID_AXES, 0, 0, tiled=True)
    adjoint, pilot = kernel_call(
        functools.partial(solve_body, devices // peers), (shape(nz, nx, ny), shape(each, LANES))
    )(in_specs=[SMEM] + [VMEM] * 2, out_specs=(VMEM, VMEM))(where, parts, own)
    return adjoint, pilot.reshape(-1)


def solution(mesh):
    return jax.shard_map(
        on_device,
        mesh=mesh,
        in_specs=(
            P(("groups", "layers"), "cols", "rows"),
            P(("groups", "layers"), "cols", "rows"),
            P(("groups", "layers"), "cols", "rows"),
            P(("groups", "cols", "rows", "layers")),
            P(("groups", "cols", "rows", "layers")),
            P(("groups", "cols", "rows", "layers")),
            P(("groups", "cols", "rows", "layers")),
            P("cols", "rows"),
        ),
        out_specs=(P(("groups", "layers"), "cols", "rows"), P(("groups", "cols", "rows"))),
        check_vma=False,
    )
```

time: 90.8 us -> 73.3 us (0.81)
  starting transfers between devices: 22.9 us -> 13.5 us
  blocking collectives: 15.7 us -> 10.2 us
  waiting for transfers between devices: 17.1 us -> 15 us
  Pallas kernels: 28.3 us -> 30.2 us
  other arithmetic: 1.78 us -> 0.08 us
    ppermute x8 -> x10, starting transfers between devices: 12.2 us -> 6.15 us  [the longest x1 2.19 us: on_device(): low = lax.ppermute(up, 'cols', forward)]
    all_to_all x1, blocking collectives: 15.7 us -> 10.2 us  [on_device(): parts = lax.all_to_all(send, GRID_AXES, 0, 0, tiled=True)]
    all_to_all x1 -> x0, starting transfers between devices: 3.47 us -> none  [on_device(): measures = lax.all_to_all(local, GRID_AXES, 0, 0, tiled=True)]
    ppermute x8 -> x10, waiting for transfers between devices: 10.3 us -> 8.39 us  [the longest x1 4.21 us: on_device(): high = lax.ppermute(down, 'cols', backward)]
    pallas_call x4 -> x5, Pallas kernels: 23.9 us -> 25.7 us  [the longest x1 10.3 us: on_device(): kernel_call(functools.partial(source_body, capacity // LANES), (shape(nz,...]
    another operation x1, other arithmetic: 1.06 us -> 0.08 us  [on_device(): jnp.stack([lax.axis_index(a) for a in ('layers', 'rows', 'cols', GRID_AXE...]
  transfers between devices with their start and end apart: 10 -> 11, of which waited for: 4 -> 5; matrix products, arithmetic and copies ran while one was open for 3% -> 0% of each run, Pallas kernels for 14% -> 3%
where the time goes in v2:
time: 73.3 us; the launch traced here: 72.7 us
  Pallas kernels  30.2 us (41%)
  waiting for transfers between devices  15 us (20%)
  starting transfers between devices  13.5 us (18%)
  blocking collectives  10.2 us (14%)
  local copies, waits for them, and re-layouts  2.88 us (4%)
  between operations  0.74 us (1%)
    pallas_call x1, Pallas kernels, on_device(): kernel_call(functools.partial(source_body, capacity // LANES), (shape(nz,...  10.3 us
    all_to_all x1, blocking collectives, on_device(): parts = lax.all_to_all(send, GRID_AXES, 0, 0, tiled=True)  10.2 us
    pallas_call x1, Pallas kernels, on_device(): kernel_call(functools.partial(basis_body, peers, len(sides) // 2), (shape...  9.13 us
    all_to_all x1, starting transfers between devices, on_device(): got = lax.all_to_all(payload, PEER_AXES, 0, 0, tiled=True)  7.4 us
    all_to_all x1, waiting for transfers between devices, on_device(): got = lax.all_to_all(payload, PEER_AXES, 0, 0, tiled=True)  6.65 us
    pallas_call x1, Pallas kernels, on_device(): kernel_call(functools.partial(route_body, peers, capacity), shape(peers,...  4.49 us
    ppermute x1, waiting for transfers between devices, on_device(): high = lax.ppermute(down, 'cols', backward)  4.21 us
    pallas_call x1, Pallas kernels, on_device(): kernel_call(functools.partial(solve_body, devices // peers), (shape(nz, n...  4.11 us
  transfers between devices with their start and end apart: 11, of which 5 were waited for; matrix products, arithmetic and copies ran while one was open for 0% of the time, Pallas kernels for 3%

profile of v2, /device:TPU:0, one launch (start us, length us, event | category | flops | bytes accessed | tf_op | source)
XLA Modules:
  0.0 72.7 jit_solution(7080408576691698521)
XLA Ops:
  0.6 0.0 copy-start.3
  0.6 0.7 copy-done.3
  1.4 0.0 copy-start.4
  1.4 0.7 copy-done.4
  2.1 0.0 copy-start.5
  2.1 0.7 copy-done.5
  2.8 0.0 copy-start.6
  2.8 0.7 copy-done.6
  3.5 0.0 copy-start.7
  3.5 4.5 %shard_map.95 = f32[8,48,128]{2,1,0:T(8,128)} custom-call(s32[32,128]{1,0:T(8,128)S(1)} %bitcast.9, s32[32,128]{1,0:T(8,128)S(1)} %bitcast.10, f32[32,128]{1,0:T(8,128)S(1)} %bitcast.11, f32[32,128]{1,0:T(8,128)S(1)} %bitcast.12), custom_call_target="tpu_custom_call" | custom-call | bytes 15000000 | tf_op jit(solution)/shard_map/pallas_call | solution.py:602
  8.0 0.0 copy-start
  8.0 0.0 copy-start.1
  8.0 0.0 copy-start.2
  8.0 7.4 %all-to-all-start = ((f32[8,48,128]{2,1,0:T(8,128)}), f32[8,48,128]{2,1,0:T(8,128)S(1)}, u32[]{:S(2)}, u32[]{:S(2)}) async-start(f32[8,48,128]{2,1,0:T(8,128)} %shard_map.95), calls=%async_computation | async-start | bytes 393216 | tf_op jit(solution)/shard_map/all_to_all | solution.py:611
  15.4 0.0 copy-done.7
  15.4 1.3 %shard_map.96 = (s32[8,128]{1,0:T(8,128)S(1)}, f32[8,128]{1,0:T(8,128)S(1)}) custom-call(s32[32,128]{1,0:T(8,128)S(1)} %copy-done.7), custom_call_target="tpu_custom_call" | custom-call | bytes 3000000 | tf_op jit(solution)/shard_map/pallas_call | solution.py:612
  16.7 6.7 %all-to-all-done.got_ref = f32[8,48,128]{2,1,0:T(8,128)S(1)} async-done(((f32[8,48,128]{2,1,0:T(8,128)}), f32[8,48,128]{2,1,0:T(8,128)S(1)}, u32[]{:S(2)}, u32[]{:S(2)}) %all-to-all-start) | async-done | bytes 196640 | tf_op jit(solution)/shard_map/all_to_all | solution.py:611
  23.4 0.0 copy-done
  23.4 0.0 copy-done.1
  23.4 0.0 copy-done.2
  23.4 10.3 %shard_map.97 = (f32[8,32,128]{2,1,0:T(8,128)S(1)}, f32[4,8,8,128]{3,2,1,0:T(8,128)S(1)}, f32[4,8,8,128]{3,2,1,0:T(8,128)S(1)}) custom-call(f32[8,48,128]{2,1,0:T(8,128)S(1)} %all-to-all-done.got_ref, f32[8,32,128]{2,1,0:T(8,128)S(1)} %copy-done, f32[8,32,128]{2,1,0:T(8,128)S(1)} %copy-done.1, f32[8,32,128]{2,1,0:T(8,128)S(1)} %copy-done.2), custom_call_target="tpu_custom_call" | custom-call | bytes 30000000 | tf_op jit(solution)/shard_map/pallas_call | solution.py:620
  33.7 2.2 %collective-permute-start.4 = (f32[4,8,8,128]{3,2,1,0:T(8,128)S(1)}, f32[4,8,8,128]{3,2,1,0:T(8,128)S(1)}, u32[]{:S(2)}, u32[]{:S(2)}) collective-permute-start(f32[4,8,8,128]{3,2,1,0:T(8,128)S(1)} %get-tuple-element.26), channel_id=1, source_target_pairs={{0,4},{4,8},{8,12},{1,5},{5,9},{9,13},{2,6},{6,10},{10,14},{3,7},{... | collective-permute-start | bytes 393224 | tf_op jit(solution)/shard_map/ppermute | solution.py:627
  35.9 1.5 %collective-permute-start.5 = (f32[4,8,8,128]{3,2,1,0:T(8,128)S(1)}, f32[4,8,8,128]{3,2,1,0:T(8,128)S(1)}, u32[]{:S(2)}, u32[]{:S(2)}) collective-permute-start(f32[4,8,8,128]{3,2,1,0:T(8,128)S(1)} %get-tuple-element.27), channel_id=1, source_target_pairs={{4,0},{8,4},{12,8},{5,1},{9,5},{13,9},{6,2},{10,6},{14,10},{7,3},{... | collective-permute-start | bytes 393224 | tf_op jit(solution)/shard_map/ppermute | solution.py:628
  37.4 0.1 collective-permute-start
  37.4 0.5 collective-permute-start.1
  37.9 0.1 pad_add_fusion.where_ref
  38.0 0.1 collective-permute-start.2
  38.1 0.3 collective-permute-done.4.refs_4_.refs_8_
  38.4 0.2 collective-permute-start.3
  38.5 4.2 %collective-permute-done.5.refs_5_.refs_9_ = f32[4,8,8,128]{3,2,1,0:T(8,128)S(1)} collective-permute-done((f32[4,8,8,128]{3,2,1,0:T(8,128)S(1)}, f32[4,8,8,128]{3,2,1,0:T(8,128)S(1)}, u32[]{:S(2)}, u32[]{:S(2)}) %collective-permute-start.5) | collective-permute-done | bytes 131104 | tf_op jit(solution)/shard_map/ppermute | solution.py:628
  42.7 0.9 %shard_map.98 = f32[16,8,128]{2,1,0:T(8,128)S(1)} custom-call(s32[4]{0:T(128)S(1)} %pad_add_fusion.where_ref, f32[8,32,128]{2,1,0:T(8,128)S(1)} %copy-done, f32[8,32,128]{2,1,0:T(8,128)S(1)} %copy-done.1, f32[8,32,128]{2,1,0:T(8,128)S(1)} %copy-done.2, f32[8,32,128]{2,1,0:T(8,128)S(1)} %get-tuple-element.25.refs_3_, ...), custom_call_target="tpu_custom_call" | custom-call | bytes 3000000 | tf_op jit(solution)/shard_map/pallas_call | solution.py:634
  43.6 1.2 %collective-permute-start.8 = (f32[16,8,128]{2,1,0:T(8,128)S(1)}, f32[16,8,128]{2,1,0:T(8,128)S(1)}, u32[]{:S(2)}, u32[]{:S(2)}) collective-permute-start(f32[16,8,128]{2,1,0:T(8,128)S(1)} %shard_map.98), channel_id=1, source_target_pairs={{0,2},{2,0},{1,3},{3,1},{4,6},{6,4},{5,7},{7,5},{8,10},{10,8},{9,1... | collective-permute-start | bytes 196616 | tf_op jit(solution)/shard_map/ppermute | solution.py:639
  44.8 0.0 collective-permute-done.refs_4_
  44.8 0.0 collective-permute-start.6
  44.8 0.0 collective-permute-done.1.refs_5_
  44.8 0.5 collective-permute-start.7
  45.3 2.6 %collective-permute-done.8.refs_12_ = f32[16,8,128]{2,1,0:T(8,128)S(1)} collective-permute-done((f32[16,8,128]{2,1,0:T(8,128)S(1)}, f32[16,8,128]{2,1,0:T(8,128)S(1)}, u32[]{:S(2)}, u32[]{:S(2)}) %collective-permute-start.8) | collective-permute-done | bytes 65568 | tf_op jit(solution)/shard_map/ppermute | solution.py:639
  48.0 0.0 collective-permute-start.9
  48.0 0.0 collective-permute-done.2.refs_6_
  48.0 0.0 collective-permute-done.3.refs_7_
  48.0 1.2 %collective-permute-done.9.refs_13_ = f32[16,8,128]{2,1,0:T(8,128)S(1)} collective-permute-done((f32[16,8,128]{2,1,0:T(8,128)S(1)}, f32[16,8,128]{2,1,0:T(8,128)S(1)}, u32[]{:S(2)}, u32[]{:S(2)}) %collective-permute-start.9) | collective-permute-done | bytes 65568 | tf_op jit(solution)/shard_map/ppermute | solution.py:569
  49.2 0.0 collective-permute-done.6.refs_10_
  49.2 0.0 collective-permute-done.7.refs_11_
  49.2 9.1 %shard_map.99 = (f32[8,8,32,128]{3,2,1,0:T(8,128)S(1)}, f32[16,8,128]{2,1,0:T(8,128)S(1)}) custom-call(s32[4]{0:T(128)S(1)} %pad_add_fusion.where_ref, f32[8,32,128]{2,1,0:T(8,128)S(1)} %copy-done, f32[8,32,128]{2,1,0:T(8,128)S(1)} %copy-done.1, f32[8,32,128]{2,1,0:T(8,128)S(1)} %copy-done.2, f32[8,32,128]{2,1,0:T(8,128)S(1)} %get-tuple-element.25.refs_3_, ...), custom_call_target="tpu_custom_call" | custom-call | bytes 30000000 | tf_op jit(solution)/shard_map/pallas_call | solution.py:652
  58.4 10.2 %all_to_all.10.got_ref = f32[16,8,128]{2,1,0:T(8,128)S(1)} all-to-all(f32[16,8,128]{2,1,0:T(8,128)S(1)} %get-tuple-element.30), channel_id=1, replica_groups=mesh['groups'=2,'cols'=4,'rows'=2,'layers'=2] {'cols','rows','layers'}, dimensions={0} | all-to-all | bytes 131072 | tf_op jit(solution)/shard_map/all_to_all | solution.py:664
  68.6 4.1 %shard_map.100 = (f32[8,32,128]{2,1,0:T(8,128)}, f32[4,128]{1,0:T(4,128)}) custom-call(s32[4]{0:T(128)S(1)} %pad_add_fusion.where_ref, f32[16,8,128]{2,1,0:T(8,128)S(1)} %all_to_all.10.got_ref, f32[8,8,32,128]{3,2,1,0:T(8,128)S(1)} %get-tuple-element.31.own_ref), custom_call_target="tpu_custom_call" | custom-call | bytes 3000000 | tf_op jit(solution)/shard_map/pallas_call | solution.py:665
Async XLA Ops:
  0.6 0.7 copy-start.3
  1.4 0.7 copy-start.4
  2.1 0.7 copy-start.5
  2.8 0.7 copy-start.6
  3.5 11.9 %copy-start.7 = (s32[32,128]{1,0:T(8,128)S(1)}, s32[32,128]{1,0:T(8,128)}, u32[]{:S(2)}) copy-start(s32[32,128]{1,0:T(8,128)} %pilot_ref) | copy-start | bytes 49156
  8.0 15.4 %copy-start = (f32[8,32,128]{2,1,0:T(8,128)S(1)}, f32[8,32,128]{2,1,0:T(8,128)}, u32[]{:S(2)}) copy-start(f32[8,32,128]{2,1,0:T(8,128)} %refs_0_.1) | copy-start | bytes 393220
  8.0 15.4 %copy-start.1 = (f32[8,32,128]{2,1,0:T(8,128)S(1)}, f32[8,32,128]{2,1,0:T(8,128)}, u32[]{:S(2)}) copy-start(f32[8,32,128]{2,1,0:T(8,128)} %refs_1_.1) | copy-start | bytes 393220
  8.0 15.4 %copy-start.2 = (f32[8,32,128]{2,1,0:T(8,128)S(1)}, f32[8,32,128]{2,1,0:T(8,128)}, u32[]{:S(2)}) copy-start(f32[8,32,128]{2,1,0:T(8,128)} %refs_2_.1) | copy-start | bytes 393220
  8.0 15.4 %all-to-all-start = ((f32[8,48,128]{2,1,0:T(8,128)}), f32[8,48,128]{2,1,0:T(8,128)S(1)}, u32[]{:S(2)}, u32[]{:S(2)}) async-start(f32[8,48,128]{2,1,0:T(8,128)} %shard_map.95), calls=%async_computation | async-start | bytes 393216 | tf_op jit(solution)/shard_map/all_to_all | solution.py:611
  33.7 4.7 %collective-permute-start.4 = (f32[4,8,8,128]{3,2,1,0:T(8,128)S(1)}, f32[4,8,8,128]{3,2,1,0:T(8,128)S(1)}, u32[]{:S(2)}, u32[]{:S(2)}) collective-permute-start(f32[4,8,8,128]{3,2,1,0:T(8,128)S(1)} %get-tuple-element.26), channel_id=1, source_target_pairs={{0,4},{4,8},{8,12},{1,5},{5,9},{9,13},{2,6},{6,10},{10,14},{3,7},{... | collective-permute-start | bytes 393224 | tf_op jit(solution)/shard_map/ppermute | solution.py:627
  35.9 6.9 %collective-permute-start.5 = (f32[4,8,8,128]{3,2,1,0:T(8,128)S(1)}, f32[4,8,8,128]{3,2,1,0:T(8,128)S(1)}, u32[]{:S(2)}, u32[]{:S(2)}) collective-permute-start(f32[4,8,8,128]{3,2,1,0:T(8,128)S(1)} %get-tuple-element.27), channel_id=1, source_target_pairs={{4,0},{8,4},{12,8},{5,1},{9,5},{13,9},{6,2},{10,6},{14,10},{7,3},{... | collective-permute-start | bytes 393224 | tf_op jit(solution)/shard_map/ppermute | solution.py:628
  37.4 7.5 %collective-permute-start = (f32[8,32,128]{2,1,0:T(8,128)S(1)}, f32[8,32,128]{2,1,0:T(8,128)S(1)}, u32[]{:S(2)}, u32[]{:S(2)}) collective-permute-start(f32[8,32,128]{2,1,0:T(8,128)S(1)} %copy-done), channel_id=1, source_target_pairs={{0,1},{1,0},{2,3},{3,2},{4,5},{5,4},{6,7},{7,6},{8,9},{9,8},{10,11... | collective-permute-start | bytes 393224 | tf_op jit(solution)/shard_map/ppermute | solution.py:569
  37.4 7.4 %collective-permute-start.1 = (f32[8,32,128]{2,1,0:T(8,128)S(1)}, f32[8,32,128]{2,1,0:T(8,128)S(1)}, u32[]{:S(2)}, u32[]{:S(2)}) collective-permute-start(f32[8,32,128]{2,1,0:T(8,128)S(1)} %copy-done.1), channel_id=1, source_target_pairs={{0,1},{1,0},{2,3},{3,2},{4,5},{5,4},{6,7},{7,6},{8,9},{9,8},{10,11... | collective-permute-start | bytes 393224 | tf_op jit(solution)/shard_map/ppermute | solution.py:569
  38.0 10.0 %collective-permute-start.2 = (f32[8,32,128]{2,1,0:T(8,128)S(1)}, f32[8,32,128]{2,1,0:T(8,128)S(1)}, u32[]{:S(2)}, u32[]{:S(2)}) collective-permute-start(f32[8,32,128]{2,1,0:T(8,128)S(1)} %copy-done.2), channel_id=1, source_target_pairs={{0,1},{1,0},{2,3},{3,2},{4,5},{5,4},{6,7},{7,6},{8,9},{9,8},{10,11... | collective-permute-start | bytes 393224 | tf_op jit(solution)/shard_map/ppermute | solution.py:569
  38.4 9.6 %collective-permute-start.3 = (f32[8,32,128]{2,1,0:T(8,128)S(1)}, f32[8,32,128]{2,1,0:T(8,128)S(1)}, u32[]{:S(2)}, u32[]{:S(2)}) collective-permute-start(f32[8,32,128]{2,1,0:T(8,128)S(1)} %get-tuple-element.25.refs_3_), channel_id=1, source_target_pairs={{0,1},{1,0},{2,3},{3,2},{4,5},{5,4},{6,7},{7,6},{8,9},{9,8},{10,11... | collective-permute-start | bytes 393224 | tf_op jit(solution)/shard_map/ppermute | solution.py:569
  43.6 4.3 %collective-permute-start.8 = (f32[16,8,128]{2,1,0:T(8,128)S(1)}, f32[16,8,128]{2,1,0:T(8,128)S(1)}, u32[]{:S(2)}, u32[]{:S(2)}) collective-permute-start(f32[16,8,128]{2,1,0:T(8,128)S(1)} %shard_map.98), channel_id=1, source_target_pairs={{0,2},{2,0},{1,3},{3,1},{4,6},{6,4},{5,7},{7,5},{8,10},{10,8},{9,1... | collective-permute-start | bytes 196616 | tf_op jit(solution)/shard_map/ppermute | solution.py:639
  44.8 4.4 %collective-permute-start.6 = (f32[4,8,8,128]{3,2,1,0:T(8,128)S(1)}, f32[4,8,8,128]{3,2,1,0:T(8,128)S(1)}, u32[]{:S(2)}, u32[]{:S(2)}) collective-permute-start(f32[4,8,8,128]{3,2,1,0:T(8,128)S(1)} %collective-permute-done.4.refs_4_.refs_8_), channel_id=1, source_target_pairs={{0,1},{1,0},{2,3},{3,2},{4,5},{5,4},{6,7},{7,6},{8,9},{9,8},{10,11... | collective-permute-start | bytes 393224 | tf_op jit(solution)/shard_map/ppermute | solution.py:569
  44.8 4.4 %collective-permute-start.7 = (f32[4,8,8,128]{3,2,1,0:T(8,128)S(1)}, f32[4,8,8,128]{3,2,1,0:T(8,128)S(1)}, u32[]{:S(2)}, u32[]{:S(2)}) collective-permute-start(f32[4,8,8,128]{3,2,1,0:T(8,128)S(1)} %collective-permute-done.5.refs_5_.refs_9_), channel_id=1, source_target_pairs={{0,1},{1,0},{2,3},{3,2},{4,5},{5,4},{6,7},{7,6},{8,9},{9,8},{10,11... | collective-permute-start | bytes 393224 | tf_op jit(solution)/shard_map/ppermute | solution.py:569
  48.0 1.3 %collective-permute-start.9 = (f32[16,8,128]{2,1,0:T(8,128)S(1)}, f32[16,8,128]{2,1,0:T(8,128)S(1)}, u32[]{:S(2)}, u32[]{:S(2)}) collective-permute-start(f32[16,8,128]{2,1,0:T(8,128)S(1)} %collective-permute-done.8.refs_12_), channel_id=1, source_target_pairs={{0,1},{1,0},{2,3},{3,2},{4,5},{5,4},{6,7},{7,6},{8,9},{9,8},{10,11... | collective-permute-start | bytes 196616 | tf_op jit(solution)/shard_map/ppermute | solution.py:569

commit v3 on v2

--- a/solution.py
+++ b/solution.py
@@ -20,13 +20,13 @@
 VMEM_BYTES = 50 * 1024 * 1024
 
 
-def kernel_call(body, out_shape, scratch=(), weight=1):
+def kernel_call(body, out_shape, scratch=(), weight=1, vmem=VMEM_BYTES):
     return functools.partial(
         pl.pallas_call,
         body,
         out_shape=out_shape,
         scratch_shapes=list(scratch),
-        compiler_params=pltpu.CompilerParams(vmem_limit_bytes=VMEM_BYTES),
+        compiler_params=pltpu.CompilerParams(vmem_limit_bytes=vmem),
         cost_estimate=pl.CostEstimate(
             flops=0, bytes_accessed=weight * 3_000_000, transcendentals=0
         ),
@@ -35,7 +35,7 @@
 
 VMEM = pl.BlockSpec(memory_space=pltpu.VMEM)
 SMEM = pl.BlockSpec(memory_space=pltpu.SMEM)
-ANY = pl.BlockSpec(memory_space=pl.ANY)
+HBM = pl.BlockSpec(memory_space=pltpu.HBM)
 
 
 def pieces_of(x):
@@ -55,6 +55,23 @@
 
 def picked(mask, row):
     return jnp.where(mask, row, jnp.zeros_like(row)).astype(jnp.bfloat16)
+
+
+TILE = 16
+
+
+def spread16(x, r):
+    return jnp.broadcast_to(x[r : r + 1], (TILE, LANES)).astype(jnp.bfloat16)
+
+
+def hits16(count, row):
+    at = row_iota(TILE).astype(jnp.float32).astype(jnp.bfloat16)
+    return [at + jnp.bfloat16(TILE * i) == row for i in range(count // TILE)]
+
+
+def filled16(masks, value):
+    zero = jnp.zeros((TILE, LANES), jnp.bfloat16)
+    return jnp.concatenate([jnp.where(m, value, zero) for m in masks], axis=0)
 
 
 def mm(a, b, dims=(((1,), (0,)), ((), ())), precision=None):
@@ -68,19 +85,18 @@
     earlier_row = jnp.where(row_iota(rows, rows) > lane_iota(rows, rows), 1.0, 0.0).astype(
         jnp.bfloat16
     )
-
-    def one(peer, rank):
-        hit = owner == peer
-        counts = mm(jnp.where(hit, 1.0, 0.0).astype(jnp.bfloat16), earlier_lane)
-        before = mm(earlier_row, counts[:, LANES:].astype(jnp.bfloat16))
-        return rank + jnp.where(hit, counts[:, :LANES] + before, 0.0)
-
+    hits = [owner == peer for peer in range(peers)]
+    ones = jnp.concatenate([jnp.where(h, 1.0, 0.0).astype(jnp.bfloat16) for h in hits], axis=0)
+    counts = mm(ones, earlier_lane)
+    part = [counts[p * rows : (p + 1) * rows] for p in range(peers)]
+    before = mm(
+        earlier_row, jnp.concatenate([c[:, LANES:] for c in part], axis=1).astype(jnp.bfloat16)
+    )
     rank = jnp.zeros((rows, LANES), jnp.float32)
-    if peers <= 16:
-        for peer in range(peers):
-            rank = one(peer, rank)
-    else:
-        rank = lax.fori_loop(0, peers, one, rank)
+    for p in range(peers):
+        rank = jnp.where(
+            hits[p], part[p][:, :LANES] + before[:, p * LANES : (p + 1) * LANES], rank
+        )
     return rank.astype(jnp.int32)
 
 
@@ -106,8 +122,8 @@
     rows = owner_ref.shape[0]
     owner = owner_ref[...]
     position = owner * capacity + ranks(owner, peers)
-    slot_row = lax.shift_right_logical(position, LANE_BITS)
-    slot_lane = position & (LANES - 1)
+    slot_row = lax.shift_right_logical(position, LANE_BITS).astype(jnp.float32)
+    slot_lane = (position & (LANES - 1)).astype(jnp.float32)
     cell = cell_ref[...]
     columns = [
         lax.shift_right_logical(cell, LANE_BITS).astype(jnp.float32),
@@ -116,28 +132,26 @@
         *pieces_of(weight_ref[...]),
     ]
     slot_rows = peers * capacity // LANES
-    rows_at, lanes_at = row_iota(slot_rows), row_iota(LANES)
-    total = jnp.zeros((slot_rows, len(columns) * LANES), jnp.float32)
-    step = 8
-    for start in range(0, rows, step):
-        left, right = [], [[] for _ in columns]
-        for r in range(start, start + step):
-            left.append(
-                jnp.where(rows_at == slot_row[r : r + 1], 1.0, 0.0).astype(jnp.bfloat16)
-            )
-            lane_hit = lanes_at == slot_lane[r : r + 1]
+    one = jnp.ones((TILE, LANES), jnp.bfloat16)
+    total = None
+    for start in range(0, rows, TILE):
+        at_row, at_lane = [], [[] for _ in columns]
+        for r in range(start, start + TILE):
+            at_row.append(filled16(hits16(slot_rows, spread16(slot_row, r)), one))
+            masks = hits16(LANES, spread16(slot_lane, r))
             for q, column in enumerate(columns):
-                right[q].append(picked(lane_hit, column[r : r + 1]))
-        right = jnp.concatenate([jnp.concatenate(q, axis=1) for q in right], axis=0)
-        total = total + mm(jnp.concatenate(left, axis=1), right, NT)
-    part = [total[:, q * LANES : (q + 1) * LANES] for q in range(len(columns))]
+                at_lane[q].append(filled16(masks, spread16(column, r)))
+        at_lane = jnp.concatenate([jnp.concatenate(q, axis=1) for q in at_lane], axis=0)
+        part = mm(at_lane, jnp.concatenate(at_row, axis=1), NT)
+        total = part if total is None else total + part
+    part = [total[q * LANES : (q + 1) * LANES] for q in range(len(columns))]
     fields = [
         part[0] * LANES + part[1],
         part[2] + part[3] + part[4],
         part[5] + part[6] + part[7],
     ]
+    fields = [jnp.transpose(f) for f in fields]
     each = capacity // LANES
-
     for peer in range(peers):
         for q, field in enumerate(fields):
             out_ref[peer, q * each : (q + 1) * each, :] = field[peer * each : (peer + 1) * each]
@@ -169,46 +183,49 @@
 
 
 def source_body(
-    each, got_ref, conductivity_ref, storage_ref, state_ref, out_ref, up_ref, down_ref, acc_ref
+    each, got_ref, conductivity_ref, storage_ref, state_ref, out_ref, up_ref, down_ref
 ):
     peers = got_ref.shape[0]
-    nz, nx = conductivity_ref.shape[0], conductivity_ref.shape[1]
+    nz, nx = state_ref.shape[0], state_ref.shape[1]
     cells = nz * nx
-    state_t = jnp.concatenate(
-        [p.astype(jnp.bfloat16) for p in pieces_of(jnp.transpose(state_ref[...].reshape(cells, LANES)))], axis=0
-    )
-    acc_ref[...] = jnp.zeros_like(acc_ref)
-    rows_at, lanes_at = row_iota(cells), row_iota(LANES)
-
-    def one_peer(peer, carry):
-        cell = got_ref[peer, 0:each, :].astype(jnp.int32)
-        value = got_ref[peer, each : 2 * each, :]
-        weight = got_ref[peer, 2 * each : 3 * each, :]
+    one = jnp.ones((TILE, LANES), jnp.bfloat16)
+
+    def sixteen(group, q):
+        peer, row = divmod(group * TILE, each)
+        if each >= TILE:
+            return got_ref[peer, q * each + row : q * each + row + TILE, :]
+        return jnp.concatenate(
+            [got_ref[peer + i, q * each : (q + 1) * each, :] for i in range(TILE // each)], axis=0
+        )
+
+    total = None
+    for group in range(peers * each // TILE):
+        cell = sixteen(group, 0).astype(jnp.int32)
         high = lax.shift_right_logical(cell, LANE_BITS)
         low = cell & (LANES - 1)
-        row_hits = jnp.concatenate(
-            [
-                jnp.where(rows_at == high[r : r + 1], 1.0, 0.0).astype(jnp.bfloat16)
-                for r in range(each)
-            ],
-            axis=1,
-        )
-        heads = mm(state_t, row_hits)
-        right = [[], [], []]
-        for r in range(each):
-            lane_hit = lanes_at == low[r : r + 1]
-            here = heads[:, r * LANES : (r + 1) * LANES]
-            head = here[:LANES] + here[LANES : 2 * LANES] + here[2 * LANES :]
-            head = jnp.sum(jnp.where(lane_hit, head, 0.0), axis=0, keepdims=True)
-            misfit = weight[r : r + 1] * (head - value[r : r + 1])
-            for q, piece in enumerate(pieces_of(misfit)):
-                right[q].append(picked(lane_hit, piece))
-        right = jnp.concatenate([jnp.concatenate(q, axis=1) for q in right], axis=0)
-        acc_ref[...] += mm(row_hits, right, NT)
-        return carry
-
-    lax.fori_loop(0, peers, one_peer, 0)
-    total = acc_ref[:, :LANES] + acc_ref[:, LANES : 2 * LANES] + acc_ref[:, 2 * LANES :]
+        heads = []
+        for r in range(0, TILE, 8):
+            head = jnp.zeros((8, LANES), jnp.float32)
+            for z in range(nz):
+                for x in range(nx):
+                    line = jnp.broadcast_to(state_ref[z, x : x + 1, :], (8, LANES))
+                    line = jnp.take_along_axis(line, low[r : r + 8], axis=1)
+                    head = jnp.where(high[r : r + 8] == z * nx + x, line, head)
+            heads.append(head)
+        misfit = sixteen(group, 2) * (jnp.concatenate(heads, axis=0) - sixteen(group, 1))
+        coarse = misfit.astype(jnp.bfloat16).astype(jnp.float32)
+        pieces = (coarse, misfit - coarse)
+        high, low = high.astype(jnp.float32), low.astype(jnp.float32)
+        at_row, at_lane = [], [[] for _ in pieces]
+        for r in range(TILE):
+            at_row.append(filled16(hits16(cells, spread16(high, r)), one))
+            masks = hits16(LANES, spread16(low, r))
+            for q, piece in enumerate(pieces):
+                at_lane[q].append(filled16(masks, spread16(piece, r)))
+        at_lane = jnp.concatenate([jnp.concatenate(q, axis=1) for q in at_lane], axis=0)
+        part = mm(at_lane, jnp.concatenate(at_row, axis=1), NT)
+        total = part if total is None else total + part
+    total = jnp.transpose(total[:LANES] + total[LANES:])
     out_ref[...] = total.reshape(nz, nx, LANES)
     for f, field in enumerate((conductivity_ref, storage_ref, state_ref, out_ref)):
         up_ref[f] = field[:, nx - HALO :, :]
@@ -604,7 +621,8 @@
         shape(peers, 3 * capacity // LANES, LANES),
         [obs_int, obs_int, obs, obs, pltpu.SemaphoreType.DMA((4,))],
         weight=5,
-    )(in_specs=[ANY] * 4, out_specs=VMEM)(
+        vmem=64 * 1024 * 1024,
+    )(in_specs=[HBM] * 4, out_specs=VMEM)(
         flat(gauge_owner), flat(gauge_cell), flat(gauge_value), flat(gauge_weight)
     )
     payload, pilot_index = tied(payload, pilot_index)
@@ -620,8 +638,7 @@
     source, up, down = kernel_call(
         functools.partial(source_body, capacity // LANES),
         (shape(nz, nx, LANES), edge, edge),
-        [pltpu.VMEM((nz * nx, 3 * LANES), f32)],
-        weight=10,
+        weight=6,
     )(in_specs=[VMEM] * 4, out_specs=(VMEM,) * 3)(got, *fixed)
     forward, backward = neighbour_pairs("cols")
     low = lax.ppermute(up, "cols", forward)

time: 73.3 us -> 65 us (0.89)
  Pallas kernels: 30.2 us -> 24 us
  local copies, waits for them, and re-layouts: 2.88 us -> 0.73 us
    pallas_call x1, Pallas kernels: 10.3 us -> 5.19 us  [on_device(): kernel_call(functools.partial(source_body, capacity // LANES), (shape(nz,...]
    unnamed x16 -> x8, local copies, waits for them, and re-layouts: 2.88 us -> 0.73 us
    pallas_call x1, Pallas kernels: 1.29 us -> 0.48 us  [on_device(): kernel_call(pilot_body, (shape(nx // 4, LANES, dtype=jnp.int32), shape(pe...]
  transfers between devices with their start and end apart: 11 -> 11, of which waited for: 5 -> 5; matrix products, arithmetic and copies ran while one was open for 0% -> 0% of each run, Pallas kernels for 3% -> 2%
where the time goes in v3:
time: 65 us; the launch traced here: 64.5 us
  Pallas kernels  24 us (37%)
  waiting for transfers between devices  15.1 us (23%)
  starting transfers between devices  13.5 us (21%)
  blocking collectives  10.2 us (16%)
  local copies, waits for them, and re-layouts  0.73 us (1%)
  between operations  0.73 us (1%)
    all_to_all x1, blocking collectives, on_device(): parts = lax.all_to_all(send, GRID_AXES, 0, 0, tiled=True)  10.2 us
    pallas_call x1, Pallas kernels, on_device(): kernel_call(functools.partial(basis_body, peers, len(sides) // 2), (shape...  9.13 us
    all_to_all x1, starting transfers between devices, on_device(): got = lax.all_to_all(payload, PEER_AXES, 0, 0, tiled=True)  7.4 us
    all_to_all x1, waiting for transfers between devices, on_device(): got = lax.all_to_all(payload, PEER_AXES, 0, 0, tiled=True)  6.75 us
    pallas_call x1, Pallas kernels, on_device(): kernel_call(functools.partial(source_body, capacity // LANES), (shape(nz,...  5.19 us
    pallas_call x1, Pallas kernels, on_device(): kernel_call(functools.partial(route_body, peers, capacity), shape(peers,...  4.22 us
    ppermute x1, waiting for transfers between devices, on_device(): high = lax.ppermute(down, 'cols', backward)  4.21 us
    pallas_call x1, Pallas kernels, on_device(): kernel_call(functools.partial(solve_body, devices // peers), (shape(nz, n...  4.11 us
  transfers between devices with their start and end apart: 11, of which 5 were waited for; matrix products, arithmetic and copies ran while one was open for 0% of the time, Pallas kernels for 2%

profile of v3, /device:TPU:0, one launch (start us, length us, event | category | flops | bytes accessed | tf_op | source)
XLA Modules:
  0.0 64.5 jit_solution(6607142877465280560)
XLA Ops:
  0.6 4.2 %shard_map.95 = f32[8,48,128]{2,1,0:T(8,128)} custom-call(s32[32,128]{1,0:T(8,128)} %bitcast.9, s32[32,128]{1,0:T(8,128)} %bitcast.10, f32[32,128]{1,0:T(8,128)} %bitcast.11, f32[32,128]{1,0:T(8,128)} %bitcast.12), custom_call_target="tpu_custom_call" | custom-call | bytes 15000000 | tf_op jit(solution)/shard_map/pallas_call | solution.py:619
  4.9 0.0 copy-start
  4.9 0.0 copy-start.1
  4.9 0.0 copy-start.2
  4.9 7.4 %all-to-all-start = ((f32[8,48,128]{2,1,0:T(8,128)}), f32[8,48,128]{2,1,0:T(8,128)S(1)}, u32[]{:S(2)}, u32[]{:S(2)}) async-start(f32[8,48,128]{2,1,0:T(8,128)} %shard_map.95), calls=%async_computation | async-start | bytes 393216 | tf_op jit(solution)/shard_map/all_to_all | solution.py:629
  12.3 0.0 copy-start.3
  12.3 0.7 %copy-done.3 = s32[32,128]{1,0:T(8,128)S(1)} copy-done((s32[32,128]{1,0:T(8,128)S(1)}, s32[32,128]{1,0:T(8,128)}, u32[]{:S(2)}) %copy-start.3) | copy-done | bytes 16408
  13.0 0.5 shard_map.96
  13.5 6.7 %all-to-all-done.got_ref = f32[8,48,128]{2,1,0:T(8,128)S(1)} async-done(((f32[8,48,128]{2,1,0:T(8,128)}), f32[8,48,128]{2,1,0:T(8,128)S(1)}, u32[]{:S(2)}, u32[]{:S(2)}) %all-to-all-start) | async-done | bytes 196640 | tf_op jit(solution)/shard_map/all_to_all | solution.py:629
  20.2 0.0 copy-done
  20.3 0.0 copy-done.1
  20.3 0.0 copy-done.2
  20.3 5.2 %shard_map.97 = (f32[8,32,128]{2,1,0:T(8,128)S(1)}, f32[4,8,8,128]{3,2,1,0:T(8,128)S(1)}, f32[4,8,8,128]{3,2,1,0:T(8,128)S(1)}) custom-call(f32[8,48,128]{2,1,0:T(8,128)S(1)} %all-to-all-done.got_ref, f32[8,32,128]{2,1,0:T(8,128)S(1)} %copy-done, f32[8,32,128]{2,1,0:T(8,128)S(1)} %copy-done.1, f32[8,32,128]{2,1,0:T(8,128)S(1)} %copy-done.2), custom_call_target="tpu_custom_call" | custom-call | bytes 18000000 | tf_op jit(solution)/shard_map/pallas_call | solution.py:638
  25.5 2.2 %collective-permute-start.4 = (f32[4,8,8,128]{3,2,1,0:T(8,128)S(1)}, f32[4,8,8,128]{3,2,1,0:T(8,128)S(1)}, u32[]{:S(2)}, u32[]{:S(2)}) collective-permute-start(f32[4,8,8,128]{3,2,1,0:T(8,128)S(1)} %get-tuple-element.26), channel_id=1, source_target_pairs={{0,4},{4,8},{8,12},{1,5},{5,9},{9,13},{2,6},{6,10},{10,14},{3,7},{... | collective-permute-start | bytes 393224 | tf_op jit(solution)/shard_map/ppermute | solution.py:644
  27.7 1.5 %collective-permute-start.5 = (f32[4,8,8,128]{3,2,1,0:T(8,128)S(1)}, f32[4,8,8,128]{3,2,1,0:T(8,128)S(1)}, u32[]{:S(2)}, u32[]{:S(2)}) collective-permute-start(f32[4,8,8,128]{3,2,1,0:T(8,128)S(1)} %get-tuple-element.27), channel_id=1, source_target_pairs={{4,0},{8,4},{12,8},{5,1},{9,5},{13,9},{6,2},{10,6},{14,10},{7,3},{... | collective-permute-start | bytes 393224 | tf_op jit(solution)/shard_map/ppermute | solution.py:645
  29.1 0.1 collective-permute-start
  29.2 0.5 collective-permute-start.1
  29.7 0.1 pad_add_fusion.where_ref
  29.8 0.1 collective-permute-start.2
  29.9 0.3 collective-permute-done.4.refs_4_.refs_8_
  30.2 0.2 collective-permute-start.3
  30.3 4.2 %collective-permute-done.5.refs_5_.refs_9_ = f32[4,8,8,128]{3,2,1,0:T(8,128)S(1)} collective-permute-done((f32[4,8,8,128]{3,2,1,0:T(8,128)S(1)}, f32[4,8,8,128]{3,2,1,0:T(8,128)S(1)}, u32[]{:S(2)}, u32[]{:S(2)}) %collective-permute-start.5) | collective-permute-done | bytes 131104 | tf_op jit(solution)/shard_map/ppermute | solution.py:645
  34.5 0.9 %shard_map.98 = f32[16,8,128]{2,1,0:T(8,128)S(1)} custom-call(s32[4]{0:T(128)S(1)} %pad_add_fusion.where_ref, f32[8,32,128]{2,1,0:T(8,128)S(1)} %copy-done, f32[8,32,128]{2,1,0:T(8,128)S(1)} %copy-done.1, f32[8,32,128]{2,1,0:T(8,128)S(1)} %copy-done.2, f32[8,32,128]{2,1,0:T(8,128)S(1)} %get-tuple-element.25.refs_3_, ...), custom_call_target="tpu_custom_call" | custom-call | bytes 3000000 | tf_op jit(solution)/shard_map/pallas_call | solution.py:651
  35.4 1.2 %collective-permute-start.8 = (f32[16,8,128]{2,1,0:T(8,128)S(1)}, f32[16,8,128]{2,1,0:T(8,128)S(1)}, u32[]{:S(2)}, u32[]{:S(2)}) collective-permute-start(f32[16,8,128]{2,1,0:T(8,128)S(1)} %shard_map.98), channel_id=1, source_target_pairs={{0,2},{2,0},{1,3},{3,1},{4,6},{6,4},{5,7},{7,5},{8,10},{10,8},{9,1... | collective-permute-start | bytes 196616 | tf_op jit(solution)/shard_map/ppermute | solution.py:656
  36.6 0.0 collective-permute-done.refs_4_
  36.6 0.0 collective-permute-start.6
  36.6 0.0 collective-permute-done.1.refs_5_
  36.6 0.5 collective-permute-start.7
  37.1 2.6 %collective-permute-done.8.refs_12_ = f32[16,8,128]{2,1,0:T(8,128)S(1)} collective-permute-done((f32[16,8,128]{2,1,0:T(8,128)S(1)}, f32[16,8,128]{2,1,0:T(8,128)S(1)}, u32[]{:S(2)}, u32[]{:S(2)}) %collective-permute-start.8) | collective-permute-done | bytes 65568 | tf_op jit(solution)/shard_map/ppermute | solution.py:656
  39.7 0.0 collective-permute-start.9
  39.8 0.0 collective-permute-done.2.refs_6_
  39.8 0.0 collective-permute-done.3.refs_7_
  39.8 1.2 %collective-permute-done.9.refs_13_ = f32[16,8,128]{2,1,0:T(8,128)S(1)} collective-permute-done((f32[16,8,128]{2,1,0:T(8,128)S(1)}, f32[16,8,128]{2,1,0:T(8,128)S(1)}, u32[]{:S(2)}, u32[]{:S(2)}) %collective-permute-start.9) | collective-permute-done | bytes 65568 | tf_op jit(solution)/shard_map/ppermute | solution.py:586
  41.0 0.0 collective-permute-done.6.refs_10_
  41.0 0.0 collective-permute-done.7.refs_11_
  41.0 9.1 %shard_map.99 = (f32[8,8,32,128]{3,2,1,0:T(8,128)S(1)}, f32[16,8,128]{2,1,0:T(8,128)S(1)}) custom-call(s32[4]{0:T(128)S(1)} %pad_add_fusion.where_ref, f32[8,32,128]{2,1,0:T(8,128)S(1)} %copy-done, f32[8,32,128]{2,1,0:T(8,128)S(1)} %copy-done.1, f32[8,32,128]{2,1,0:T(8,128)S(1)} %copy-done.2, f32[8,32,128]{2,1,0:T(8,128)S(1)} %get-tuple-element.25.refs_3_, ...), custom_call_target="tpu_custom_call" | custom-call | bytes 30000000 | tf_op jit(solution)/shard_map/pallas_call | solution.py:669
  50.1 10.2 %all_to_all.10.got_ref = f32[16,8,128]{2,1,0:T(8,128)S(1)} all-to-all(f32[16,8,128]{2,1,0:T(8,128)S(1)} %get-tuple-element.30), channel_id=1, replica_groups=mesh['groups'=2,'cols'=4,'rows'=2,'layers'=2] {'cols','rows','layers'}, dimensions={0} | all-to-all | bytes 131072 | tf_op jit(solution)/shard_map/all_to_all | solution.py:681
  60.4 4.1 %shard_map.100 = (f32[8,32,128]{2,1,0:T(8,128)}, f32[4,128]{1,0:T(4,128)}) custom-call(s32[4]{0:T(128)S(1)} %pad_add_fusion.where_ref, f32[16,8,128]{2,1,0:T(8,128)S(1)} %all_to_all.10.got_ref, f32[8,8,32,128]{3,2,1,0:T(8,128)S(1)} %get-tuple-element.31.own_ref), custom_call_target="tpu_custom_call" | custom-call | bytes 3000000 | tf_op jit(solution)/shard_map/pallas_call | solution.py:682
Async XLA Ops:
  4.9 15.4 %copy-start = (f32[8,32,128]{2,1,0:T(8,128)S(1)}, f32[8,32,128]{2,1,0:T(8,128)}, u32[]{:S(2)}) copy-start(f32[8,32,128]{2,1,0:T(8,128)} %refs_0_.1) | copy-start | bytes 393220
  4.9 15.4 %copy-start.1 = (f32[8,32,128]{2,1,0:T(8,128)S(1)}, f32[8,32,128]{2,1,0:T(8,128)}, u32[]{:S(2)}) copy-start(f32[8,32,128]{2,1,0:T(8,128)} %refs_1_.1) | copy-start | bytes 393220
  4.9 15.4 %copy-start.2 = (f32[8,32,128]{2,1,0:T(8,128)S(1)}, f32[8,32,128]{2,1,0:T(8,128)}, u32[]{:S(2)}) copy-start(f32[8,32,128]{2,1,0:T(8,128)} %refs_2_.1) | copy-start | bytes 393220
  4.9 15.4 %all-to-all-start = ((f32[8,48,128]{2,1,0:T(8,128)}), f32[8,48,128]{2,1,0:T(8,128)S(1)}, u32[]{:S(2)}, u32[]{:S(2)}) async-start(f32[8,48,128]{2,1,0:T(8,128)} %shard_map.95), calls=%async_computation | async-start | bytes 393216 | tf_op jit(solution)/shard_map/all_to_all | solution.py:629
  12.3 0.7 %copy-start.3 = (s32[32,128]{1,0:T(8,128)S(1)}, s32[32,128]{1,0:T(8,128)}, u32[]{:S(2)}) copy-start(s32[32,128]{1,0:T(8,128)} %pilot_ref) | copy-start | bytes 49156
  25.5 4.7 %collective-permute-start.4 = (f32[4,8,8,128]{3,2,1,0:T(8,128)S(1)}, f32[4,8,8,128]{3,2,1,0:T(8,128)S(1)}, u32[]{:S(2)}, u32[]{:S(2)}) collective-permute-start(f32[4,8,8,128]{3,2,1,0:T(8,128)S(1)} %get-tuple-element.26), channel_id=1, source_target_pairs={{0,4},{4,8},{8,12},{1,5},{5,9},{9,13},{2,6},{6,10},{10,14},{3,7},{... | collective-permute-start | bytes 393224 | tf_op jit(solution)/shard_map/ppermute | solution.py:644
  27.7 6.9 %collective-permute-start.5 = (f32[4,8,8,128]{3,2,1,0:T(8,128)S(1)}, f32[4,8,8,128]{3,2,1,0:T(8,128)S(1)}, u32[]{:S(2)}, u32[]{:S(2)}) collective-permute-start(f32[4,8,8,128]{3,2,1,0:T(8,128)S(1)} %get-tuple-element.27), channel_id=1, source_target_pairs={{4,0},{8,4},{12,8},{5,1},{9,5},{13,9},{6,2},{10,6},{14,10},{7,3},{... | collective-permute-start | bytes 393224 | tf_op jit(solution)/shard_map/ppermute | solution.py:645
  29.1 7.4 %collective-permute-start = (f32[8,32,128]{2,1,0:T(8,128)S(1)}, f32[8,32,128]{2,1,0:T(8,128)S(1)}, u32[]{:S(2)}, u32[]{:S(2)}) collective-permute-start(f32[8,32,128]{2,1,0:T(8,128)S(1)} %copy-done), channel_id=1, source_target_pairs={{0,1},{1,0},{2,3},{3,2},{4,5},{5,4},{6,7},{7,6},{8,9},{9,8},{10,11... | collective-permute-start | bytes 393224 | tf_op jit(solution)/shard_map/ppermute | solution.py:586
  29.2 7.4 %collective-permute-start.1 = (f32[8,32,128]{2,1,0:T(8,128)S(1)}, f32[8,32,128]{2,1,0:T(8,128)S(1)}, u32[]{:S(2)}, u32[]{:S(2)}) collective-permute-start(f32[8,32,128]{2,1,0:T(8,128)S(1)} %copy-done.1), channel_id=1, source_target_pairs={{0,1},{1,0},{2,3},{3,2},{4,5},{5,4},{6,7},{7,6},{8,9},{9,8},{10,11... | collective-permute-start | bytes 393224 | tf_op jit(solution)/shard_map/ppermute | solution.py:586
  29.8 10.0 %collective-permute-start.2 = (f32[8,32,128]{2,1,0:T(8,128)S(1)}, f32[8,32,128]{2,1,0:T(8,128)S(1)}, u32[]{:S(2)}, u32[]{:S(2)}) collective-permute-start(f32[8,32,128]{2,1,0:T(8,128)S(1)} %copy-done.2), channel_id=1, source_target_pairs={{0,1},{1,0},{2,3},{3,2},{4,5},{5,4},{6,7},{7,6},{8,9},{9,8},{10,11... | collective-permute-start | bytes 393224 | tf_op jit(solution)/shard_map/ppermute | solution.py:586
  30.2 9.6 %collective-permute-start.3 = (f32[8,32,128]{2,1,0:T(8,128)S(1)}, f32[8,32,128]{2,1,0:T(8,128)S(1)}, u32[]{:S(2)}, u32[]{:S(2)}) collective-permute-start(f32[8,32,128]{2,1,0:T(8,128)S(1)} %get-tuple-element.25.refs_3_), channel_id=1, source_target_pairs={{0,1},{1,0},{2,3},{3,2},{4,5},{5,4},{6,7},{7,6},{8,9},{9,8},{10,11... | collective-permute-start | bytes 393224 | tf_op jit(solution)/shard_map/ppermute | solution.py:586
  35.4 4.3 %collective-permute-start.8 = (f32[16,8,128]{2,1,0:T(8,128)S(1)}, f32[16,8,128]{2,1,0:T(8,128)S(1)}, u32[]{:S(2)}, u32[]{:S(2)}) collective-permute-start(f32[16,8,128]{2,1,0:T(8,128)S(1)} %shard_map.98), channel_id=1, source_target_pairs={{0,2},{2,0},{1,3},{3,1},{4,6},{6,4},{5,7},{7,5},{8,10},{10,8},{9,1... | collective-permute-start | bytes 196616 | tf_op jit(solution)/shard_map/ppermute | solution.py:656
  36.6 4.4 %collective-permute-start.6 = (f32[4,8,8,128]{3,2,1,0:T(8,128)S(1)}, f32[4,8,8,128]{3,2,1,0:T(8,128)S(1)}, u32[]{:S(2)}, u32[]{:S(2)}) collective-permute-start(f32[4,8,8,128]{3,2,1,0:T(8,128)S(1)} %collective-permute-done.4.refs_4_.refs_8_), channel_id=1, source_target_pairs={{0,1},{1,0},{2,3},{3,2},{4,5},{5,4},{6,7},{7,6},{8,9},{9,8},{10,11... | collective-permute-start | bytes 393224 | tf_op jit(solution)/shard_map/ppermute | solution.py:586
  36.6 4.4 %collective-permute-start.7 = (f32[4,8,8,128]{3,2,1,0:T(8,128)S(1)}, f32[4,8,8,128]{3,2,1,0:T(8,128)S(1)}, u32[]{:S(2)}, u32[]{:S(2)}) collective-permute-start(f32[4,8,8,128]{3,2,1,0:T(8,128)S(1)} %collective-permute-done.5.refs_5_.refs_9_), channel_id=1, source_target_pairs={{0,1},{1,0},{2,3},{3,2},{4,5},{5,4},{6,7},{7,6},{8,9},{9,8},{10,11... | collective-permute-start | bytes 393224 | tf_op jit(solution)/shard_map/ppermute | solution.py:586
  39.7 1.3 %collective-permute-start.9 = (f32[16,8,128]{2,1,0:T(8,128)S(1)}, f32[16,8,128]{2,1,0:T(8,128)S(1)}, u32[]{:S(2)}, u32[]{:S(2)}) collective-permute-start(f32[16,8,128]{2,1,0:T(8,128)S(1)} %collective-permute-done.8.refs_12_), channel_id=1, source_target_pairs={{0,1},{1,0},{2,3},{3,2},{4,5},{5,4},{6,7},{7,6},{8,9},{9,8},{10,11... | collective-permute-start | bytes 196616 | tf_op jit(solution)/shard_map/ppermute | solution.py:586

commit v4 on v3

--- a/solution.py
+++ b/solution.py
@@ -17,7 +17,7 @@
 PEER_AXES = ("cols", "rows")
 NT = (((1,), (1,)), ((), ()))
 EXACT = lax.Precision.HIGHEST
-VMEM_BYTES = 50 * 1024 * 1024
+VMEM_BYTES = 24 * 1024 * 1024
 
 
 def kernel_call(body, out_shape, scratch=(), weight=1, vmem=VMEM_BYTES):
@@ -269,72 +269,54 @@
     out_ref[...] = jnp.transpose(tall).reshape(out_ref.shape)
 
 
-def unpack(layer, f, own, other, edges, beside, padded):
+def joined(a, b):
+    return jnp.where((a > 0.0) & (b > 0.0), 0.5 * (a + b), 0.0)
+
+
+def right(x):
+    return pltpu.roll(x, x.shape[1] - 1, 1)
+
+
+def left(x):
+    return pltpu.roll(x, 1, 1)
+
+
+def fore(x):
+    return pltpu.roll(x, x.shape[0] - 1, 0)
+
+
+def back(x):
+    return pltpu.roll(x, 1, 0)
+
+
+def unpack(layer, f, own, other, edges, padded, top=0):
     nz, nx = own.shape[0], own.shape[1]
-    tall = nx + 2 * HALO
-    at = lane_iota(tall)
-    rows = slice((f % 2) * tall, (f % 2 + 1) * tall)
     for half, block in ((0, own), (1, other)):
         low, high = edges[2 * half], edges[2 * half + 1]
         for i in range(nz):
             j = jnp.where(layer == 0, i, nz - 1 - i)
             to = half * nz + i
-            padded[to, HALO : HALO + nx, :LANES] = block[j]
-            padded[to, :HALO, :LANES] = low[f, j]
-            padded[to, HALO + nx :, :LANES] = high[f, j]
-            strip = jnp.zeros((tall, LANES), jnp.float32)
-            for tiles, first in beside[half]:
-                shift = (2 * LANES + first - (f // 2 * nz + j) * HALO) & (LANES - 1)
-                strip = jnp.where(
-                    (at >= first) & (at < first + HALO), pltpu.roll(tiles[rows], shift, 1), strip
-                )
-            padded[to, :, LANES:] = strip
-
-
-def basis_body(peers, side_count, where_ref, *refs):
-    own, other = refs[:4], refs[4:8]
-    edges = refs[8:12]
-    sides = (refs[12 : 12 + side_count], refs[12 + side_count : 12 + 2 * side_count])
-    refs = refs[12 + 2 * side_count :]
-    spot_ref, slots_ref, own_ref, send_ref = refs[:4]
-    c_pad, s_pad, h_pad, diag, wx, wy, wz, image, basis, grads = refs[4:]
-    layer, row = where_ref[0], where_ref[1]
+            padded[to, top : top + HALO, :] = low[f, j]
+            padded[to, top + HALO : top + HALO + nx, :] = block[j]
+            padded[to, top + HALO + nx : top + 2 * HALO + nx, :] = high[f, j]
+
+
+def prepare_body(where_ref, *refs):
+    own, other, edges = refs[:3], refs[3:6], refs[6:10]
+    c_pad, diag, wx, wx_back, wy, wz, grads, outer, s_pad, h_pad = refs[10:]
+    layer = where_ref[0]
     nz, nx = own[0].shape[0], own[0].shape[1]
     planes, width = c_pad.shape[0], c_pad.shape[1]
-    high_side, low_side = 0, LANES - HALO
-    if side_count == 1:
-        firsts = [jnp.where(row == 0, high_side, low_side)]
-    else:
-        firsts = [low_side, high_side]
-    beside = [
-        [
-            (jnp.transpose(side[...].reshape(LANES, LANES)), first)
-            for side, first in zip(half, firsts)
-        ]
-        for half in sides
-    ]
-    for f, target in enumerate((c_pad, s_pad, h_pad, basis.at[0])):
-        unpack(layer, f, own[f], other[f], edges, beside, target)
-    def right(x):
-        return pltpu.roll(x, x.shape[1] - 1, 1)
-
-    def left(x):
-        return pltpu.roll(x, 1, 1)
-
-    def fore(x):
-        return pltpu.roll(x, x.shape[0] - 1, 0)
-
-    def back(x):
-        return pltpu.roll(x, 1, 0)
-
-    def joined(a, b):
-        return jnp.where((a > 0.0) & (b > 0.0), 0.5 * (a + b), 0.0)
-
+    for f, target in enumerate((c_pad, s_pad, h_pad)):
+        unpack(layer, f, own[f], other[f], edges, target)
+    lanes = lane_iota(width)
+    last = lanes == LANES - 1
     for z in range(planes):
         c = c_pad[z]
-        cf, cr = fore(c), right(c)
-        total = cf + back(c) + cr + left(c)
+        cf, cr = fore(c), jnp.where(last, 0.0, right(c))
+        total = cf + back(c) + cr + jnp.where(lanes == 0, 0.0, left(c))
         wx[z] = joined(c, cf)
+        wx_back[z] = joined(c, back(c))
         wy[z] = joined(c, cr)
         if z + 1 < planes:
             wz[z] = joined(c, c_pad[z + 1])
@@ -343,60 +325,198 @@
             total = total + c_pad[z - 1]
         diag[z] = s_pad[z] + 3.0 * c + 0.5 * total
 
-    alphas, gammas, norms = [], [], []
-
-    def member(k, z, rows=slice(None), lanes=slice(None)):
-        u = image[z, rows, lanes] - alphas[k - 1] * basis[k - 1, z, rows, lanes]
-        if k > 1:
-            u = u - gammas[k - 1] * basis[k - 2, z, rows, lanes]
-        basis[k, z, rows, lanes] = u
+    span = HALO + nx
+    rows, lanes = row_iota(width), lane_iota(width)
+    mine = (rows >= HALO) & (rows < span)
+    before = (rows >= HALO - 1) & (rows < span - 1)
+    odd = (lanes & 1) == 1
+    inside = mine & (lanes < LANES - 1)
+
+    def kept(mask, x):
+        return jnp.where(mask, x, 0.0)[:span]
+
+    for z in range(nz):
+        c, h = -0.5 * c_pad[z], h_pad[z]
+        fall = h - fore(h)
+        grads[0, z] = kept(mine, c * fall)
+        grads[1, z] = kept(before, fore(c) * fall)
+        fall = h - right(h)
+        following = right(c) * fall
+        grads[2, z] = kept(inside, c * fall + jnp.where(odd, 0.0, following))
+        grads[3, z] = kept(inside & odd, following)
+        weight = c + -0.5 * c_pad[z + 1] if z + 1 < nz else c
+        grads[4, z] = kept(mine, weight * (h - h_pad[z + 1]))
+        grads[5, z] = kept(mine & ((lanes == 0) | (lanes == LANES - 1)), c * h)
+    outer[...] = kept(mine, -0.5 * c_pad[0] * h_pad[0])
+
+
+def basis_body(peers, side_count, where_ref, *refs):
+    c_pad, diag_in, wx, wx_back, wy, wz, grads, outer = refs[:8]
+    b_own, b_other, edges, refs = refs[8], refs[9], refs[10:14], refs[14:]
+    sides = list(zip(refs[:side_count], refs[side_count : 2 * side_count]))
+    spot_ref, slots_ref, own_ref, send_ref = refs[2 * side_count : 2 * side_count + 4]
+    diag, ws, edge_grads, image, basis = refs[2 * side_count + 4 :]
+    layer, row = where_ref[0], where_ref[1]
+    nz, nx = b_own.shape[0], b_own.shape[1]
+    planes, width = c_pad.shape[0], c_pad.shape[1]
+    span = HALO + nx
+    inner = slice(HALO, span)
+    top = HALO
+    body = slice(top, top + width)
+    for k in range(ITERS):
+        for z in range(planes):
+            basis[k, z, :top, :] = jnp.zeros((top, LANES), jnp.float32)
+            basis[k, z, top + width :, :] = jnp.zeros((top, LANES), jnp.float32)
+    unpack(layer, 3, b_own, b_other, edges, basis.at[0], top)
+
+    lanes, rows = lane_iota(width), row_iota(width)
+    y_at = lanes & (HALO - 1)
+    if side_count == 1:
+        meetings = [(jnp.where(row == 0, LANES - 1, 0), jnp.where(row == 0, 0, HALO - 1))]
+    else:
+        meetings = [(0, HALO - 1), (LANES - 1, 0)]
+    strips = []
+    for (here, there), (edge, meet) in zip(sides, meetings):
+        halves = [jnp.transpose(x[...].reshape(LANES, LANES)) for x in (here, there)]
+        first = jnp.where(layer == 0, halves[0], halves[1])
+        second = jnp.where(layer == 0, halves[1], halves[0])
+        fields = []
+        for f in range(4):
+            part = slice((f % 2) * width, (f % 2 + 1) * width)
+            half = LANES // 2
+            fields.append(
+                jnp.where(
+                    lanes < half,
+                    pltpu.roll(first[part], half, 1) if f // 2 else first[part],
+                    second[part] if f // 2 else pltpu.roll(second[part], half, 1),
+                )
+            )
+        shifts = []
+        for z in range(planes):
+            spot = jnp.where(layer == 0, z, planes - 1 - z) * HALO + meet
+            shifts.append(
+                ((edge - spot) & (LANES - 1), (spot - edge) & (LANES - 1))
+            )
+        strips.append((fields, lanes == edge, shifts))
+
+    def from_strips(values, z):
+        total = jnp.zeros((width, LANES), jnp.float32)
+        for (_, at_edge, shifts), value in zip(strips, values):
+            total = jnp.where(at_edge, pltpu.roll(value, shifts[z][0], 1), total)
+        return total
+
+    def to_strip(strip, value, z):
+        _, at_edge, shifts = strip
+        if side_count > 1:
+            value = jnp.where(at_edge, value, 0.0)
+        return pltpu.roll(value, shifts[z][1], 1)
+
+    edge_c = [jnp.zeros((width, LANES), jnp.float32) for _ in strips]
+    mine = (rows >= HALO) & (rows < span)
+    for z in range(planes):
+        c = c_pad[z]
+        c_side = from_strips([s[0][0] for s in strips], z)
+        ws[z] = joined(c, c_side)
+        diag[z] = diag_in[z] + 0.5 * c_side
+        for i, strip in enumerate(strips):
+            edge_c[i] = edge_c[i] + to_strip(strip, jnp.where(strip[1], c, 0.0), z)
+        if z < nz:
+            h_side = from_strips([s[0][2] for s in strips], z)
+            edge_grads[z] = grads[5, z] + jnp.where(mine, 0.5 * c * h_side, 0.0)[:span]
+    strip_terms = []
+    for (fields, _, _), beside in zip(strips, edge_c):
+        c = fields[0]
+        cf = fore(c)
+        cr = jnp.where(y_at < HALO - 1, right(c), 0.0)
+        cu = jnp.where(lanes < LANES - HALO, pltpu.roll(c, LANES - HALO, 1), 0.0)
+        total = cf + back(c) + cr + cu + beside
+        total = total + jnp.where(y_at > 0, left(c), 0.0)
+        total = total + jnp.where(lanes >= HALO, pltpu.roll(c, HALO, 1), 0.0)
+        strip_terms.append(
+            (fields[1] + 3.0 * c + 0.5 * total, joined(c, cf), joined(c, cr), joined(c, cu))
+        )
+
+    alphas, gammas, norms, sums = [], [], [], []
+
+    def following(k, image_now, now, before):
+        u = image_now - alphas[k - 1] * now
+        return u - gammas[k - 1] * before if k > 1 else u
+
+    def member(k, z):
+        before = basis[k - 2, z, body, :] if k > 1 else None
+        u = following(k, image[z], basis[k - 1, z, body, :], before)
+        basis[k, z, body, :] = u
+        return u
 
     def folded(x):
-        x = x[:, :LANES] + x[:, LANES:]
         return sum(x[r : r + 8] for r in range(8, width, 8)) + x[:8]
 
+    side_now = [s[0][3] for s in strips]
+    side_last, side_image = None, None
     for k in range(ITERS):
+        above = member(k, 0) if k else basis[0, 0, body, :]
+        v = None
         if k:
-            member(k, 0)
+            side_next = [
+                following(k, side_image[i], side_now[i], side_last[i] if k > 1 else None)
+                for i in range(side_count)
+            ]
+            side_now, side_last = side_next, side_now
         norm = jnp.zeros((8, LANES), jnp.float32)
         energy = jnp.zeros((8, LANES), jnp.float32)
+        side_image = []
+        for x, (d, sx, sy, sz) in zip(side_now, strip_terms):
+            ax = d * x - sx * fore(x) - back(sx * x) - sy * right(x) - left(sy * x)
+            ax = ax - sz * pltpu.roll(x, LANES - HALO, 1) - pltpu.roll(sz * x, HALO, 1)
+            side_image.append(ax)
+        acc = basis[k, 0, top : top + span, :] * outer[...]
+        acc_x = jnp.zeros((span, LANES), jnp.float32)
+        acc_y = jnp.zeros((span, LANES), jnp.float32)
         for z in range(nz + ITERS - 1 - k):
-            if k:
-                member(k, z + 1)
-            v = basis[k, z]
-            wxz, wyz = wx[z], wy[z]
-            av = diag[z] * v - wz[z] * basis[k, z + 1]
+            below, v = v, above
+            above = member(k, z + 1) if k else basis[0, z + 1, body, :]
+            side = from_strips(side_now, z)
+            vf, vr = basis[k, z, top + 1 : top + 1 + width, :], right(v)
+            vb = basis[k, z, top - 1 : top - 1 + width, :]
+            wyz, wsz = wy[z], ws[z]
+            av = diag[z] * v - wz[z] * above
             if z:
-                av = av - wz[z - 1] * basis[k, z - 1]
-            av = av - wxz * fore(v) - back(wxz * v) - wyz * right(v) - left(wyz * v)
+                av = av - wz[z - 1] * below
+            av = av - wx[z] * vf - wx_back[z] * vb - wyz * vr - left(wyz * v) - wsz * side
             image[z] = av
+            edge = wsz * v
+            for i, strip in enumerate(strips):
+                side_image[i] = side_image[i] - to_strip(strip, edge, z)
             norm = norm + folded(v * v)
             energy = energy + folded(v * av)
+            if z < nz:
+                fall = (v - vf)[:span]
+                acc = acc + fall * grads[0, z]
+                acc_x = acc_x + fall * grads[1, z]
+                fall = (v - vr)[:span]
+                acc = acc + fall * grads[2, z]
+                acc_y = acc_y + fall * grads[3, z]
+                acc = acc + (v - above)[:span] * grads[4, z]
+                acc = acc + (v - side)[:span] * edge_grads[z]
+                own_ref[k, jnp.where(layer == 0, z, nz - 1 - z)] = v[inner]
+        for x, ax in zip(side_now, side_image):
+            norm = norm + folded(x * x)
+            energy = energy + folded(x * ax)
+        sums.append((acc + back(acc_x) + left(acc_y))[inner])
         norm = all_sum(norm)
         alphas.append(safe_ratio(all_sum(energy), norm))
         gammas.append(safe_ratio(norm, norms[-1]) if k else jnp.zeros_like(norm))
         norms.append(norm)
-    inner = slice(HALO, HALO + nx)
     for z in range(nz):
-        member(ITERS, z, inner, slice(LANES))
-
-    for z in range(nz):
-        c = -0.5 * c_pad[z, inner, :LANES]
-        h = h_pad[z, inner, :LANES]
-        wide = h_pad[z, inner, :]
-        grads[0, z] = c * (h - h_pad[z, HALO + 1 : HALO + nx + 1, :LANES])
-        grads[1, z] = c * (h - h_pad[z, HALO - 1 : HALO + nx - 1, :LANES])
-        grads[2, z] = c * (h - right(wide)[:, :LANES])
-        grads[3, z] = c * (h - left(wide)[:, :LANES])
-        grads[4, z] = c * (h - h_pad[z + 1, inner, :LANES])
-        grads[5, z] = c * (h - h_pad[z - 1, inner, :LANES]) if z else c * h
+        member(ITERS, z)
+    own_rows = slice(top + HALO, top + span)
 
     dots = {}
     for i in range(ITERS + 1):
         for j in range(i + 1):
-            acc = basis[i, 0, inner, :LANES] * basis[j, 0, inner, :LANES]
+            acc = basis[i, 0, own_rows, :] * basis[j, 0, own_rows, :]
             for z in range(1, nz):
-                acc = acc + basis[i, z, inner, :LANES] * basis[j, z, inner, :LANES]
+                acc = acc + basis[i, z, own_rows, :] * basis[j, z, own_rows, :]
             dots[i, j] = dots[j, i] = all_sum(acc)
 
     def operator(i, j):
@@ -413,23 +533,6 @@
             entries = jnp.where(lanes == FACTS + place, entry, entries)
         facts.append(entries)
 
-    sums = []
-    for k in range(ITERS):
-        acc = jnp.zeros((nx, LANES), jnp.float32)
-        for z in range(nz):
-            u = basis[k, z, inner, :LANES]
-            wide = basis[k, z, inner, :]
-            acc = acc + (u - basis[k, z, HALO + 1 : HALO + nx + 1, :LANES]) * grads[0, z]
-            acc = acc + (u - basis[k, z, HALO - 1 : HALO + nx - 1, :LANES]) * grads[1, z]
-            acc = acc + (u - right(wide)[:, :LANES]) * grads[2, z]
-            acc = acc + (u - left(wide)[:, :LANES]) * grads[3, z]
-            acc = acc + (u - basis[k, z + 1, inner, :LANES]) * grads[4, z]
-            if z:
-                acc = acc + (u - basis[k, z - 1, inner, :LANES]) * grads[5, z]
-            else:
-                acc = acc + u * grads[5, z]
-            own_ref[k, jnp.where(layer == 0, z, nz - 1 - z)] = u
-        sums.append(acc)
     blocks_x = nx // 4
     four = jnp.where(
         lax.shift_right_logical(lane_iota(blocks_x, nx), 2) == row_iota(blocks_x, nx), 1.0, 0.0
@@ -500,33 +603,30 @@
         now, last, norm_last = following, now, norm
 
     lanes = lane_iota(ITERS)
-    ra, ca = row_iota(LANES), lane_iota(LANES)
-    same = lax.shift_right_logical(ra, 3) == lax.shift_right_logical(ca, 3)
-    spread = jnp.concatenate(
-        [jnp.where(same & ((ra & (ITERS - 1)) == m), 1.0, 0.0) for m in range(ITERS)], axis=1
-    )
     system = jnp.zeros((ITERS, LANES), jnp.float32)
     stacked = []
+    per = LANES // ITERS
     for g in range(groups):
         t = jnp.concatenate([c[g : g + 1] for c in common], axis=0)
         stacked.append(t)
-        wide = mm(t, spread, precision=EXACT)
-        image = jnp.zeros((ITERS, LANES), jnp.float32)
-        for m in range(ITERS):
-            image = image + turned[g][m : m + 1] * wide[:, m * LANES : (m + 1) * LANES]
-        right = jnp.concatenate(
+        blocks = []
+        for i in range(per):
+            block = pltpu.roll(got_ref[g * per + i], (ITERS * i - FACTS) % LANES, 1)
+            blocks.append(
+                jnp.where((lanes >= ITERS * i) & (lanes < ITERS * (i + 1)), block, 0.0)
+            )
+        image = mm(t, jnp.concatenate(blocks, axis=0), precision=EXACT)
+        beside = jnp.concatenate(
             [image, rhs[g : g + 1], jnp.zeros((LANES - ITERS - 1, LANES), jnp.float32)], axis=0
         )
-        system = system + mm(t, right, NT, precision=EXACT)
+        system = system + mm(t, beside, NT, precision=EXACT)
     rows = row_iota(ITERS)
     for p in range(ITERS):
-        pivot_row = system[p : p + 1]
-        pivot = jnp.sum(jnp.where(lanes == p, system, 0.0), axis=1, keepdims=True)
-        inverse = jnp.sum(jnp.where(rows[:, :1] == p, pivot, 0.0), axis=0, keepdims=True)
-        inverse = jnp.where(inverse > 0.0, 1.0 / jnp.where(inverse > 0.0, inverse, 1.0), 0.0)
-        pivot_row = pivot_row * inverse
-        system = jnp.where(rows == p, pivot_row, system - pivot * pivot_row)
-    answer = jnp.sum(jnp.where(lanes == ITERS, system, 0.0), axis=1, keepdims=True)
+        pivot = system[p : p + 1, p : p + 1]
+        inverse = jnp.where(pivot > 0.0, 1.0 / jnp.where(pivot > 0.0, pivot, 1.0), 0.0)
+        pivot_row = system[p : p + 1] * inverse
+        system = jnp.where(rows == p, pivot_row, system - system[:, p : p + 1] * pivot_row)
+    answer = system[:, ITERS : ITERS + 1]
 
     weights = [jnp.sum(answer * t, axis=0, keepdims=True) for t in stacked]
     me = where_ref[3]
@@ -632,8 +732,7 @@
     )(in_specs=[VMEM], out_specs=(VMEM, VMEM))(pilot_index)
 
     fixed = (conductivity, storage, state_field)
-    got, spot, *fixed = tied(got, spot, *fixed)
-    fixed_other = [swapped(x) for x in fixed]
+    got, spot, *fixed_other = tied(got, spot, *(swapped(x) for x in fixed))
     edge = shape(4, nz, HALO, LANES)
     source, up, down = kernel_call(
         functools.partial(source_body, capacity // LANES),
@@ -645,38 +744,43 @@
     high = lax.ppermute(down, "cols", backward)
     other = swapped(source)
 
-    mine = (*fixed, source)
-
     def packed(low_side):
         return kernel_call(
             functools.partial(pack_body, low_side), shape(2 * nz, HALO, LANES)
-        )(in_specs=[SMEM] + [VMEM] * 6, out_specs=VMEM)(where, *mine, low, high)
+        )(in_specs=[SMEM] + [VMEM] * 6, out_specs=VMEM)(where, *fixed, source, low, high)
 
     if row_count == 2:
-        sides = [lax.ppermute(packed(None), "rows", [(0, 1), (1, 0)])]
+        send = [(packed(None), [(0, 1), (1, 0)])]
     else:
         forward, backward = neighbour_pairs("rows")
-        sides = [
-            lax.ppermute(packed(False), "rows", forward),
-            lax.ppermute(packed(True), "rows", backward),
-        ]
-    edges = [low, high, swapped(low), swapped(high)]
+        send = [(packed(False), forward), (packed(True), backward)]
+    edges = tied(low, high, swapped(low), swapped(high), *(x for x, _ in send))[:4]
+    sides = [lax.ppermute(x, "rows", pairs) for x, pairs in send]
+    planes, width, span = 2 * nz, nx + 2 * HALO, nx + HALO
+    padded = (planes, width, LANES)
+    prepared = kernel_call(
+        prepare_body,
+        (*(shape(*padded) for _ in range(6)), shape(6, nz, span, LANES), shape(span, LANES)),
+        [pltpu.VMEM(padded, f32)] * 2,
+        weight=3,
+    )(in_specs=[SMEM] + [VMEM] * 10, out_specs=(VMEM,) * 8)(where, *fixed, *fixed_other, *edges)
+    *sides, prepared = tied(*sides, prepared)
     sides = sides + [swapped(x) for x in sides]
 
     each = nx * ny // 8 // LANES
-    planes, width = 2 * nz, nx + 2 * HALO
-    padded = pltpu.VMEM((planes, width, 2 * LANES), f32)
     own, send = kernel_call(
         functools.partial(basis_body, peers, len(sides) // 2),
         (shape(ITERS, nz, nx, LANES), shape(devices, ITERS, LANES)),
-        [padded] * 8
-        + [
-            pltpu.VMEM((ITERS + 1, planes, width, 2 * LANES), f32),
-            pltpu.VMEM((6, nz, nx, LANES), f32),
+        [
+            pltpu.VMEM(padded, f32),
+            pltpu.VMEM(padded, f32),
+            pltpu.VMEM((nz, span, LANES), f32),
+            pltpu.VMEM(padded, f32),
+            pltpu.VMEM((ITERS + 1, planes, width + 2 * HALO, LANES), f32),
         ],
         weight=10,
-    )(in_specs=[SMEM] + [VMEM] * (14 + len(sides)), out_specs=(VMEM, VMEM))(
-        where, *mine, *fixed_other, other, *edges, *sides, spot, slots
+    )(in_specs=[SMEM] + [VMEM] * (16 + len(sides)), out_specs=(VMEM, VMEM))(
+        where, *prepared, source, other, *edges, *sides, spot, slots
     )
     parts = lax.all_to_all(send, GRID_AXES, 0, 0, tiled=True)
     adjoint, pilot = kernel_call(

time: 65 us -> 63.1 us (0.971)
  Pallas kernels: 24 us -> 23 us
    pallas_call x1, Pallas kernels: 9.13 us -> 7.25 us  [on_device(): kernel_call(functools.partial(basis_body, peers, len(sides) // 2), (shape...]
    pallas_call x0 -> x1, Pallas kernels: none -> 1.16 us  [on_device(): kernel_call(prepare_body, (*(shape(*padded) for _ in range(6)), shape(6,...]
    all_to_all x1, waiting for transfers between devices: 6.75 us -> 6.02 us  [on_device(): got = lax.all_to_all(payload, PEER_AXES, 0, 0, tiled=True)]
    ppermute x1, waiting for transfers between devices: 0.28 us -> 1.01 us  [on_device(): low = lax.ppermute(up, 'cols', forward)]
  transfers between devices with their start and end apart: 11 -> 11, of which waited for: 5 -> 5; matrix products, arithmetic and copies ran while one was open for 0% -> 0% of each run, Pallas kernels for 2% -> 4%
where the time goes in v4:
time: 63.1 us; the launch traced here: 62.6 us
  Pallas kernels  23 us (36%)
  waiting for transfers between devices  14.7 us (23%)
  starting transfers between devices  13.1 us (21%)
  blocking collectives  10.2 us (16%)
  local copies, waits for them, and re-layouts  0.74 us (1%)
  between operations  0.74 us (1%)
    all_to_all x1, blocking collectives, on_device(): parts = lax.all_to_all(send, GRID_AXES, 0, 0, tiled=True)  10.2 us
    all_to_all x1, starting transfers between devices, on_device(): got = lax.all_to_all(payload, PEER_AXES, 0, 0, tiled=True)  7.4 us
    pallas_call x1, Pallas kernels, on_device(): kernel_call(functools.partial(basis_body, peers, len(sides) // 2), (shape...  7.25 us
    all_to_all x1, waiting for transfers between devices, on_device(): got = lax.all_to_all(payload, PEER_AXES, 0, 0, tiled=True)  6.02 us
    pallas_call x1, Pallas kernels, on_device(): kernel_call(functools.partial(source_body, capacity // LANES), (shape(nz,...  5.19 us
    ppermute x1, waiting for transfers between devices, on_device(): high = lax.ppermute(down, 'cols', backward)  4.36 us
    pallas_call x1, Pallas kernels, on_device(): kernel_call(functools.partial(route_body, peers, capacity), shape(peers,...  4.22 us
    pallas_call x1, Pallas kernels, on_device(): kernel_call(functools.partial(solve_body, devices // peers), (shape(nz, n...  3.84 us
  transfers between devices with their start and end apart: 11, of which 5 were waited for; matrix products, arithmetic and copies ran while one was open for 0% of the time, Pallas kernels for 4%

profile of v4, /device:TPU:0, one launch (start us, length us, event | category | flops | bytes accessed | tf_op | source)
XLA Modules:
  0.0 62.6 jit_solution(8847408890835268846)
XLA Ops:
  0.6 4.2 %shard_map.95 = f32[8,48,128]{2,1,0:T(8,128)} custom-call(s32[32,128]{1,0:T(8,128)} %bitcast.9, s32[32,128]{1,0:T(8,128)} %bitcast.10, f32[32,128]{1,0:T(8,128)} %bitcast.11, f32[32,128]{1,0:T(8,128)} %bitcast.12), custom_call_target="tpu_custom_call" | custom-call | bytes 15000000 | tf_op jit(solution)/shard_map/pallas_call | solution.py:719
  4.9 0.0 copy-start.2
  4.9 0.0 copy-start
  4.9 0.0 copy-start.1
  4.9 7.4 %all-to-all-start = ((f32[8,48,128]{2,1,0:T(8,128)}), f32[8,48,128]{2,1,0:T(8,128)S(1)}, u32[]{:S(2)}, u32[]{:S(2)}) async-start(f32[8,48,128]{2,1,0:T(8,128)} %shard_map.95), calls=%async_computation | async-start | bytes 393216 | tf_op jit(solution)/shard_map/all_to_all | solution.py:729
  12.3 0.0 copy-done.2
  12.3 0.1 collective-permute-start.2
  12.4 0.0 copy-done
  12.4 0.5 collective-permute-start
  12.9 0.0 copy-done.1
  12.9 0.1 collective-permute-start.1
  13.0 0.0 copy-start.3
  13.0 0.7 %copy-done.3 = s32[32,128]{1,0:T(8,128)S(1)} copy-done((s32[32,128]{1,0:T(8,128)S(1)}, s32[32,128]{1,0:T(8,128)}, u32[]{:S(2)}) %copy-start.3) | copy-done | bytes 16408
  13.7 0.5 shard_map.96
  14.2 0.0 collective-permute-done.2.refs_5_
  14.2 0.0 collective-permute-done.refs_3_
  14.2 0.0 collective-permute-done.1.refs_4_
  14.2 6.0 %all-to-all-done.got_ref = f32[8,48,128]{2,1,0:T(8,128)S(1)} async-done(((f32[8,48,128]{2,1,0:T(8,128)}), f32[8,48,128]{2,1,0:T(8,128)S(1)}, u32[]{:S(2)}, u32[]{:S(2)}) %all-to-all-start) | async-done | bytes 196640 | tf_op jit(solution)/shard_map/all_to_all | solution.py:729
  20.2 5.2 %shard_map.97 = (f32[8,32,128]{2,1,0:T(8,128)S(1)}, f32[4,8,8,128]{3,2,1,0:T(8,128)S(1)}, f32[4,8,8,128]{3,2,1,0:T(8,128)S(1)}) custom-call(f32[8,48,128]{2,1,0:T(8,128)S(1)} %all-to-all-done.got_ref, f32[8,32,128]{2,1,0:T(8,128)S(1)} %copy-done, f32[8,32,128]{2,1,0:T(8,128)S(1)} %copy-done.1, f32[8,32,128]{2,1,0:T(8,128)S(1)} %copy-done.2), custom_call_target="tpu_custom_call" | custom-call | bytes 18000000 | tf_op jit(solution)/shard_map/pallas_call | solution.py:737
  25.4 2.2 %collective-permute-start.3 = (f32[4,8,8,128]{3,2,1,0:T(8,128)S(1)}, f32[4,8,8,128]{3,2,1,0:T(8,128)S(1)}, u32[]{:S(2)}, u32[]{:S(2)}) collective-permute-start(f32[4,8,8,128]{3,2,1,0:T(8,128)S(1)} %get-tuple-element.44), channel_id=1, source_target_pairs={{0,4},{4,8},{8,12},{1,5},{5,9},{9,13},{2,6},{6,10},{10,14},{3,7},{... | collective-permute-start | bytes 393224 | tf_op jit(solution)/shard_map/ppermute | solution.py:743
  27.6 1.5 %collective-permute-start.4 = (f32[4,8,8,128]{3,2,1,0:T(8,128)S(1)}, f32[4,8,8,128]{3,2,1,0:T(8,128)S(1)}, u32[]{:S(2)}, u32[]{:S(2)}) collective-permute-start(f32[4,8,8,128]{3,2,1,0:T(8,128)S(1)} %get-tuple-element.45), channel_id=1, source_target_pairs={{4,0},{8,4},{12,8},{5,1},{9,5},{13,9},{6,2},{10,6},{14,10},{7,3},{... | collective-permute-start | bytes 393224 | tf_op jit(solution)/shard_map/ppermute | solution.py:744
  29.1 1.0 %collective-permute-done.3.refs_4_.refs_6_.refs_10_ = f32[4,8,8,128]{3,2,1,0:T(8,128)S(1)} collective-permute-done((f32[4,8,8,128]{3,2,1,0:T(8,128)S(1)}, f32[4,8,8,128]{3,2,1,0:T(8,128)S(1)}, u32[]{:S(2)}, u32[]{:S(2)}) %collective-permute-start.3) | collective-permute-done | bytes 131104 | tf_op jit(solution)/shard_map/ppermute | solution.py:743
  30.1 0.0 collective-permute-start.6
  30.1 4.4 %collective-permute-done.4.refs_5_.refs_7_.refs_11_ = f32[4,8,8,128]{3,2,1,0:T(8,128)S(1)} collective-permute-done((f32[4,8,8,128]{3,2,1,0:T(8,128)S(1)}, f32[4,8,8,128]{3,2,1,0:T(8,128)S(1)}, u32[]{:S(2)}, u32[]{:S(2)}) %collective-permute-start.4) | collective-permute-done | bytes 131104 | tf_op jit(solution)/shard_map/ppermute | solution.py:744
  34.5 0.0 collective-permute-start.7
  34.5 0.1 pad_add_fusion.where_ref
  34.6 0.9 %shard_map.98 = f32[16,8,128]{2,1,0:T(8,128)S(1)} custom-call(s32[4]{0:T(128)S(1)} %pad_add_fusion.where_ref, f32[8,32,128]{2,1,0:T(8,128)S(1)} %copy-done, f32[8,32,128]{2,1,0:T(8,128)S(1)} %copy-done.1, f32[8,32,128]{2,1,0:T(8,128)S(1)} %copy-done.2, f32[8,32,128]{2,1,0:T(8,128)S(1)} %get-tuple-element.43.refs_3_.refs_8_, ...), custom_call_target="tpu_custom_call" | custom-call | bytes 3000000 | tf_op jit(solution)/shard_map/pallas_call | solution.py:748
  35.5 1.2 %collective-permute-start.5 = (f32[16,8,128]{2,1,0:T(8,128)S(1)}, f32[16,8,128]{2,1,0:T(8,128)S(1)}, u32[]{:S(2)}, u32[]{:S(2)}) collective-permute-start(f32[16,8,128]{2,1,0:T(8,128)S(1)} %shard_map.98), channel_id=1, source_target_pairs={{0,2},{2,0},{1,3},{3,1},{4,6},{6,4},{5,7},{7,5},{8,10},{10,8},{9,1... | collective-permute-start | bytes 196616 | tf_op jit(solution)/shard_map/ppermute | solution.py:758
  36.7 0.2 collective-permute-start.8
  36.9 0.0 collective-permute-done.6.refs_8_.refs_12_
  36.9 0.0 collective-permute-done.7.refs_9_.refs_13_
  36.9 1.2 %shard_map.99 = (f32[16,48,128]{2,1,0:T(8,128)S(1)}, f32[16,48,128]{2,1,0:T(8,128)S(1)}, f32[16,48,128]{2,1,0:T(8,128)S(1)}, f32[16,48,128]{2,1,0:T(8,128)S(1)},...) custom-call(s32[4]{0:T(128)S(1)} %pad_add_fusion.where_ref, ...), custom_call_target="tpu_custom_call" | custom-call | bytes 9000000 | tf_op jit(solution)/shard_map/pallas_call | solution.py:761
  38.0 2.0 %collective-permute-done.5.refs_14_ = f32[16,8,128]{2,1,0:T(8,128)S(1)} collective-permute-done((f32[16,8,128]{2,1,0:T(8,128)S(1)}, f32[16,8,128]{2,1,0:T(8,128)S(1)}, u32[]{:S(2)}, u32[]{:S(2)}) %collective-permute-start.5) | collective-permute-done | bytes 65568 | tf_op jit(solution)/shard_map/ppermute | solution.py:758
  40.0 0.0 collective-permute-start.9
  40.1 0.0 collective-permute-done.8.refs_9_
  40.1 1.2 %collective-permute-done.9.refs_15_ = f32[16,8,128]{2,1,0:T(8,128)S(1)} collective-permute-done((f32[16,8,128]{2,1,0:T(8,128)S(1)}, f32[16,8,128]{2,1,0:T(8,128)S(1)}, u32[]{:S(2)}, u32[]{:S(2)}) %collective-permute-start.9) | collective-permute-done | bytes 65568 | tf_op jit(solution)/shard_map/ppermute | solution.py:686
  41.3 7.3 %shard_map.100 = (f32[8,8,32,128]{3,2,1,0:T(8,128)S(1)}, f32[16,8,128]{2,1,0:T(8,128)S(1)}) custom-call(s32[4]{0:T(128)S(1)} %pad_add_fusion.where_ref, f32[16,48,128]{2,1,0:T(8,128)S(1)} %get-tuple-element.61.refs_0_, f32[16,48,128]{2,1,0:T(8,128)S(1)} %get-tuple-element.62.refs_1_, f32[16,48,128]{2,1,0:T(8,128)S(1)} %get-tuple-element.63.refs_2_, ...), custom_call_target="tpu_custom_call" | custom-call | bytes 30000000 | tf_op jit(solution)/shard_map/pallas_call | solution.py:771
  48.6 10.2 %all_to_all.10.got_ref = f32[16,8,128]{2,1,0:T(8,128)S(1)} all-to-all(f32[16,8,128]{2,1,0:T(8,128)S(1)} %get-tuple-element.72), channel_id=1, replica_groups=mesh['groups'=2,'cols'=4,'rows'=2,'layers'=2] {'cols','rows','layers'}, dimensions={0} | all-to-all | bytes 131072 | tf_op jit(solution)/shard_map/all_to_all | solution.py:785
  58.8 3.8 %shard_map.101 = (f32[8,32,128]{2,1,0:T(8,128)}, f32[4,128]{1,0:T(4,128)}) custom-call(s32[4]{0:T(128)S(1)} %pad_add_fusion.where_ref, f32[16,8,128]{2,1,0:T(8,128)S(1)} %all_to_all.10.got_ref, f32[8,8,32,128]{3,2,1,0:T(8,128)S(1)} %get-tuple-element.73.own_ref), custom_call_target="tpu_custom_call" | custom-call | bytes 3000000 | tf_op jit(solution)/shard_map/pallas_call | solution.py:786
Async XLA Ops:
  4.9 7.4 %copy-start.2 = (f32[8,32,128]{2,1,0:T(8,128)S(1)}, f32[8,32,128]{2,1,0:T(8,128)}, u32[]{:S(2)}) copy-start(f32[8,32,128]{2,1,0:T(8,128)} %refs_2_.3) | copy-start | bytes 393220
  4.9 7.5 %copy-start = (f32[8,32,128]{2,1,0:T(8,128)S(1)}, f32[8,32,128]{2,1,0:T(8,128)}, u32[]{:S(2)}) copy-start(f32[8,32,128]{2,1,0:T(8,128)} %refs_0_.3) | copy-start | bytes 393220
  4.9 8.0 %copy-start.1 = (f32[8,32,128]{2,1,0:T(8,128)S(1)}, f32[8,32,128]{2,1,0:T(8,128)}, u32[]{:S(2)}) copy-start(f32[8,32,128]{2,1,0:T(8,128)} %refs_1_.3) | copy-start | bytes 393220
  4.9 15.4 %all-to-all-start = ((f32[8,48,128]{2,1,0:T(8,128)}), f32[8,48,128]{2,1,0:T(8,128)S(1)}, u32[]{:S(2)}, u32[]{:S(2)}) async-start(f32[8,48,128]{2,1,0:T(8,128)} %shard_map.95), calls=%async_computation | async-start | bytes 393216 | tf_op jit(solution)/shard_map/all_to_all | solution.py:729
  12.3 1.9 %collective-permute-start.2 = (f32[8,32,128]{2,1,0:T(8,128)S(1)}, f32[8,32,128]{2,1,0:T(8,128)S(1)}, u32[]{:S(2)}, u32[]{:S(2)}) collective-permute-start(f32[8,32,128]{2,1,0:T(8,128)S(1)} %copy-done.2), channel_id=1, source_target_pairs={{0,1},{1,0},{2,3},{3,2},{4,5},{5,4},{6,7},{7,6},{8,9},{9,8},{10,11... | collective-permute-start | bytes 393224 | tf_op jit(solution)/shard_map/ppermute | solution.py:686
  12.4 1.8 %collective-permute-start = (f32[8,32,128]{2,1,0:T(8,128)S(1)}, f32[8,32,128]{2,1,0:T(8,128)S(1)}, u32[]{:S(2)}, u32[]{:S(2)}) collective-permute-start(f32[8,32,128]{2,1,0:T(8,128)S(1)} %copy-done), channel_id=1, source_target_pairs={{0,1},{1,0},{2,3},{3,2},{4,5},{5,4},{6,7},{7,6},{8,9},{9,8},{10,11... | collective-permute-start | bytes 393224 | tf_op jit(solution)/shard_map/ppermute | solution.py:686
  12.9 1.3 %collective-permute-start.1 = (f32[8,32,128]{2,1,0:T(8,128)S(1)}, f32[8,32,128]{2,1,0:T(8,128)S(1)}, u32[]{:S(2)}, u32[]{:S(2)}) collective-permute-start(f32[8,32,128]{2,1,0:T(8,128)S(1)} %copy-done.1), channel_id=1, source_target_pairs={{0,1},{1,0},{2,3},{3,2},{4,5},{5,4},{6,7},{7,6},{8,9},{9,8},{10,11... | collective-permute-start | bytes 393224 | tf_op jit(solution)/shard_map/ppermute | solution.py:686
  13.0 0.7 %copy-start.3 = (s32[32,128]{1,0:T(8,128)S(1)}, s32[32,128]{1,0:T(8,128)}, u32[]{:S(2)}) copy-start(s32[32,128]{1,0:T(8,128)} %pilot_ref) | copy-start | bytes 49156
  25.4 4.7 %collective-permute-start.3 = (f32[4,8,8,128]{3,2,1,0:T(8,128)S(1)}, f32[4,8,8,128]{3,2,1,0:T(8,128)S(1)}, u32[]{:S(2)}, u32[]{:S(2)}) collective-permute-start(f32[4,8,8,128]{3,2,1,0:T(8,128)S(1)} %get-tuple-element.44), channel_id=1, source_target_pairs={{0,4},{4,8},{8,12},{1,5},{5,9},{9,13},{2,6},{6,10},{10,14},{3,7},{... | collective-permute-start | bytes 393224 | tf_op jit(solution)/shard_map/ppermute | solution.py:743
  27.6 6.9 %collective-permute-start.4 = (f32[4,8,8,128]{3,2,1,0:T(8,128)S(1)}, f32[4,8,8,128]{3,2,1,0:T(8,128)S(1)}, u32[]{:S(2)}, u32[]{:S(2)}) collective-permute-start(f32[4,8,8,128]{3,2,1,0:T(8,128)S(1)} %get-tuple-element.45), channel_id=1, source_target_pairs={{4,0},{8,4},{12,8},{5,1},{9,5},{13,9},{6,2},{10,6},{14,10},{7,3},{... | collective-permute-start | bytes 393224 | tf_op jit(solution)/shard_map/ppermute | solution.py:744
  30.1 6.7 %collective-permute-start.6 = (f32[4,8,8,128]{3,2,1,0:T(8,128)S(1)}, f32[4,8,8,128]{3,2,1,0:T(8,128)S(1)}, u32[]{:S(2)}, u32[]{:S(2)}) collective-permute-start(f32[4,8,8,128]{3,2,1,0:T(8,128)S(1)} %collective-permute-done.3.refs_4_.refs_6_.refs_10_), channel_id=1, source_target_pairs={{0,1},{1,0},{2,3},{3,2},{4,5},{5,4},{6,7},{7,6},{8,9},{9,8},{10,11... | collective-permute-start | bytes 393224 | tf_op jit(solution)/shard_map/ppermute | solution.py:686
  34.5 2.4 %collective-permute-start.7 = (f32[4,8,8,128]{3,2,1,0:T(8,128)S(1)}, f32[4,8,8,128]{3,2,1,0:T(8,128)S(1)}, u32[]{:S(2)}, u32[]{:S(2)}) collective-permute-start(f32[4,8,8,128]{3,2,1,0:T(8,128)S(1)} %collective-permute-done.4.refs_5_.refs_7_.refs_11_), channel_id=1, source_target_pairs={{0,1},{1,0},{2,3},{3,2},{4,5},{5,4},{6,7},{7,6},{8,9},{9,8},{10,11... | collective-permute-start | bytes 393224 | tf_op jit(solution)/shard_map/ppermute | solution.py:686
  35.5 4.6 %collective-permute-start.5 = (f32[16,8,128]{2,1,0:T(8,128)S(1)}, f32[16,8,128]{2,1,0:T(8,128)S(1)}, u32[]{:S(2)}, u32[]{:S(2)}) collective-permute-start(f32[16,8,128]{2,1,0:T(8,128)S(1)} %shard_map.98), channel_id=1, source_target_pairs={{0,2},{2,0},{1,3},{3,1},{4,6},{6,4},{5,7},{7,5},{8,10},{10,8},{9,1... | collective-permute-start | bytes 196616 | tf_op jit(solution)/shard_map/ppermute | solution.py:758
  36.7 3.4 %collective-permute-start.8 = (f32[8,32,128]{2,1,0:T(8,128)S(1)}, f32[8,32,128]{2,1,0:T(8,128)S(1)}, u32[]{:S(2)}, u32[]{:S(2)}) collective-permute-start(f32[8,32,128]{2,1,0:T(8,128)S(1)} %get-tuple-element.43.refs_3_.refs_8_), channel_id=1, source_target_pairs={{0,1},{1,0},{2,3},{3,2},{4,5},{5,4},{6,7},{7,6},{8,9},{9,8},{10,11... | collective-permute-start | bytes 393224 | tf_op jit(solution)/shard_map/ppermute | solution.py:686
  40.0 1.3 %collective-permute-start.9 = (f32[16,8,128]{2,1,0:T(8,128)S(1)}, f32[16,8,128]{2,1,0:T(8,128)S(1)}, u32[]{:S(2)}, u32[]{:S(2)}) collective-permute-start(f32[16,8,128]{2,1,0:T(8,128)S(1)} %collective-permute-done.5.refs_14_), channel_id=1, source_target_pairs={{0,1},{1,0},{2,3},{3,2},{4,5},{5,4},{6,7},{7,6},{8,9},{9,8},{10,11... | collective-permute-start | bytes 196616 | tf_op jit(solution)/shard_map/ppermute | solution.py:686

commit v5 on v4

--- a/solution.py
+++ b/solution.py
@@ -34,7 +34,6 @@
 
 
 VMEM = pl.BlockSpec(memory_space=pltpu.VMEM)
-SMEM = pl.BlockSpec(memory_space=pltpu.SMEM)
 HBM = pl.BlockSpec(memory_space=pltpu.HBM)
 
 
@@ -183,7 +182,7 @@
 
 
 def source_body(
-    each, got_ref, conductivity_ref, storage_ref, state_ref, out_ref, up_ref, down_ref
+    each, got_ref, conductivity_ref, storage_ref, state_ref, out_ref, near_ref, far_ref
 ):
     peers = got_ref.shape[0]
     nz, nx = state_ref.shape[0], state_ref.shape[1]
@@ -227,9 +226,12 @@
         total = part if total is None else total + part
     total = jnp.transpose(total[:LANES] + total[LANES:])
     out_ref[...] = total.reshape(nz, nx, LANES)
-    for f, field in enumerate((conductivity_ref, storage_ref, state_ref, out_ref)):
-        up_ref[f] = field[:, nx - HALO :, :]
-        down_ref[f] = field[:, :HALO, :]
+    even = (lax.axis_index("cols") & 1) == 0
+    total = total.reshape(nz, nx, LANES)
+    for f, field in enumerate((conductivity_ref, storage_ref, state_ref, total)):
+        low, high = field[:, :HALO, :], field[:, nx - HALO :, :]
+        near_ref[f] = jnp.where(even, high, low)
+        far_ref[f] = jnp.where(even, low, high)
 
 
 def all_sum(x):
@@ -242,8 +244,9 @@
     return jnp.where(b > 0.0, a / jnp.where(b > 0.0, b, 1.0), 0.0)
 
 
-def pack_body(low_side, where_ref, *refs):
-    *fields, low_ref, high_ref, out_ref = refs
+def pack_body(low_side, *refs):
+    *fields, near_ref, far_ref, out_ref = refs
+    even = (lax.axis_index("cols") & 1) == 0
     nz, nx = fields[0].shape[0], fields[0].shape[1]
     lanes = lane_iota(2 * (nx + 2 * HALO))
     tall = jnp.zeros(lanes.shape, jnp.float32)
@@ -254,12 +257,16 @@
                 [
                     part
                     for f in (2 * pair, 2 * pair + 1)
-                    for part in (low_ref[f, z], fields[f][z], high_ref[f, z])
+                    for part in (
+                        jnp.where(even, far_ref[f, z], near_ref[f, z]),
+                        fields[f][z],
+                        jnp.where(even, near_ref[f, z], far_ref[f, z]),
+                    )
                 ],
                 axis=0,
             )
             if low_side is None:
-                shift = (at + jnp.where(where_ref[1] == 0, HALO, 0)) & (LANES - 1)
+                shift = (at + jnp.where(lax.axis_index("rows") == 0, HALO, 0)) & (LANES - 1)
             else:
                 shift = at if low_side else (at + HALO) & (LANES - 1)
             x = pltpu.roll(x, shift, 1)
@@ -289,26 +296,28 @@
     return pltpu.roll(x, 1, 0)
 
 
-def unpack(layer, f, own, other, edges, padded, top=0):
+def unpack(f, own, other, edges, padded, top=0):
     nz, nx = own.shape[0], own.shape[1]
+    layer, even = lax.axis_index("layers"), (lax.axis_index("cols") & 1) == 0
+    after = pl.multiple_of(jnp.where(even, top + HALO + nx, top), HALO)
+    before = pl.multiple_of(jnp.where(even, top, top + HALO + nx), HALO)
     for half, block in ((0, own), (1, other)):
-        low, high = edges[2 * half], edges[2 * half + 1]
+        near, far = edges[2 * half], edges[2 * half + 1]
         for i in range(nz):
             j = jnp.where(layer == 0, i, nz - 1 - i)
             to = half * nz + i
-            padded[to, top : top + HALO, :] = low[f, j]
             padded[to, top + HALO : top + HALO + nx, :] = block[j]
-            padded[to, top + HALO + nx : top + 2 * HALO + nx, :] = high[f, j]
-
-
-def prepare_body(where_ref, *refs):
+            padded[to, pl.ds(after, HALO), :] = near[f, j]
+            padded[to, pl.ds(before, HALO), :] = far[f, j]
+
+
+def prepare_body(*refs):
     own, other, edges = refs[:3], refs[3:6], refs[6:10]
     c_pad, diag, wx, wx_back, wy, wz, grads, outer, s_pad, h_pad = refs[10:]
-    layer = where_ref[0]
     nz, nx = own[0].shape[0], own[0].shape[1]
     planes, width = c_pad.shape[0], c_pad.shape[1]
     for f, target in enumerate((c_pad, s_pad, h_pad)):
-        unpack(layer, f, own[f], other[f], edges, target)
+        unpack(f, own[f], other[f], edges, target)
     lanes = lane_iota(width)
     last = lanes == LANES - 1
     for z in range(planes):
@@ -350,13 +359,13 @@
     outer[...] = kept(mine, -0.5 * c_pad[0] * h_pad[0])
 
 
-def basis_body(peers, side_count, where_ref, *refs):
+def basis_body(peers, side_count, *refs):
     c_pad, diag_in, wx, wx_back, wy, wz, grads, outer = refs[:8]
     b_own, b_other, edges, refs = refs[8], refs[9], refs[10:14], refs[14:]
     sides = list(zip(refs[:side_count], refs[side_count : 2 * side_count]))
     spot_ref, slots_ref, own_ref, send_ref = refs[2 * side_count : 2 * side_count + 4]
     diag, ws, edge_grads, image, basis = refs[2 * side_count + 4 :]
-    layer, row = where_ref[0], where_ref[1]
+    layer, row = lax.axis_index("layers"), lax.axis_index("rows")
     nz, nx = b_own.shape[0], b_own.shape[1]
     planes, width = c_pad.shape[0], c_pad.shape[1]
     span = HALO + nx
@@ -367,7 +376,7 @@
         for z in range(planes):
             basis[k, z, :top, :] = jnp.zeros((top, LANES), jnp.float32)
             basis[k, z, top + width :, :] = jnp.zeros((top, LANES), jnp.float32)
-    unpack(layer, 3, b_own, b_other, edges, basis.at[0], top)
+    unpack(3, b_own, b_other, edges, basis.at[0], top)
 
     lanes, rows = lane_iota(width), row_iota(width)
     y_at = lanes & (HALO - 1)
@@ -573,7 +582,7 @@
                 send_ref[peer * copies + copy, k : k + 1, :] = rows[peer : peer + 1]
 
 
-def solve_body(copies, where_ref, got_ref, own_ref, adjoint_ref, pilot_ref):
+def solve_body(copies, got_ref, own_ref, adjoint_ref, pilot_ref):
     senders = got_ref.shape[0]
     peers = senders // copies
     groups = senders * ITERS // LANES
@@ -587,20 +596,25 @@
     at = lane_iota(groups) & (ITERS - 1)
     gamma_next = jnp.where(at < ITERS - 1, pltpu.roll(gamma, LANES - 1, 1), 0.0)
 
+    def over_senders(x):
+        for shift in (8, 16, 32, 64):
+            x = x + pltpu.roll(x, shift, 1)
+        return jnp.sum(x, axis=0, keepdims=True)
+
+    norm = over_senders(weight)
+    means = safe_ratio(over_senders(weight * alpha), norm)
+    growth = safe_ratio(norm, pltpu.roll(norm, 1, 1))
     now = jnp.where(at == 0, 1.0, 0.0)
-    last, norm_last = None, None
-    common = []
-    for k in range(ITERS):
-        common.append(now)
-        if k == ITERS - 1:
-            break
+    last = None
+    common = [now]
+    for k in range(ITERS - 1):
         image = jnp.where(at > 0, pltpu.roll(now, 1, 1), 0.0) + alpha * now
         image = image + gamma_next * pltpu.roll(now, LANES - 1, 1)
-        norm = all_sum(weight * now * now)
-        following = image - safe_ratio(all_sum(weight * now * image), norm) * now
+        following = image - means[:, k : k + 1] * now
         if k:
-            following = following - safe_ratio(norm, norm_last) * last
-        now, last, norm_last = following, now, norm
+            following = following - growth[:, k : k + 1] * last
+        now, last = following, now
+        common.append(now)
 
     lanes = lane_iota(ITERS)
     system = jnp.zeros((ITERS, LANES), jnp.float32)
@@ -629,7 +643,7 @@
     answer = system[:, ITERS : ITERS + 1]
 
     weights = [jnp.sum(answer * t, axis=0, keepdims=True) for t in stacked]
-    me = where_ref[3]
+    me = lax.axis_index(GRID_AXES)
     mine = []
     for k in range(ITERS):
         w = jnp.zeros((1, 1), jnp.float32)
@@ -682,6 +696,11 @@
     return forward, [(b, a) for a, b in forward]
 
 
+def swap_pairs(axis, first):
+    pairs = [(i, i + 1) for i in range(first, lax.axis_size(axis) - 1, 2)]
+    return pairs + [(b, a) for a, b in pairs]
+
+
 def swapped(x):
     return lax.ppermute(x, "layers", [(0, 1), (1, 0)])
 
@@ -710,10 +729,6 @@
     def flat(x):
         return x.reshape(gauges // LANES, LANES)
 
-    where = jnp.stack(
-        [lax.axis_index(a) for a in ("layers", "rows", "cols", GRID_AXES)]
-    ).astype(jnp.int32)
-
     obs = pltpu.VMEM((gauges // LANES, LANES), f32)
     obs_int = pltpu.VMEM((gauges // LANES, LANES), jnp.int32)
     payload = kernel_call(
@@ -734,27 +749,26 @@
     fixed = (conductivity, storage, state_field)
     got, spot, *fixed_other = tied(got, spot, *(swapped(x) for x in fixed))
     edge = shape(4, nz, HALO, LANES)
-    source, up, down = kernel_call(
+    source, near, far = kernel_call(
         functools.partial(source_body, capacity // LANES),
         (shape(nz, nx, LANES), edge, edge),
         weight=6,
     )(in_specs=[VMEM] * 4, out_specs=(VMEM,) * 3)(got, *fixed)
-    forward, backward = neighbour_pairs("cols")
-    low = lax.ppermute(up, "cols", forward)
-    high = lax.ppermute(down, "cols", backward)
+    near = lax.ppermute(near, "cols", swap_pairs("cols", 0))
+    far = lax.ppermute(far, "cols", swap_pairs("cols", 1))
     other = swapped(source)
 
     def packed(low_side):
         return kernel_call(
             functools.partial(pack_body, low_side), shape(2 * nz, HALO, LANES)
-        )(in_specs=[SMEM] + [VMEM] * 6, out_specs=VMEM)(where, *fixed, source, low, high)
+        )(in_specs=[VMEM] * 6, out_specs=VMEM)(*fixed, source, near, far)
 
     if row_count == 2:
         send = [(packed(None), [(0, 1), (1, 0)])]
     else:
         forward, backward = neighbour_pairs("rows")
         send = [(packed(False), forward), (packed(True), backward)]
-    edges = tied(low, high, swapped(low), swapped(high), *(x for x, _ in send))[:4]
+    edges = tied(near, far, swapped(near), swapped(far), *(x for x, _ in send))[:4]
     sides = [lax.ppermute(x, "rows", pairs) for x, pairs in send]
     planes, width, span = 2 * nz, nx + 2 * HALO, nx + HALO
     padded = (planes, width, LANES)
@@ -763,7 +777,7 @@
         (*(shape(*padded) for _ in range(6)), shape(6, nz, span, LANES), shape(span, LANES)),
         [pltpu.VMEM(padded, f32)] * 2,
         weight=3,
-    )(in_specs=[SMEM] + [VMEM] * 10, out_specs=(VMEM,) * 8)(where, *fixed, *fixed_other, *edges)
+    )(in_specs=[VMEM] * 10, out_specs=(VMEM,) * 8)(*fixed, *fixed_other, *edges)
     *sides, prepared = tied(*sides, prepared)
     sides = sides + [swapped(x) for x in sides]
 
@@ -779,13 +793,13 @@
             pltpu.VMEM((ITERS + 1, planes, width + 2 * HALO, LANES), f32),
         ],
         weight=10,
-    )(in_specs=[SMEM] + [VMEM] * (16 + len(sides)), out_specs=(VMEM, VMEM))(
-        where, *prepared, source, other, *edges, *sides, spot, slots
+    )(in_specs=[VMEM] * (16 + len(sides)), out_specs=(VMEM, VMEM))(
+        *prepared, source, other, *edges, *sides, spot, slots
     )
     parts = lax.all_to_all(send, GRID_AXES, 0, 0, tiled=True)
     adjoint, pilot = kernel_call(
         functools.partial(solve_body, devices // peers), (shape(nz, nx, ny), shape(each, LANES))
-    )(in_specs=[SMEM] + [VMEM] * 2, out_specs=(VMEM, VMEM))(where, parts, own)
+    )(in_specs=[VMEM] * 2, out_specs=(VMEM, VMEM))(parts, own)
     return adjoint, pilot.reshape(-1)
 
 

time: 63.1 us -> 59 us (0.935)
  Pallas kernels: 23 us -> 20.3 us
  starting transfers between devices: 13.1 us -> 10.9 us
  blocking collectives: 10.2 us -> 12.2 us
  waiting for transfers between devices: 14.7 us -> 13.7 us
    ppermute x2, starting transfers between devices: 3.67 us -> 1.19 us  [the longest x1 0.84 us: on_device(): far = lax.ppermute(far, 'cols', swap_pairs('cols', 1))]
    all_to_all x1, blocking collectives: 10.2 us -> 12.2 us  [on_device(): parts = lax.all_to_all(send, GRID_AXES, 0, 0, tiled=True)]
    ppermute x2, waiting for transfers between devices: 5.37 us -> 3.84 us  [the longest x1 3.84 us: on_device(): near = lax.ppermute(near, 'cols', swap_pairs('cols', 0))]
    pallas_call x1, Pallas kernels: 7.25 us -> 6.35 us  [on_device(): kernel_call(functools.partial(basis_body, peers, len(sides) // 2), (shape...]
    pallas_call x1, Pallas kernels: 3.84 us -> 3.03 us  [on_device(): kernel_call(functools.partial(solve_body, devices // peers), (shape(nz, n...]
  transfers between devices with their start and end apart: 11 -> 11, of which waited for: 5 -> 4; matrix products, arithmetic and copies ran while one was open for 0% -> 0% of each run, Pallas kernels for 4% -> 3%
where the time goes in v5:
time: 59 us; the launch traced here: 58.5 us
  Pallas kernels  20.3 us (34%)
  waiting for transfers between devices  13.7 us (23%)
  blocking collectives  12.2 us (21%)
  starting transfers between devices  10.9 us (18%)
  local copies, waits for them, and re-layouts  0.74 us (1%)
  between operations  0.73 us (1%)
    all_to_all x1, blocking collectives, on_device(): parts = lax.all_to_all(send, GRID_AXES, 0, 0, tiled=True)  12.2 us
    all_to_all x1, starting transfers between devices, on_device(): got = lax.all_to_all(payload, PEER_AXES, 0, 0, tiled=True)  7.4 us
    pallas_call x1, Pallas kernels, on_device(): kernel_call(functools.partial(basis_body, peers, len(sides) // 2), (shape...  6.35 us
    all_to_all x1, waiting for transfers between devices, on_device(): got = lax.all_to_all(payload, PEER_AXES, 0, 0, tiled=True)  6.02 us
    pallas_call x1, Pallas kernels, on_device(): kernel_call(functools.partial(source_body, capacity // LANES), (shape(nz,...  5.19 us
    pallas_call x1, Pallas kernels, on_device(): kernel_call(functools.partial(route_body, peers, capacity), shape(peers,...  4.22 us
    ppermute x1, waiting for transfers between devices, on_device(): near = lax.ppermute(near, 'cols', swap_pairs('cols', 0))  3.84 us
    pallas_call x1, Pallas kernels, on_device(): kernel_call(functools.partial(solve_body, devices // peers), (shape(nz, n...  3.03 us
  transfers between devices with their start and end apart: 11, of which 4 were waited for; matrix products, arithmetic and copies ran while one was open for 0% of the time, Pallas kernels for 3%

profile of v5, /device:TPU:0, one launch (start us, length us, event | category | flops | bytes accessed | tf_op | source)
XLA Modules:
  0.0 58.5 jit_solution(4166542879761078475)
XLA Ops:
  0.6 4.2 %shard_map.95 = f32[8,48,128]{2,1,0:T(8,128)} custom-call(s32[32,128]{1,0:T(8,128)} %bitcast.5, s32[32,128]{1,0:T(8,128)} %bitcast.6, f32[32,128]{1,0:T(8,128)} %bitcast.7, f32[32,128]{1,0:T(8,128)} %bitcast.8), custom_call_target="tpu_custom_call" | custom-call | bytes 15000000 | tf_op jit(solution)/shard_map/pallas_call | solution.py:734
  4.9 0.0 copy-start.2
  4.9 0.0 copy-start
  4.9 0.0 copy-start.1
  4.9 7.4 %all-to-all-start = ((f32[8,48,128]{2,1,0:T(8,128)}), f32[8,48,128]{2,1,0:T(8,128)S(1)}, u32[]{:S(2)}, u32[]{:S(2)}) async-start(f32[8,48,128]{2,1,0:T(8,128)} %shard_map.95), calls=%async_computation | async-start | bytes 393216 | tf_op jit(solution)/shard_map/all_to_all | solution.py:744
  12.3 0.0 copy-done.2
  12.3 0.1 collective-permute-start.2
  12.4 0.0 copy-done
  12.4 0.5 collective-permute-start
  12.9 0.0 copy-done.1
  12.9 0.1 collective-permute-start.1
  13.0 0.0 copy-start.3
  13.0 0.7 %copy-done.3 = s32[32,128]{1,0:T(8,128)S(1)} copy-done((s32[32,128]{1,0:T(8,128)S(1)}, s32[32,128]{1,0:T(8,128)}, u32[]{:S(2)}) %copy-start.3) | copy-done | bytes 16408
  13.7 0.5 shard_map.96
  14.2 0.0 collective-permute-done.2.refs_5_
  14.2 0.0 collective-permute-done.refs_3_
  14.2 0.0 collective-permute-done.1.refs_4_
  14.2 6.0 %all-to-all-done.got_ref = f32[8,48,128]{2,1,0:T(8,128)S(1)} async-done(((f32[8,48,128]{2,1,0:T(8,128)}), f32[8,48,128]{2,1,0:T(8,128)S(1)}, u32[]{:S(2)}, u32[]{:S(2)}) %all-to-all-start) | async-done | bytes 196640 | tf_op jit(solution)/shard_map/all_to_all | solution.py:744
  20.2 5.2 %shard_map.97 = (f32[8,32,128]{2,1,0:T(8,128)S(1)}, f32[4,8,8,128]{3,2,1,0:T(8,128)S(1)}, f32[4,8,8,128]{3,2,1,0:T(8,128)S(1)}) custom-call(f32[8,48,128]{2,1,0:T(8,128)S(1)} %all-to-all-done.got_ref, f32[8,32,128]{2,1,0:T(8,128)S(1)} %copy-done, f32[8,32,128]{2,1,0:T(8,128)S(1)} %copy-done.1, f32[8,32,128]{2,1,0:T(8,128)S(1)} %copy-done.2), custom_call_target="tpu_custom_call" | custom-call | bytes 18000000 | tf_op jit(solution)/shard_map/pallas_call | solution.py:752
  25.4 0.3 collective-permute-start.3
  25.8 0.8 %collective-permute-start.4 = (f32[4,8,8,128]{3,2,1,0:T(8,128)S(1)}, f32[4,8,8,128]{3,2,1,0:T(8,128)S(1)}, u32[]{:S(2)}, u32[]{:S(2)}) collective-permute-start(f32[4,8,8,128]{3,2,1,0:T(8,128)S(1)} %get-tuple-element.45), channel_id=1, source_target_pairs={{4,8},{8,4},{5,9},{9,5},{6,10},{10,6},{7,11},{11,7},{20,24},{24,20... | collective-permute-start | bytes 393224 | tf_op jit(solution)/shard_map/ppermute | solution.py:758
  26.6 3.8 %collective-permute-done.3.refs_4_.refs_6_.refs_10_ = f32[4,8,8,128]{3,2,1,0:T(8,128)S(1)} collective-permute-done((f32[4,8,8,128]{3,2,1,0:T(8,128)S(1)}, f32[4,8,8,128]{3,2,1,0:T(8,128)S(1)}, u32[]{:S(2)}, u32[]{:S(2)}) %collective-permute-start.3) | collective-permute-done | bytes 131104 | tf_op jit(solution)/shard_map/ppermute | solution.py:757
  30.5 0.0 collective-permute-start.6
  30.5 0.0 collective-permute-done.4.refs_5_.refs_7_.refs_11_
  30.5 0.5 collective-permute-start.7
  31.0 0.4 shard_map.98
  31.4 1.1 %collective-permute-start.5 = (f32[16,8,128]{2,1,0:T(8,128)S(1)}, f32[16,8,128]{2,1,0:T(8,128)S(1)}, u32[]{:S(2)}, u32[]{:S(2)}) collective-permute-start(f32[16,8,128]{2,1,0:T(8,128)S(1)} %shard_map.98), channel_id=1, source_target_pairs={{0,2},{2,0},{1,3},{3,1},{4,6},{6,4},{5,7},{7,5},{8,10},{10,8},{9,1... | collective-permute-start | bytes 196616 | tf_op jit(solution)/shard_map/ppermute | solution.py:772
  32.5 0.0 collective-permute-start.8
  32.5 0.0 collective-permute-done.6.refs_8_.refs_12_
  32.5 0.0 collective-permute-done.7.refs_9_.refs_13_
  32.5 0.6 %shard_map.99 = (f32[16,48,128]{2,1,0:T(8,128)S(1)}, f32[16,48,128]{2,1,0:T(8,128)S(1)}, f32[16,48,128]{2,1,0:T(8,128)S(1)}, f32[16,48,128]{2,1,0:T(8,128)S(1)},...) custom-call(f32[8,32,128]{2,1,0:T(8,128)S(1)} %copy-done, ...), custom_call_target="tpu_custom_call" | custom-call | bytes 9000000 | tf_op jit(solution)/shard_map/pallas_call | solution.py:775
  33.1 2.5 %collective-permute-done.5.refs_14_ = f32[16,8,128]{2,1,0:T(8,128)S(1)} collective-permute-done((f32[16,8,128]{2,1,0:T(8,128)S(1)}, f32[16,8,128]{2,1,0:T(8,128)S(1)}, u32[]{:S(2)}, u32[]{:S(2)}) %collective-permute-start.5) | collective-permute-done | bytes 65568 | tf_op jit(solution)/shard_map/ppermute | solution.py:772
  35.7 0.0 collective-permute-start.9
  35.7 0.0 collective-permute-done.8.refs_9_
  35.7 1.2 %collective-permute-done.9.refs_15_ = f32[16,8,128]{2,1,0:T(8,128)S(1)} collective-permute-done((f32[16,8,128]{2,1,0:T(8,128)S(1)}, f32[16,8,128]{2,1,0:T(8,128)S(1)}, u32[]{:S(2)}, u32[]{:S(2)}) %collective-permute-start.9) | collective-permute-done | bytes 65568 | tf_op jit(solution)/shard_map/ppermute | solution.py:705
  36.9 6.3 %shard_map.100 = (f32[8,8,32,128]{3,2,1,0:T(8,128)S(1)}, f32[16,8,128]{2,1,0:T(8,128)S(1)}) custom-call(f32[16,48,128]{2,1,0:T(8,128)S(1)} %get-tuple-element.61.refs_0_, f32[16,48,128]{2,1,0:T(8,128)S(1)} %get-tuple-element.62.refs_1_, f32[16,48,128]{2,1,0:T(8,128)S(1)} %get-tuple-element.63.refs_2_, f32[16,48,128]{2,1,0:T(8,128)S(1)} %get-tuple-element.64.refs_3_, ...), custom_call_target="tpu_custom_call" | custom-call | bytes 30000000 | tf_op jit(solution)/shard_map/pallas_call | solution.py:785
  43.3 12.2 %all_to_all.10.got_ref = f32[16,8,128]{2,1,0:T(8,128)S(1)} all-to-all(f32[16,8,128]{2,1,0:T(8,128)S(1)} %get-tuple-element.72), channel_id=1, replica_groups=mesh['groups'=2,'cols'=4,'rows'=2,'layers'=2] {'cols','rows','layers'}, dimensions={0} | all-to-all | bytes 131072 | tf_op jit(solution)/shard_map/all_to_all | solution.py:799
  55.5 3.0 %shard_map.101 = (f32[8,32,128]{2,1,0:T(8,128)}, f32[4,128]{1,0:T(4,128)}) custom-call(f32[16,8,128]{2,1,0:T(8,128)S(1)} %all_to_all.10.got_ref, f32[8,8,32,128]{3,2,1,0:T(8,128)S(1)} %get-tuple-element.73.own_ref), custom_call_target="tpu_custom_call" | custom-call | bytes 3000000 | tf_op jit(solution)/shard_map/pallas_call | solution.py:800
Async XLA Ops:
  4.9 7.4 %copy-start.2 = (f32[8,32,128]{2,1,0:T(8,128)S(1)}, f32[8,32,128]{2,1,0:T(8,128)}, u32[]{:S(2)}) copy-start(f32[8,32,128]{2,1,0:T(8,128)} %refs_2_.3) | copy-start | bytes 393220
  4.9 7.5 %copy-start = (f32[8,32,128]{2,1,0:T(8,128)S(1)}, f32[8,32,128]{2,1,0:T(8,128)}, u32[]{:S(2)}) copy-start(f32[8,32,128]{2,1,0:T(8,128)} %refs_0_.3) | copy-start | bytes 393220
  4.9 8.0 %copy-start.1 = (f32[8,32,128]{2,1,0:T(8,128)S(1)}, f32[8,32,128]{2,1,0:T(8,128)}, u32[]{:S(2)}) copy-start(f32[8,32,128]{2,1,0:T(8,128)} %refs_1_.3) | copy-start | bytes 393220
  4.9 15.4 %all-to-all-start = ((f32[8,48,128]{2,1,0:T(8,128)}), f32[8,48,128]{2,1,0:T(8,128)S(1)}, u32[]{:S(2)}, u32[]{:S(2)}) async-start(f32[8,48,128]{2,1,0:T(8,128)} %shard_map.95), calls=%async_computation | async-start | bytes 393216 | tf_op jit(solution)/shard_map/all_to_all | solution.py:744
  12.3 1.9 %collective-permute-start.2 = (f32[8,32,128]{2,1,0:T(8,128)S(1)}, f32[8,32,128]{2,1,0:T(8,128)S(1)}, u32[]{:S(2)}, u32[]{:S(2)}) collective-permute-start(f32[8,32,128]{2,1,0:T(8,128)S(1)} %copy-done.2), channel_id=1, source_target_pairs={{0,1},{1,0},{2,3},{3,2},{4,5},{5,4},{6,7},{7,6},{8,9},{9,8},{10,11... | collective-permute-start | bytes 393224 | tf_op jit(solution)/shard_map/ppermute | solution.py:705
  12.4 1.8 %collective-permute-start = (f32[8,32,128]{2,1,0:T(8,128)S(1)}, f32[8,32,128]{2,1,0:T(8,128)S(1)}, u32[]{:S(2)}, u32[]{:S(2)}) collective-permute-start(f32[8,32,128]{2,1,0:T(8,128)S(1)} %copy-done), channel_id=1, source_target_pairs={{0,1},{1,0},{2,3},{3,2},{4,5},{5,4},{6,7},{7,6},{8,9},{9,8},{10,11... | collective-permute-start | bytes 393224 | tf_op jit(solution)/shard_map/ppermute | solution.py:705
  12.9 1.3 %collective-permute-start.1 = (f32[8,32,128]{2,1,0:T(8,128)S(1)}, f32[8,32,128]{2,1,0:T(8,128)S(1)}, u32[]{:S(2)}, u32[]{:S(2)}) collective-permute-start(f32[8,32,128]{2,1,0:T(8,128)S(1)} %copy-done.1), channel_id=1, source_target_pairs={{0,1},{1,0},{2,3},{3,2},{4,5},{5,4},{6,7},{7,6},{8,9},{9,8},{10,11... | collective-permute-start | bytes 393224 | tf_op jit(solution)/shard_map/ppermute | solution.py:705
  13.0 0.7 %copy-start.3 = (s32[32,128]{1,0:T(8,128)S(1)}, s32[32,128]{1,0:T(8,128)}, u32[]{:S(2)}) copy-start(s32[32,128]{1,0:T(8,128)} %pilot_ref) | copy-start | bytes 49156
  25.4 5.0 %collective-permute-start.3 = (f32[4,8,8,128]{3,2,1,0:T(8,128)S(1)}, f32[4,8,8,128]{3,2,1,0:T(8,128)S(1)}, u32[]{:S(2)}, u32[]{:S(2)}) collective-permute-start(f32[4,8,8,128]{3,2,1,0:T(8,128)S(1)} %get-tuple-element.44), channel_id=1, source_target_pairs={{0,4},{8,12},{4,0},{12,8},{1,5},{9,13},{5,1},{13,9},{2,6},{10,14},... | collective-permute-start | bytes 393224 | tf_op jit(solution)/shard_map/ppermute | solution.py:757
  25.8 4.7 %collective-permute-start.4 = (f32[4,8,8,128]{3,2,1,0:T(8,128)S(1)}, f32[4,8,8,128]{3,2,1,0:T(8,128)S(1)}, u32[]{:S(2)}, u32[]{:S(2)}) collective-permute-start(f32[4,8,8,128]{3,2,1,0:T(8,128)S(1)} %get-tuple-element.45), channel_id=1, source_target_pairs={{4,8},{8,4},{5,9},{9,5},{6,10},{10,6},{7,11},{11,7},{20,24},{24,20... | collective-permute-start | bytes 393224 | tf_op jit(solution)/shard_map/ppermute | solution.py:758
  30.5 2.0 %collective-permute-start.6 = (f32[4,8,8,128]{3,2,1,0:T(8,128)S(1)}, f32[4,8,8,128]{3,2,1,0:T(8,128)S(1)}, u32[]{:S(2)}, u32[]{:S(2)}) collective-permute-start(f32[4,8,8,128]{3,2,1,0:T(8,128)S(1)} %collective-permute-done.3.refs_4_.refs_6_.refs_10_), channel_id=1, source_target_pairs={{0,1},{1,0},{2,3},{3,2},{4,5},{5,4},{6,7},{7,6},{8,9},{9,8},{10,11... | collective-permute-start | bytes 393224 | tf_op jit(solution)/shard_map/ppermute | solution.py:705
  30.5 2.0 %collective-permute-start.7 = (f32[4,8,8,128]{3,2,1,0:T(8,128)S(1)}, f32[4,8,8,128]{3,2,1,0:T(8,128)S(1)}, u32[]{:S(2)}, u32[]{:S(2)}) collective-permute-start(f32[4,8,8,128]{3,2,1,0:T(8,128)S(1)} %collective-permute-done.4.refs_5_.refs_7_.refs_11_), channel_id=1, source_target_pairs={{0,1},{1,0},{2,3},{3,2},{4,5},{5,4},{6,7},{7,6},{8,9},{9,8},{10,11... | collective-permute-start | bytes 393224 | tf_op jit(solution)/shard_map/ppermute | solution.py:705
  31.4 4.3 %collective-permute-start.5 = (f32[16,8,128]{2,1,0:T(8,128)S(1)}, f32[16,8,128]{2,1,0:T(8,128)S(1)}, u32[]{:S(2)}, u32[]{:S(2)}) collective-permute-start(f32[16,8,128]{2,1,0:T(8,128)S(1)} %shard_map.98), channel_id=1, source_target_pairs={{0,2},{2,0},{1,3},{3,1},{4,6},{6,4},{5,7},{7,5},{8,10},{10,8},{9,1... | collective-permute-start | bytes 196616 | tf_op jit(solution)/shard_map/ppermute | solution.py:772
  32.5 3.2 %collective-permute-start.8 = (f32[8,32,128]{2,1,0:T(8,128)S(1)}, f32[8,32,128]{2,1,0:T(8,128)S(1)}, u32[]{:S(2)}, u32[]{:S(2)}) collective-permute-start(f32[8,32,128]{2,1,0:T(8,128)S(1)} %get-tuple-element.43.refs_3_.refs_8_), channel_id=1, source_target_pairs={{0,1},{1,0},{2,3},{3,2},{4,5},{5,4},{6,7},{7,6},{8,9},{9,8},{10,11... | collective-permute-start | bytes 393224 | tf_op jit(solution)/shard_map/ppermute | solution.py:705
  35.7 1.3 %collective-permute-start.9 = (f32[16,8,128]{2,1,0:T(8,128)S(1)}, f32[16,8,128]{2,1,0:T(8,128)S(1)}, u32[]{:S(2)}, u32[]{:S(2)}) collective-permute-start(f32[16,8,128]{2,1,0:T(8,128)S(1)} %collective-permute-done.5.refs_14_), channel_id=1, source_target_pairs={{0,1},{1,0},{2,3},{3,2},{4,5},{5,4},{6,7},{7,6},{8,9},{9,8},{10,11... | collective-permute-start | bytes 196616 | tf_op jit(solution)/shard_map/ppermute | solution.py:705

commit v6 on v5

--- a/solution.py
+++ b/solution.py
@@ -9,6 +9,7 @@
 
 ITERS = 8
 HALO = 8
+EDGE = (0, 1, 1, 2)
 FACTS = 64
 SLOTS = 96
 LANES = 128
@@ -42,6 +43,11 @@
     rest = x - first
     second = rest.astype(jnp.bfloat16).astype(jnp.float32)
     return first, second, rest - second
+
+
+def halves_of(x):
+    first = x.astype(jnp.bfloat16).astype(jnp.float32)
+    return first, x - first
 
 
 def row_iota(rows, lanes=LANES):
@@ -116,11 +122,12 @@
     ]
     for copy in copies:
         copy.start()
-    for copy in copies:
-        copy.wait()
+    copies[0].wait()
     rows = owner_ref.shape[0]
     owner = owner_ref[...]
     position = owner * capacity + ranks(owner, peers)
+    for copy in copies[1:]:
+        copy.wait()
     slot_row = lax.shift_right_logical(position, LANE_BITS).astype(jnp.float32)
     slot_lane = (position & (LANES - 1)).astype(jnp.float32)
     cell = cell_ref[...]
@@ -128,7 +135,7 @@
         lax.shift_right_logical(cell, LANE_BITS).astype(jnp.float32),
         (cell & (LANES - 1)).astype(jnp.float32),
         *pieces_of(value_ref[...]),
-        *pieces_of(weight_ref[...]),
+        *halves_of(weight_ref[...]),
     ]
     slot_rows = peers * capacity // LANES
     one = jnp.ones((TILE, LANES), jnp.bfloat16)
@@ -147,7 +154,7 @@
     fields = [
         part[0] * LANES + part[1],
         part[2] + part[3] + part[4],
-        part[5] + part[6] + part[7],
+        part[5] + part[6],
     ]
     fields = [jnp.transpose(f) for f in fields]
     each = capacity // LANES
@@ -202,8 +209,25 @@
         cell = sixteen(group, 0).astype(jnp.int32)
         high = lax.shift_right_logical(cell, LANE_BITS)
         low = cell & (LANES - 1)
+        at_row = jnp.concatenate(
+            [
+                filled16(hits16(cells, spread16(high.astype(jnp.float32), r)), one)
+                for r in range(TILE)
+            ],
+            axis=1,
+        )
         heads = []
-        for r in range(0, TILE, 8):
+        if group == 0:
+            state = jnp.transpose(state_ref[...].reshape(cells, LANES))
+            lines = mm(
+                jnp.concatenate([p.astype(jnp.bfloat16) for p in pieces_of(state)], axis=0), at_row
+            )
+            for r in range(TILE):
+                line = lines[:, r * LANES : (r + 1) * LANES]
+                line = line[:LANES] + line[LANES : 2 * LANES] + line[2 * LANES :]
+                hit = row_iota(LANES) == low[r : r + 1]
+                heads.append(jnp.sum(jnp.where(hit, line, 0.0), axis=0, keepdims=True))
+        for r in range(0, 0 if heads else TILE, 8):
             head = jnp.zeros((8, LANES), jnp.float32)
             for z in range(nz):
                 for x in range(nx):
@@ -212,24 +236,26 @@
                     head = jnp.where(high[r : r + 8] == z * nx + x, line, head)
             heads.append(head)
         misfit = sixteen(group, 2) * (jnp.concatenate(heads, axis=0) - sixteen(group, 1))
-        coarse = misfit.astype(jnp.bfloat16).astype(jnp.float32)
-        pieces = (coarse, misfit - coarse)
-        high, low = high.astype(jnp.float32), low.astype(jnp.float32)
-        at_row, at_lane = [], [[] for _ in pieces]
+        pieces = halves_of(misfit)
+        low = low.astype(jnp.float32)
+        at_lane = [[] for _ in pieces]
         for r in range(TILE):
-            at_row.append(filled16(hits16(cells, spread16(high, r)), one))
             masks = hits16(LANES, spread16(low, r))
             for q, piece in enumerate(pieces):
                 at_lane[q].append(filled16(masks, spread16(piece, r)))
         at_lane = jnp.concatenate([jnp.concatenate(q, axis=1) for q in at_lane], axis=0)
-        part = mm(at_lane, jnp.concatenate(at_row, axis=1), NT)
+        part = mm(at_lane, at_row, NT)
         total = part if total is None else total + part
     total = jnp.transpose(total[:LANES] + total[LANES:])
     out_ref[...] = total.reshape(nz, nx, LANES)
     even = (lax.axis_index("cols") & 1) == 0
     total = total.reshape(nz, nx, LANES)
-    for f, field in enumerate((conductivity_ref, storage_ref, state_ref, total)):
+    at = lax.broadcasted_iota(jnp.int32, (nz, HALO, LANES), 1)
+    for f, field in enumerate((conductivity_ref, storage_ref, total)):
         low, high = field[:, :HALO, :], field[:, nx - HALO :, :]
+        if f == 1:
+            low = jnp.where(at == HALO - 1, state_ref[:, :1, :], low)
+            high = jnp.where(at == 0, state_ref[:, nx - 1 :, :], high)
         near_ref[f] = jnp.where(even, high, low)
         far_ref[f] = jnp.where(even, low, high)
 
@@ -258,9 +284,9 @@
                     part
                     for f in (2 * pair, 2 * pair + 1)
                     for part in (
-                        jnp.where(even, far_ref[f, z], near_ref[f, z]),
+                        jnp.where(even, far_ref[EDGE[f], z], near_ref[EDGE[f], z]),
                         fields[f][z],
-                        jnp.where(even, near_ref[f, z], far_ref[f, z]),
+                        jnp.where(even, near_ref[EDGE[f], z], far_ref[EDGE[f], z]),
                     )
                 ],
                 axis=0,
@@ -307,8 +333,8 @@
             j = jnp.where(layer == 0, i, nz - 1 - i)
             to = half * nz + i
             padded[to, top + HALO : top + HALO + nx, :] = block[j]
-            padded[to, pl.ds(after, HALO), :] = near[f, j]
-            padded[to, pl.ds(before, HALO), :] = far[f, j]
+            padded[to, pl.ds(after, HALO), :] = near[EDGE[f], j]
+            padded[to, pl.ds(before, HALO), :] = far[EDGE[f], j]
 
 
 def prepare_body(*refs):
@@ -318,6 +344,12 @@
     planes, width = c_pad.shape[0], c_pad.shape[1]
     for f, target in enumerate((c_pad, s_pad, h_pad)):
         unpack(f, own[f], other[f], edges, target)
+    none = jnp.zeros((1, LANES), jnp.float32)
+    for z in range(planes):
+        h_pad[z, HALO - 1 : HALO, :] = s_pad[z, :1, :]
+        h_pad[z, width - HALO : width - HALO + 1, :] = s_pad[z, width - 1 :, :]
+        s_pad[z, :1, :] = none
+        s_pad[z, width - 1 :, :] = none
     lanes = lane_iota(width)
     last = lanes == LANES - 1
     for z in range(planes):
@@ -400,6 +432,7 @@
                     second[part] if f // 2 else pltpu.roll(second[part], half, 1),
                 )
             )
+        fields[1] = jnp.where((rows == 0) | (rows == width - 1), 0.0, fields[1])
         shifts = []
         for z in range(planes):
             spot = jnp.where(layer == 0, z, planes - 1 - z) * HALO + meet
@@ -748,7 +781,7 @@
 
     fixed = (conductivity, storage, state_field)
     got, spot, *fixed_other = tied(got, spot, *(swapped(x) for x in fixed))
-    edge = shape(4, nz, HALO, LANES)
+    edge = shape(3, nz, HALO, LANES)
     source, near, far = kernel_call(
         functools.partial(source_body, capacity // LANES),
         (shape(nz, nx, LANES), edge, edge),

time: 59 us -> 58.1 us (0.985)
  Pallas kernels: 20.3 us -> 19.7 us
where the time goes in v6:
time: 58.1 us; the launch traced here: 57.7 us
  Pallas kernels  19.7 us (34%)
  waiting for transfers between devices  13.3 us (23%)
  blocking collectives  12.2 us (21%)
  starting transfers between devices  10.9 us (19%)
  local copies, waits for them, and re-layouts  0.74 us (1%)
  between operations  0.74 us (1%)
    all_to_all x1, blocking collectives, on_device(): parts = lax.all_to_all(send, GRID_AXES, 0, 0, tiled=True)  12.2 us
    all_to_all x1, starting transfers between devices, on_device(): got = lax.all_to_all(payload, PEER_AXES, 0, 0, tiled=True)  7.4 us
    pallas_call x1, Pallas kernels, on_device(): kernel_call(functools.partial(basis_body, peers, len(sides) // 2), (shape...  6.35 us
    all_to_all x1, waiting for transfers between devices, on_device(): got = lax.all_to_all(payload, PEER_AXES, 0, 0, tiled=True)  6.01 us
    pallas_call x1, Pallas kernels, on_device(): kernel_call(functools.partial(source_body, capacity // LANES), (shape(nz,...  4.98 us
    pallas_call x1, Pallas kernels, on_device(): kernel_call(functools.partial(route_body, peers, capacity), shape(peers,...  3.89 us
    ppermute x1, waiting for transfers between devices, on_device(): near = lax.ppermute(near, 'cols', swap_pairs('cols', 0))  3.48 us
    pallas_call x1, Pallas kernels, on_device(): kernel_call(functools.partial(solve_body, devices // peers), (shape(nz, n...  3.03 us
  transfers between devices with their start and end apart: 11, of which 4 were waited for; matrix products, arithmetic and copies ran while one was open for 0% of the time, Pallas kernels for 3%

profile of v6, /device:TPU:0, one launch (start us, length us, event | category | flops | bytes accessed | tf_op | source)
XLA Modules:
  0.0 57.7 jit_solution(3129599391484352724)
XLA Ops:
  0.6 3.9 %shard_map.95 = f32[8,48,128]{2,1,0:T(8,128)} custom-call(s32[32,128]{1,0:T(8,128)} %bitcast.5, s32[32,128]{1,0:T(8,128)} %bitcast.6, f32[32,128]{1,0:T(8,128)} %bitcast.7, f32[32,128]{1,0:T(8,128)} %bitcast.8), custom_call_target="tpu_custom_call" | custom-call | bytes 15000000 | tf_op jit(solution)/shard_map/pallas_call | solution.py:767
  4.5 0.0 copy-start.2
  4.5 0.0 copy-start
  4.6 0.0 copy-start.1
  4.6 7.4 %all-to-all-start = ((f32[8,48,128]{2,1,0:T(8,128)}), f32[8,48,128]{2,1,0:T(8,128)S(1)}, u32[]{:S(2)}, u32[]{:S(2)}) async-start(f32[8,48,128]{2,1,0:T(8,128)} %shard_map.95), calls=%async_computation | async-start | bytes 393216 | tf_op jit(solution)/shard_map/all_to_all | solution.py:777
  12.0 0.0 copy-done.2
  12.0 0.1 collective-permute-start.2
  12.1 0.0 copy-done
  12.1 0.5 collective-permute-start
  12.6 0.0 copy-done.1
  12.6 0.1 collective-permute-start.1
  12.6 0.0 copy-start.3
  12.6 0.7 %copy-done.3 = s32[32,128]{1,0:T(8,128)S(1)} copy-done((s32[32,128]{1,0:T(8,128)S(1)}, s32[32,128]{1,0:T(8,128)}, u32[]{:S(2)}) %copy-start.3) | copy-done | bytes 16408
  13.4 0.5 shard_map.96
  13.8 0.0 collective-permute-done.2.refs_5_
  13.8 0.0 collective-permute-done.refs_3_
  13.9 0.0 collective-permute-done.1.refs_4_
  13.9 6.0 %all-to-all-done.got_ref = f32[8,48,128]{2,1,0:T(8,128)S(1)} async-done(((f32[8,48,128]{2,1,0:T(8,128)}), f32[8,48,128]{2,1,0:T(8,128)S(1)}, u32[]{:S(2)}, u32[]{:S(2)}) %all-to-all-start) | async-done | bytes 196640 | tf_op jit(solution)/shard_map/all_to_all | solution.py:777
  19.9 5.0 %shard_map.97 = (f32[8,32,128]{2,1,0:T(8,128)S(1)}, f32[3,8,8,128]{3,2,1,0:T(8,128)S(1)}, f32[3,8,8,128]{3,2,1,0:T(8,128)S(1)}) custom-call(f32[8,48,128]{2,1,0:T(8,128)S(1)} %all-to-all-done.got_ref, f32[8,32,128]{2,1,0:T(8,128)S(1)} %copy-done, f32[8,32,128]{2,1,0:T(8,128)S(1)} %copy-done.1, f32[8,32,128]{2,1,0:T(8,128)S(1)} %copy-done.2), custom_call_target="tpu_custom_call" | custom-call | bytes 18000000 | tf_op jit(solution)/shard_map/pallas_call | solution.py:785
  24.9 0.4 collective-permute-start.3
  25.3 0.8 %collective-permute-start.4 = (f32[3,8,8,128]{3,2,1,0:T(8,128)S(1)}, f32[3,8,8,128]{3,2,1,0:T(8,128)S(1)}, u32[]{:S(2)}, u32[]{:S(2)}) collective-permute-start(f32[3,8,8,128]{3,2,1,0:T(8,128)S(1)} %get-tuple-element.45), channel_id=1, source_target_pairs={{4,8},{8,4},{5,9},{9,5},{6,10},{10,6},{7,11},{11,7},{20,24},{24,20... | collective-permute-start | bytes 294920 | tf_op jit(solution)/shard_map/ppermute | solution.py:791
  26.1 3.5 %collective-permute-done.3.refs_4_.refs_6_.refs_10_ = f32[3,8,8,128]{3,2,1,0:T(8,128)S(1)} collective-permute-done((f32[3,8,8,128]{3,2,1,0:T(8,128)S(1)}, f32[3,8,8,128]{3,2,1,0:T(8,128)S(1)}, u32[]{:S(2)}, u32[]{:S(2)}) %collective-permute-start.3) | collective-permute-done | bytes 98336 | tf_op jit(solution)/shard_map/ppermute | solution.py:790
  29.6 0.0 collective-permute-start.6
  29.6 0.0 collective-permute-done.4.refs_5_.refs_7_.refs_11_
  29.6 0.5 collective-permute-start.7
  30.1 0.4 shard_map.98
  30.4 1.1 %collective-permute-start.5 = (f32[16,8,128]{2,1,0:T(8,128)S(1)}, f32[16,8,128]{2,1,0:T(8,128)S(1)}, u32[]{:S(2)}, u32[]{:S(2)}) collective-permute-start(f32[16,8,128]{2,1,0:T(8,128)S(1)} %shard_map.98), channel_id=1, source_target_pairs={{0,2},{2,0},{1,3},{3,1},{4,6},{6,4},{5,7},{7,5},{8,10},{10,8},{9,1... | collective-permute-start | bytes 196616 | tf_op jit(solution)/shard_map/ppermute | solution.py:805
  31.6 0.0 collective-permute-start.8
  31.6 0.0 collective-permute-done.6.refs_8_.refs_12_
  31.6 0.0 collective-permute-done.7.refs_9_.refs_13_
  31.6 0.6 %shard_map.99 = (f32[16,48,128]{2,1,0:T(8,128)S(1)}, f32[16,48,128]{2,1,0:T(8,128)S(1)}, f32[16,48,128]{2,1,0:T(8,128)S(1)}, f32[16,48,128]{2,1,0:T(8,128)S(1)},...) custom-call(f32[8,32,128]{2,1,0:T(8,128)S(1)} %copy-done, ...), custom_call_target="tpu_custom_call" | custom-call | bytes 9000000 | tf_op jit(solution)/shard_map/pallas_call | solution.py:808
  32.2 2.5 %collective-permute-done.5.refs_14_ = f32[16,8,128]{2,1,0:T(8,128)S(1)} collective-permute-done((f32[16,8,128]{2,1,0:T(8,128)S(1)}, f32[16,8,128]{2,1,0:T(8,128)S(1)}, u32[]{:S(2)}, u32[]{:S(2)}) %collective-permute-start.5) | collective-permute-done | bytes 65568 | tf_op jit(solution)/shard_map/ppermute | solution.py:805
  34.8 0.0 collective-permute-start.9
  34.8 0.0 collective-permute-done.8.refs_9_
  34.8 1.2 %collective-permute-done.9.refs_15_ = f32[16,8,128]{2,1,0:T(8,128)S(1)} collective-permute-done((f32[16,8,128]{2,1,0:T(8,128)S(1)}, f32[16,8,128]{2,1,0:T(8,128)S(1)}, u32[]{:S(2)}, u32[]{:S(2)}) %collective-permute-start.9) | collective-permute-done | bytes 65568 | tf_op jit(solution)/shard_map/ppermute | solution.py:738
  36.0 6.3 %shard_map.100 = (f32[8,8,32,128]{3,2,1,0:T(8,128)S(1)}, f32[16,8,128]{2,1,0:T(8,128)S(1)}) custom-call(f32[16,48,128]{2,1,0:T(8,128)S(1)} %get-tuple-element.61.refs_0_, f32[16,48,128]{2,1,0:T(8,128)S(1)} %get-tuple-element.62.refs_1_, f32[16,48,128]{2,1,0:T(8,128)S(1)} %get-tuple-element.63.refs_2_, f32[16,48,128]{2,1,0:T(8,128)S(1)} %get-tuple-element.64.refs_3_, ...), custom_call_target="tpu_custom_call" | custom-call | bytes 30000000 | tf_op jit(solution)/shard_map/pallas_call | solution.py:818
  42.4 12.2 %all_to_all.10.got_ref = f32[16,8,128]{2,1,0:T(8,128)S(1)} all-to-all(f32[16,8,128]{2,1,0:T(8,128)S(1)} %get-tuple-element.72), channel_id=1, replica_groups=mesh['groups'=2,'cols'=4,'rows'=2,'layers'=2] {'cols','rows','layers'}, dimensions={0} | all-to-all | bytes 131072 | tf_op jit(solution)/shard_map/all_to_all | solution.py:832
  54.6 3.0 %shard_map.101 = (f32[8,32,128]{2,1,0:T(8,128)}, f32[4,128]{1,0:T(4,128)}) custom-call(f32[16,8,128]{2,1,0:T(8,128)S(1)} %all_to_all.10.got_ref, f32[8,8,32,128]{3,2,1,0:T(8,128)S(1)} %get-tuple-element.73.own_ref), custom_call_target="tpu_custom_call" | custom-call | bytes 3000000 | tf_op jit(solution)/shard_map/pallas_call | solution.py:833
Async XLA Ops:
  4.5 7.4 %copy-start.2 = (f32[8,32,128]{2,1,0:T(8,128)S(1)}, f32[8,32,128]{2,1,0:T(8,128)}, u32[]{:S(2)}) copy-start(f32[8,32,128]{2,1,0:T(8,128)} %refs_2_.3) | copy-start | bytes 393220
  4.5 7.5 %copy-start = (f32[8,32,128]{2,1,0:T(8,128)S(1)}, f32[8,32,128]{2,1,0:T(8,128)}, u32[]{:S(2)}) copy-start(f32[8,32,128]{2,1,0:T(8,128)} %refs_0_.3) | copy-start | bytes 393220
  4.6 8.0 %copy-start.1 = (f32[8,32,128]{2,1,0:T(8,128)S(1)}, f32[8,32,128]{2,1,0:T(8,128)}, u32[]{:S(2)}) copy-start(f32[8,32,128]{2,1,0:T(8,128)} %refs_1_.3) | copy-start | bytes 393220
  4.6 15.3 %all-to-all-start = ((f32[8,48,128]{2,1,0:T(8,128)}), f32[8,48,128]{2,1,0:T(8,128)S(1)}, u32[]{:S(2)}, u32[]{:S(2)}) async-start(f32[8,48,128]{2,1,0:T(8,128)} %shard_map.95), calls=%async_computation | async-start | bytes 393216 | tf_op jit(solution)/shard_map/all_to_all | solution.py:777
  12.0 1.9 %collective-permute-start.2 = (f32[8,32,128]{2,1,0:T(8,128)S(1)}, f32[8,32,128]{2,1,0:T(8,128)S(1)}, u32[]{:S(2)}, u32[]{:S(2)}) collective-permute-start(f32[8,32,128]{2,1,0:T(8,128)S(1)} %copy-done.2), channel_id=1, source_target_pairs={{0,1},{1,0},{2,3},{3,2},{4,5},{5,4},{6,7},{7,6},{8,9},{9,8},{10,11... | collective-permute-start | bytes 393224 | tf_op jit(solution)/shard_map/ppermute | solution.py:738
  12.1 1.8 %collective-permute-start = (f32[8,32,128]{2,1,0:T(8,128)S(1)}, f32[8,32,128]{2,1,0:T(8,128)S(1)}, u32[]{:S(2)}, u32[]{:S(2)}) collective-permute-start(f32[8,32,128]{2,1,0:T(8,128)S(1)} %copy-done), channel_id=1, source_target_pairs={{0,1},{1,0},{2,3},{3,2},{4,5},{5,4},{6,7},{7,6},{8,9},{9,8},{10,11... | collective-permute-start | bytes 393224 | tf_op jit(solution)/shard_map/ppermute | solution.py:738
  12.6 1.3 %collective-permute-start.1 = (f32[8,32,128]{2,1,0:T(8,128)S(1)}, f32[8,32,128]{2,1,0:T(8,128)S(1)}, u32[]{:S(2)}, u32[]{:S(2)}) collective-permute-start(f32[8,32,128]{2,1,0:T(8,128)S(1)} %copy-done.1), channel_id=1, source_target_pairs={{0,1},{1,0},{2,3},{3,2},{4,5},{5,4},{6,7},{7,6},{8,9},{9,8},{10,11... | collective-permute-start | bytes 393224 | tf_op jit(solution)/shard_map/ppermute | solution.py:738
  12.6 0.7 %copy-start.3 = (s32[32,128]{1,0:T(8,128)S(1)}, s32[32,128]{1,0:T(8,128)}, u32[]{:S(2)}) copy-start(s32[32,128]{1,0:T(8,128)} %pilot_ref) | copy-start | bytes 49156
  24.9 4.7 %collective-permute-start.3 = (f32[3,8,8,128]{3,2,1,0:T(8,128)S(1)}, f32[3,8,8,128]{3,2,1,0:T(8,128)S(1)}, u32[]{:S(2)}, u32[]{:S(2)}) collective-permute-start(f32[3,8,8,128]{3,2,1,0:T(8,128)S(1)} %get-tuple-element.44), channel_id=1, source_target_pairs={{0,4},{8,12},{4,0},{12,8},{1,5},{9,13},{5,1},{13,9},{2,6},{10,14},... | collective-permute-start | bytes 294920 | tf_op jit(solution)/shard_map/ppermute | solution.py:790
  25.3 4.3 %collective-permute-start.4 = (f32[3,8,8,128]{3,2,1,0:T(8,128)S(1)}, f32[3,8,8,128]{3,2,1,0:T(8,128)S(1)}, u32[]{:S(2)}, u32[]{:S(2)}) collective-permute-start(f32[3,8,8,128]{3,2,1,0:T(8,128)S(1)} %get-tuple-element.45), channel_id=1, source_target_pairs={{4,8},{8,4},{5,9},{9,5},{6,10},{10,6},{7,11},{11,7},{20,24},{24,20... | collective-permute-start | bytes 294920 | tf_op jit(solution)/shard_map/ppermute | solution.py:791
  29.6 2.0 %collective-permute-start.6 = (f32[3,8,8,128]{3,2,1,0:T(8,128)S(1)}, f32[3,8,8,128]{3,2,1,0:T(8,128)S(1)}, u32[]{:S(2)}, u32[]{:S(2)}) collective-permute-start(f32[3,8,8,128]{3,2,1,0:T(8,128)S(1)} %collective-permute-done.3.refs_4_.refs_6_.refs_10_), channel_id=1, source_target_pairs={{0,1},{1,0},{2,3},{3,2},{4,5},{5,4},{6,7},{7,6},{8,9},{9,8},{10,11... | collective-permute-start | bytes 294920 | tf_op jit(solution)/shard_map/ppermute | solution.py:738
  29.6 2.0 %collective-permute-start.7 = (f32[3,8,8,128]{3,2,1,0:T(8,128)S(1)}, f32[3,8,8,128]{3,2,1,0:T(8,128)S(1)}, u32[]{:S(2)}, u32[]{:S(2)}) collective-permute-start(f32[3,8,8,128]{3,2,1,0:T(8,128)S(1)} %collective-permute-done.4.refs_5_.refs_7_.refs_11_), channel_id=1, source_target_pairs={{0,1},{1,0},{2,3},{3,2},{4,5},{5,4},{6,7},{7,6},{8,9},{9,8},{10,11... | collective-permute-start | bytes 294920 | tf_op jit(solution)/shard_map/ppermute | solution.py:738
  30.4 4.3 %collective-permute-start.5 = (f32[16,8,128]{2,1,0:T(8,128)S(1)}, f32[16,8,128]{2,1,0:T(8,128)S(1)}, u32[]{:S(2)}, u32[]{:S(2)}) collective-permute-start(f32[16,8,128]{2,1,0:T(8,128)S(1)} %shard_map.98), channel_id=1, source_target_pairs={{0,2},{2,0},{1,3},{3,1},{4,6},{6,4},{5,7},{7,5},{8,10},{10,8},{9,1... | collective-permute-start | bytes 196616 | tf_op jit(solution)/shard_map/ppermute | solution.py:805
  31.6 3.2 %collective-permute-start.8 = (f32[8,32,128]{2,1,0:T(8,128)S(1)}, f32[8,32,128]{2,1,0:T(8,128)S(1)}, u32[]{:S(2)}, u32[]{:S(2)}) collective-permute-start(f32[8,32,128]{2,1,0:T(8,128)S(1)} %get-tuple-element.43.refs_3_.refs_8_), channel_id=1, source_target_pairs={{0,1},{1,0},{2,3},{3,2},{4,5},{5,4},{6,7},{7,6},{8,9},{9,8},{10,11... | collective-permute-start | bytes 393224 | tf_op jit(solution)/shard_map/ppermute | solution.py:738
  34.8 1.3 %collective-permute-start.9 = (f32[16,8,128]{2,1,0:T(8,128)S(1)}, f32[16,8,128]{2,1,0:T(8,128)S(1)}, u32[]{:S(2)}, u32[]{:S(2)}) collective-permute-start(f32[16,8,128]{2,1,0:T(8,128)S(1)} %collective-permute-done.5.refs_14_), channel_id=1, source_target_pairs={{0,1},{1,0},{2,3},{3,2},{4,5},{5,4},{6,7},{7,6},{8,9},{9,8},{10,11... | collective-permute-start | bytes 196616 | tf_op jit(solution)/shard_map/ppermute | solution.py:738

commit v7 on v6

--- a/solution.py
+++ b/solution.py
@@ -507,7 +507,10 @@
         norm = jnp.zeros((8, LANES), jnp.float32)
         energy = jnp.zeros((8, LANES), jnp.float32)
         side_image = []
+        final = k == ITERS - 1
         for x, (d, sx, sy, sz) in zip(side_now, strip_terms):
+            if final:
+                break
             ax = d * x - sx * fore(x) - back(sx * x) - sy * right(x) - left(sy * x)
             ax = ax - sz * pltpu.roll(x, LANES - HALO, 1) - pltpu.roll(sz * x, HALO, 1)
             side_image.append(ax)
@@ -525,12 +528,15 @@
             if z:
                 av = av - wz[z - 1] * below
             av = av - wx[z] * vf - wx_back[z] * vb - wyz * vr - left(wyz * v) - wsz * side
-            image[z] = av
-            edge = wsz * v
-            for i, strip in enumerate(strips):
-                side_image[i] = side_image[i] - to_strip(strip, edge, z)
-            norm = norm + folded(v * v)
-            energy = energy + folded(v * av)
+            if final:
+                basis[ITERS, z, body, :] = av
+            else:
+                image[z] = av
+                edge = wsz * v
+                for i, strip in enumerate(strips):
+                    side_image[i] = side_image[i] - to_strip(strip, edge, z)
+                norm = norm + folded(v * v)
+                energy = energy + folded(v * av)
             if z < nz:
                 fall = (v - vf)[:span]
                 acc = acc + fall * grads[0, z]
@@ -545,12 +551,10 @@
             norm = norm + folded(x * x)
             energy = energy + folded(x * ax)
         sums.append((acc + back(acc_x) + left(acc_y))[inner])
-        norm = all_sum(norm)
-        alphas.append(safe_ratio(all_sum(energy), norm))
+        norm = all_sum(norm) if not final else jnp.zeros((1, 1), jnp.float32)
+        alphas.append(safe_ratio(all_sum(energy), norm) if not final else norm)
         gammas.append(safe_ratio(norm, norms[-1]) if k else jnp.zeros_like(norm))
         norms.append(norm)
-    for z in range(nz):
-        member(ITERS, z)
     own_rows = slice(top + HALO, top + span)
 
     dots = {}

time: 58.1 us -> 57.8 us (level)
  no operation moved by 1% of the time
where the time goes in v7:
time: 57.8 us; the launch traced here: 57.4 us
  Pallas kernels  19.5 us (34%)
  waiting for transfers between devices  13.3 us (23%)
  blocking collectives  12.2 us (21%)
  starting transfers between devices  10.9 us (19%)
  local copies, waits for them, and re-layouts  0.74 us (1%)
  between operations  0.74 us (1%)
    all_to_all x1, blocking collectives, on_device(): parts = lax.all_to_all(send, GRID_AXES, 0, 0, tiled=True)  12.2 us
    all_to_all x1, starting transfers between devices, on_device(): got = lax.all_to_all(payload, PEER_AXES, 0, 0, tiled=True)  7.4 us
    pallas_call x1, Pallas kernels, on_device(): kernel_call(functools.partial(basis_body, peers, len(sides) // 2), (shape...  6.12 us
    all_to_all x1, waiting for transfers between devices, on_device(): got = lax.all_to_all(payload, PEER_AXES, 0, 0, tiled=True)  6.01 us
    pallas_call x1, Pallas kernels, on_device(): kernel_call(functools.partial(source_body, capacity // LANES), (shape(nz,...  4.98 us
    pallas_call x1, Pallas kernels, on_device(): kernel_call(functools.partial(route_body, peers, capacity), shape(peers,...  3.89 us
    ppermute x1, waiting for transfers between devices, on_device(): near = lax.ppermute(near, 'cols', swap_pairs('cols', 0))  3.48 us
    pallas_call x1, Pallas kernels, on_device(): kernel_call(functools.partial(solve_body, devices // peers), (shape(nz, n...  3.03 us
  transfers between devices with their start and end apart: 11, of which 4 were waited for; matrix products, arithmetic and copies ran while one was open for 0% of the time, Pallas kernels for 3%

profile of v7, /device:TPU:0, one launch (start us, length us, event | category | flops | bytes accessed | tf_op | source)
XLA Modules:
  0.0 57.4 jit_solution(11506783849613859638)
XLA Ops:
  0.6 3.9 %shard_map.95 = f32[8,48,128]{2,1,0:T(8,128)} custom-call(s32[32,128]{1,0:T(8,128)} %bitcast.5, s32[32,128]{1,0:T(8,128)} %bitcast.6, f32[32,128]{1,0:T(8,128)} %bitcast.7, f32[32,128]{1,0:T(8,128)} %bitcast.8), custom_call_target="tpu_custom_call" | custom-call | bytes 15000000 | tf_op jit(solution)/shard_map/pallas_call | solution.py:771
  4.5 0.0 copy-start.2
  4.5 0.0 copy-start
  4.6 0.0 copy-start.1
  4.6 7.4 %all-to-all-start = ((f32[8,48,128]{2,1,0:T(8,128)}), f32[8,48,128]{2,1,0:T(8,128)S(1)}, u32[]{:S(2)}, u32[]{:S(2)}) async-start(f32[8,48,128]{2,1,0:T(8,128)} %shard_map.95), calls=%async_computation | async-start | bytes 393216 | tf_op jit(solution)/shard_map/all_to_all | solution.py:781
  12.0 0.0 copy-done.2
  12.0 0.1 collective-permute-start.2
  12.1 0.0 copy-done
  12.1 0.5 collective-permute-start
  12.6 0.0 copy-done.1
  12.6 0.1 collective-permute-start.1
  12.6 0.0 copy-start.3
  12.6 0.7 %copy-done.3 = s32[32,128]{1,0:T(8,128)S(1)} copy-done((s32[32,128]{1,0:T(8,128)S(1)}, s32[32,128]{1,0:T(8,128)}, u32[]{:S(2)}) %copy-start.3) | copy-done | bytes 16408
  13.4 0.5 shard_map.96
  13.8 0.0 collective-permute-done.2.refs_5_
  13.8 0.0 collective-permute-done.refs_3_
  13.9 0.0 collective-permute-done.1.refs_4_
  13.9 6.0 %all-to-all-done.got_ref = f32[8,48,128]{2,1,0:T(8,128)S(1)} async-done(((f32[8,48,128]{2,1,0:T(8,128)}), f32[8,48,128]{2,1,0:T(8,128)S(1)}, u32[]{:S(2)}, u32[]{:S(2)}) %all-to-all-start) | async-done | bytes 196640 | tf_op jit(solution)/shard_map/all_to_all | solution.py:781
  19.9 5.0 %shard_map.97 = (f32[8,32,128]{2,1,0:T(8,128)S(1)}, f32[3,8,8,128]{3,2,1,0:T(8,128)S(1)}, f32[3,8,8,128]{3,2,1,0:T(8,128)S(1)}) custom-call(f32[8,48,128]{2,1,0:T(8,128)S(1)} %all-to-all-done.got_ref, f32[8,32,128]{2,1,0:T(8,128)S(1)} %copy-done, f32[8,32,128]{2,1,0:T(8,128)S(1)} %copy-done.1, f32[8,32,128]{2,1,0:T(8,128)S(1)} %copy-done.2), custom_call_target="tpu_custom_call" | custom-call | bytes 18000000 | tf_op jit(solution)/shard_map/pallas_call | solution.py:789
  24.9 0.4 collective-permute-start.3
  25.3 0.8 %collective-permute-start.4 = (f32[3,8,8,128]{3,2,1,0:T(8,128)S(1)}, f32[3,8,8,128]{3,2,1,0:T(8,128)S(1)}, u32[]{:S(2)}, u32[]{:S(2)}) collective-permute-start(f32[3,8,8,128]{3,2,1,0:T(8,128)S(1)} %get-tuple-element.45), channel_id=1, source_target_pairs={{4,8},{8,4},{5,9},{9,5},{6,10},{10,6},{7,11},{11,7},{20,24},{24,20... | collective-permute-start | bytes 294920 | tf_op jit(solution)/shard_map/ppermute | solution.py:795
  26.1 3.5 %collective-permute-done.3.refs_4_.refs_6_.refs_10_ = f32[3,8,8,128]{3,2,1,0:T(8,128)S(1)} collective-permute-done((f32[3,8,8,128]{3,2,1,0:T(8,128)S(1)}, f32[3,8,8,128]{3,2,1,0:T(8,128)S(1)}, u32[]{:S(2)}, u32[]{:S(2)}) %collective-permute-start.3) | collective-permute-done | bytes 98336 | tf_op jit(solution)/shard_map/ppermute | solution.py:794
  29.6 0.0 collective-permute-start.6
  29.6 0.0 collective-permute-done.4.refs_5_.refs_7_.refs_11_
  29.6 0.5 collective-permute-start.7
  30.1 0.4 shard_map.98
  30.4 1.1 %collective-permute-start.5 = (f32[16,8,128]{2,1,0:T(8,128)S(1)}, f32[16,8,128]{2,1,0:T(8,128)S(1)}, u32[]{:S(2)}, u32[]{:S(2)}) collective-permute-start(f32[16,8,128]{2,1,0:T(8,128)S(1)} %shard_map.98), channel_id=1, source_target_pairs={{0,2},{2,0},{1,3},{3,1},{4,6},{6,4},{5,7},{7,5},{8,10},{10,8},{9,1... | collective-permute-start | bytes 196616 | tf_op jit(solution)/shard_map/ppermute | solution.py:809
  31.6 0.0 collective-permute-start.8
  31.6 0.0 collective-permute-done.6.refs_8_.refs_12_
  31.6 0.0 collective-permute-done.7.refs_9_.refs_13_
  31.6 0.6 %shard_map.99 = (f32[16,48,128]{2,1,0:T(8,128)S(1)}, f32[16,48,128]{2,1,0:T(8,128)S(1)}, f32[16,48,128]{2,1,0:T(8,128)S(1)}, f32[16,48,128]{2,1,0:T(8,128)S(1)},...) custom-call(f32[8,32,128]{2,1,0:T(8,128)S(1)} %copy-done, ...), custom_call_target="tpu_custom_call" | custom-call | bytes 9000000 | tf_op jit(solution)/shard_map/pallas_call | solution.py:812
  32.2 2.5 %collective-permute-done.5.refs_14_ = f32[16,8,128]{2,1,0:T(8,128)S(1)} collective-permute-done((f32[16,8,128]{2,1,0:T(8,128)S(1)}, f32[16,8,128]{2,1,0:T(8,128)S(1)}, u32[]{:S(2)}, u32[]{:S(2)}) %collective-permute-start.5) | collective-permute-done | bytes 65568 | tf_op jit(solution)/shard_map/ppermute | solution.py:809
  34.8 0.0 collective-permute-start.9
  34.8 0.0 collective-permute-done.8.refs_9_
  34.8 1.2 %collective-permute-done.9.refs_15_ = f32[16,8,128]{2,1,0:T(8,128)S(1)} collective-permute-done((f32[16,8,128]{2,1,0:T(8,128)S(1)}, f32[16,8,128]{2,1,0:T(8,128)S(1)}, u32[]{:S(2)}, u32[]{:S(2)}) %collective-permute-start.9) | collective-permute-done | bytes 65568 | tf_op jit(solution)/shard_map/ppermute | solution.py:742
  36.0 6.1 %shard_map.100 = (f32[8,8,32,128]{3,2,1,0:T(8,128)S(1)}, f32[16,8,128]{2,1,0:T(8,128)S(1)}) custom-call(f32[16,48,128]{2,1,0:T(8,128)S(1)} %get-tuple-element.61.refs_0_, f32[16,48,128]{2,1,0:T(8,128)S(1)} %get-tuple-element.62.refs_1_, f32[16,48,128]{2,1,0:T(8,128)S(1)} %get-tuple-element.63.refs_2_, f32[16,48,128]{2,1,0:T(8,128)S(1)} %get-tuple-element.64.refs_3_, ...), custom_call_target="tpu_custom_call" | custom-call | bytes 30000000 | tf_op jit(solution)/shard_map/pallas_call | solution.py:822
  42.2 12.2 %all_to_all.10.got_ref = f32[16,8,128]{2,1,0:T(8,128)S(1)} all-to-all(f32[16,8,128]{2,1,0:T(8,128)S(1)} %get-tuple-element.72), channel_id=1, replica_groups=mesh['groups'=2,'cols'=4,'rows'=2,'layers'=2] {'cols','rows','layers'}, dimensions={0} | all-to-all | bytes 131072 | tf_op jit(solution)/shard_map/all_to_all | solution.py:836
  54.4 3.0 %shard_map.101 = (f32[8,32,128]{2,1,0:T(8,128)}, f32[4,128]{1,0:T(4,128)}) custom-call(f32[16,8,128]{2,1,0:T(8,128)S(1)} %all_to_all.10.got_ref, f32[8,8,32,128]{3,2,1,0:T(8,128)S(1)} %get-tuple-element.73.own_ref), custom_call_target="tpu_custom_call" | custom-call | bytes 3000000 | tf_op jit(solution)/shard_map/pallas_call | solution.py:837
Async XLA Ops:
  4.5 7.4 %copy-start.2 = (f32[8,32,128]{2,1,0:T(8,128)S(1)}, f32[8,32,128]{2,1,0:T(8,128)}, u32[]{:S(2)}) copy-start(f32[8,32,128]{2,1,0:T(8,128)} %refs_2_.3) | copy-start | bytes 393220
  4.5 7.5 %copy-start = (f32[8,32,128]{2,1,0:T(8,128)S(1)}, f32[8,32,128]{2,1,0:T(8,128)}, u32[]{:S(2)}) copy-start(f32[8,32,128]{2,1,0:T(8,128)} %refs_0_.3) | copy-start | bytes 393220
  4.6 8.0 %copy-start.1 = (f32[8,32,128]{2,1,0:T(8,128)S(1)}, f32[8,32,128]{2,1,0:T(8,128)}, u32[]{:S(2)}) copy-start(f32[8,32,128]{2,1,0:T(8,128)} %refs_1_.3) | copy-start | bytes 393220
  4.6 15.3 %all-to-all-start = ((f32[8,48,128]{2,1,0:T(8,128)}), f32[8,48,128]{2,1,0:T(8,128)S(1)}, u32[]{:S(2)}, u32[]{:S(2)}) async-start(f32[8,48,128]{2,1,0:T(8,128)} %shard_map.95), calls=%async_computation | async-start | bytes 393216 | tf_op jit(solution)/shard_map/all_to_all | solution.py:781
  12.0 1.9 %collective-permute-start.2 = (f32[8,32,128]{2,1,0:T(8,128)S(1)}, f32[8,32,128]{2,1,0:T(8,128)S(1)}, u32[]{:S(2)}, u32[]{:S(2)}) collective-permute-start(f32[8,32,128]{2,1,0:T(8,128)S(1)} %copy-done.2), channel_id=1, source_target_pairs={{0,1},{1,0},{2,3},{3,2},{4,5},{5,4},{6,7},{7,6},{8,9},{9,8},{10,11... | collective-permute-start | bytes 393224 | tf_op jit(solution)/shard_map/ppermute | solution.py:742
  12.1 1.8 %collective-permute-start = (f32[8,32,128]{2,1,0:T(8,128)S(1)}, f32[8,32,128]{2,1,0:T(8,128)S(1)}, u32[]{:S(2)}, u32[]{:S(2)}) collective-permute-start(f32[8,32,128]{2,1,0:T(8,128)S(1)} %copy-done), channel_id=1, source_target_pairs={{0,1},{1,0},{2,3},{3,2},{4,5},{5,4},{6,7},{7,6},{8,9},{9,8},{10,11... | collective-permute-start | bytes 393224 | tf_op jit(solution)/shard_map/ppermute | solution.py:742
  12.6 1.3 %collective-permute-start.1 = (f32[8,32,128]{2,1,0:T(8,128)S(1)}, f32[8,32,128]{2,1,0:T(8,128)S(1)}, u32[]{:S(2)}, u32[]{:S(2)}) collective-permute-start(f32[8,32,128]{2,1,0:T(8,128)S(1)} %copy-done.1), channel_id=1, source_target_pairs={{0,1},{1,0},{2,3},{3,2},{4,5},{5,4},{6,7},{7,6},{8,9},{9,8},{10,11... | collective-permute-start | bytes 393224 | tf_op jit(solution)/shard_map/ppermute | solution.py:742
  12.6 0.7 %copy-start.3 = (s32[32,128]{1,0:T(8,128)S(1)}, s32[32,128]{1,0:T(8,128)}, u32[]{:S(2)}) copy-start(s32[32,128]{1,0:T(8,128)} %pilot_ref) | copy-start | bytes 49156
  24.9 4.7 %collective-permute-start.3 = (f32[3,8,8,128]{3,2,1,0:T(8,128)S(1)}, f32[3,8,8,128]{3,2,1,0:T(8,128)S(1)}, u32[]{:S(2)}, u32[]{:S(2)}) collective-permute-start(f32[3,8,8,128]{3,2,1,0:T(8,128)S(1)} %get-tuple-element.44), channel_id=1, source_target_pairs={{0,4},{8,12},{4,0},{12,8},{1,5},{9,13},{5,1},{13,9},{2,6},{10,14},... | collective-permute-start | bytes 294920 | tf_op jit(solution)/shard_map/ppermute | solution.py:794
  25.3 4.3 %collective-permute-start.4 = (f32[3,8,8,128]{3,2,1,0:T(8,128)S(1)}, f32[3,8,8,128]{3,2,1,0:T(8,128)S(1)}, u32[]{:S(2)}, u32[]{:S(2)}) collective-permute-start(f32[3,8,8,128]{3,2,1,0:T(8,128)S(1)} %get-tuple-element.45), channel_id=1, source_target_pairs={{4,8},{8,4},{5,9},{9,5},{6,10},{10,6},{7,11},{11,7},{20,24},{24,20... | collective-permute-start | bytes 294920 | tf_op jit(solution)/shard_map/ppermute | solution.py:795
  29.6 2.0 %collective-permute-start.6 = (f32[3,8,8,128]{3,2,1,0:T(8,128)S(1)}, f32[3,8,8,128]{3,2,1,0:T(8,128)S(1)}, u32[]{:S(2)}, u32[]{:S(2)}) collective-permute-start(f32[3,8,8,128]{3,2,1,0:T(8,128)S(1)} %collective-permute-done.3.refs_4_.refs_6_.refs_10_), channel_id=1, source_target_pairs={{0,1},{1,0},{2,3},{3,2},{4,5},{5,4},{6,7},{7,6},{8,9},{9,8},{10,11... | collective-permute-start | bytes 294920 | tf_op jit(solution)/shard_map/ppermute | solution.py:742
  29.6 2.0 %collective-permute-start.7 = (f32[3,8,8,128]{3,2,1,0:T(8,128)S(1)}, f32[3,8,8,128]{3,2,1,0:T(8,128)S(1)}, u32[]{:S(2)}, u32[]{:S(2)}) collective-permute-start(f32[3,8,8,128]{3,2,1,0:T(8,128)S(1)} %collective-permute-done.4.refs_5_.refs_7_.refs_11_), channel_id=1, source_target_pairs={{0,1},{1,0},{2,3},{3,2},{4,5},{5,4},{6,7},{7,6},{8,9},{9,8},{10,11... | collective-permute-start | bytes 294920 | tf_op jit(solution)/shard_map/ppermute | solution.py:742
  30.4 4.3 %collective-permute-start.5 = (f32[16,8,128]{2,1,0:T(8,128)S(1)}, f32[16,8,128]{2,1,0:T(8,128)S(1)}, u32[]{:S(2)}, u32[]{:S(2)}) collective-permute-start(f32[16,8,128]{2,1,0:T(8,128)S(1)} %shard_map.98), channel_id=1, source_target_pairs={{0,2},{2,0},{1,3},{3,1},{4,6},{6,4},{5,7},{7,5},{8,10},{10,8},{9,1... | collective-permute-start | bytes 196616 | tf_op jit(solution)/shard_map/ppermute | solution.py:809
  31.6 3.2 %collective-permute-start.8 = (f32[8,32,128]{2,1,0:T(8,128)S(1)}, f32[8,32,128]{2,1,0:T(8,128)S(1)}, u32[]{:S(2)}, u32[]{:S(2)}) collective-permute-start(f32[8,32,128]{2,1,0:T(8,128)S(1)} %get-tuple-element.43.refs_3_.refs_8_), channel_id=1, source_target_pairs={{0,1},{1,0},{2,3},{3,2},{4,5},{5,4},{6,7},{7,6},{8,9},{9,8},{10,11... | collective-permute-start | bytes 393224 | tf_op jit(solution)/shard_map/ppermute | solution.py:742
  34.8 1.3 %collective-permute-start.9 = (f32[16,8,128]{2,1,0:T(8,128)S(1)}, f32[16,8,128]{2,1,0:T(8,128)S(1)}, u32[]{:S(2)}, u32[]{:S(2)}) collective-permute-start(f32[16,8,128]{2,1,0:T(8,128)S(1)} %collective-permute-done.5.refs_14_), channel_id=1, source_target_pairs={{0,1},{1,0},{2,3},{3,2},{4,5},{5,4},{6,7},{7,6},{8,9},{9,8},{10,11... | collective-permute-start | bytes 196616 | tf_op jit(solution)/shard_map/ppermute | solution.py:742

commit v8 on v7

--- a/solution.py
+++ b/solution.py
@@ -580,10 +580,9 @@
         facts.append(entries)
 
     blocks_x = nx // 4
-    four = jnp.where(
-        lax.shift_right_logical(lane_iota(blocks_x, nx), 2) == row_iota(blocks_x, nx), 1.0, 0.0
-    )
-    sums = mm(four, jnp.concatenate(sums, axis=1), precision=EXACT)
+    sums = jnp.concatenate(sums, axis=1)
+    sums = sums + fore(sums)
+    sums = sums + pltpu.roll(sums, nx - 2, 0)
     spot = [spot_ref[r : r + 1, :] for r in range(blocks_x)]
     lane_hits = jnp.concatenate(
         [
@@ -598,18 +597,17 @@
     for k in range(ITERS):
         pair = sums[:, k * LANES : (k + 1) * LANES]
         pair = pair + pltpu.roll(pair, LANES - 1, 1)
-        for p in pieces_of(pair):
+        for p in halves_of(pair):
             values.append(
                 jnp.concatenate(
-                    [picked(row_hit[r], p[r : r + 1]) for r in range(blocks_x)], axis=1
+                    [picked(row_hit[r], p[4 * r : 4 * r + 1]) for r in range(blocks_x)], axis=1
                 )
             )
     dense = mm(jnp.concatenate(values, axis=0), lane_hits, NT)
     copies = send_ref.shape[0] // peers
     for k in range(ITERS):
-        at = 3 * k * peers
+        at = 2 * k * peers
         rows = dense[at : at + peers] + dense[at + peers : at + 2 * peers]
-        rows = rows + dense[at + 2 * peers : at + 3 * peers]
         rows = jnp.where(lane_iota(peers) < FACTS, rows, facts[k])
         if k < 2:
             slots = pltpu.roll(slots_ref[...], (1 - k) * (LANES - SLOTS) + FACTS, 1)

time: 57.8 us -> 57.7 us (level)
  no operation moved by 1% of the time
where the time goes in v8:
time: 57.7 us; the launch traced here: 57.3 us
  Pallas kernels  19.4 us (34%)
  waiting for transfers between devices  13.3 us (23%)
  blocking collectives  12.2 us (21%)
  starting transfers between devices  10.9 us (19%)
  local copies, waits for them, and re-layouts  0.74 us (1%)
  between operations  0.74 us (1%)
    all_to_all x1, blocking collectives, on_device(): parts = lax.all_to_all(send, GRID_AXES, 0, 0, tiled=True)  12.2 us
    all_to_all x1, starting transfers between devices, on_device(): got = lax.all_to_all(payload, PEER_AXES, 0, 0, tiled=True)  7.4 us
    pallas_call x1, Pallas kernels, on_device(): kernel_call(functools.partial(basis_body, peers, len(sides) // 2), (shape...  6.04 us
    all_to_all x1, waiting for transfers between devices, on_device(): got = lax.all_to_all(payload, PEER_AXES, 0, 0, tiled=True)  6.01 us
    pallas_call x1, Pallas kernels, on_device(): kernel_call(functools.partial(source_body, capacity // LANES), (shape(nz,...  4.98 us
    pallas_call x1, Pallas kernels, on_device(): kernel_call(functools.partial(route_body, peers, capacity), shape(peers,...  3.89 us
    ppermute x1, waiting for transfers between devices, on_device(): near = lax.ppermute(near, 'cols', swap_pairs('cols', 0))  3.48 us
    pallas_call x1, Pallas kernels, on_device(): kernel_call(functools.partial(solve_body, devices // peers), (shape(nz, n...  3.03 us
  transfers between devices with their start and end apart: 11, of which 4 were waited for; matrix products, arithmetic and copies ran while one was open for 0% of the time, Pallas kernels for 3%

profile of v8, /device:TPU:0, one launch (start us, length us, event | category | flops | bytes accessed | tf_op | source)
XLA Modules:
  0.0 57.3 jit_solution(8040988730450850719)
XLA Ops:
  0.6 3.9 %shard_map.95 = f32[8,48,128]{2,1,0:T(8,128)} custom-call(s32[32,128]{1,0:T(8,128)} %bitcast.5, s32[32,128]{1,0:T(8,128)} %bitcast.6, f32[32,128]{1,0:T(8,128)} %bitcast.7, f32[32,128]{1,0:T(8,128)} %bitcast.8), custom_call_target="tpu_custom_call" | custom-call | bytes 15000000 | tf_op jit(solution)/shard_map/pallas_call | solution.py:769
  4.5 0.0 copy-start.2
  4.5 0.0 copy-start
  4.6 0.0 copy-start.1
  4.6 7.4 %all-to-all-start = ((f32[8,48,128]{2,1,0:T(8,128)}), f32[8,48,128]{2,1,0:T(8,128)S(1)}, u32[]{:S(2)}, u32[]{:S(2)}) async-start(f32[8,48,128]{2,1,0:T(8,128)} %shard_map.95), calls=%async_computation | async-start | bytes 393216 | tf_op jit(solution)/shard_map/all_to_all | solution.py:779
  12.0 0.0 copy-done.2
  12.0 0.1 collective-permute-start.2
  12.1 0.0 copy-done
  12.1 0.5 collective-permute-start
  12.6 0.0 copy-done.1
  12.6 0.1 collective-permute-start.1
  12.6 0.0 copy-start.3
  12.6 0.7 %copy-done.3 = s32[32,128]{1,0:T(8,128)S(1)} copy-done((s32[32,128]{1,0:T(8,128)S(1)}, s32[32,128]{1,0:T(8,128)}, u32[]{:S(2)}) %copy-start.3) | copy-done | bytes 16408
  13.4 0.5 shard_map.96
  13.8 0.0 collective-permute-done.2.refs_5_
  13.8 0.0 collective-permute-done.refs_3_
  13.9 0.0 collective-permute-done.1.refs_4_
  13.9 6.0 %all-to-all-done.got_ref = f32[8,48,128]{2,1,0:T(8,128)S(1)} async-done(((f32[8,48,128]{2,1,0:T(8,128)}), f32[8,48,128]{2,1,0:T(8,128)S(1)}, u32[]{:S(2)}, u32[]{:S(2)}) %all-to-all-start) | async-done | bytes 196640 | tf_op jit(solution)/shard_map/all_to_all | solution.py:779
  19.9 5.0 %shard_map.97 = (f32[8,32,128]{2,1,0:T(8,128)S(1)}, f32[3,8,8,128]{3,2,1,0:T(8,128)S(1)}, f32[3,8,8,128]{3,2,1,0:T(8,128)S(1)}) custom-call(f32[8,48,128]{2,1,0:T(8,128)S(1)} %all-to-all-done.got_ref, f32[8,32,128]{2,1,0:T(8,128)S(1)} %copy-done, f32[8,32,128]{2,1,0:T(8,128)S(1)} %copy-done.1, f32[8,32,128]{2,1,0:T(8,128)S(1)} %copy-done.2), custom_call_target="tpu_custom_call" | custom-call | bytes 18000000 | tf_op jit(solution)/shard_map/pallas_call | solution.py:787
  24.9 0.4 collective-permute-start.3
  25.3 0.8 %collective-permute-start.4 = (f32[3,8,8,128]{3,2,1,0:T(8,128)S(1)}, f32[3,8,8,128]{3,2,1,0:T(8,128)S(1)}, u32[]{:S(2)}, u32[]{:S(2)}) collective-permute-start(f32[3,8,8,128]{3,2,1,0:T(8,128)S(1)} %get-tuple-element.45), channel_id=1, source_target_pairs={{4,8},{8,4},{5,9},{9,5},{6,10},{10,6},{7,11},{11,7},{20,24},{24,20... | collective-permute-start | bytes 294920 | tf_op jit(solution)/shard_map/ppermute | solution.py:793
  26.1 3.5 %collective-permute-done.3.refs_4_.refs_6_.refs_10_ = f32[3,8,8,128]{3,2,1,0:T(8,128)S(1)} collective-permute-done((f32[3,8,8,128]{3,2,1,0:T(8,128)S(1)}, f32[3,8,8,128]{3,2,1,0:T(8,128)S(1)}, u32[]{:S(2)}, u32[]{:S(2)}) %collective-permute-start.3) | collective-permute-done | bytes 98336 | tf_op jit(solution)/shard_map/ppermute | solution.py:792
  29.6 0.0 collective-permute-start.6
  29.6 0.0 collective-permute-done.4.refs_5_.refs_7_.refs_11_
  29.6 0.5 collective-permute-start.7
  30.1 0.4 shard_map.98
  30.4 1.1 %collective-permute-start.5 = (f32[16,8,128]{2,1,0:T(8,128)S(1)}, f32[16,8,128]{2,1,0:T(8,128)S(1)}, u32[]{:S(2)}, u32[]{:S(2)}) collective-permute-start(f32[16,8,128]{2,1,0:T(8,128)S(1)} %shard_map.98), channel_id=1, source_target_pairs={{0,2},{2,0},{1,3},{3,1},{4,6},{6,4},{5,7},{7,5},{8,10},{10,8},{9,1... | collective-permute-start | bytes 196616 | tf_op jit(solution)/shard_map/ppermute | solution.py:807
  31.6 0.0 collective-permute-start.8
  31.6 0.0 collective-permute-done.6.refs_8_.refs_12_
  31.6 0.0 collective-permute-done.7.refs_9_.refs_13_
  31.6 0.6 %shard_map.99 = (f32[16,48,128]{2,1,0:T(8,128)S(1)}, f32[16,48,128]{2,1,0:T(8,128)S(1)}, f32[16,48,128]{2,1,0:T(8,128)S(1)}, f32[16,48,128]{2,1,0:T(8,128)S(1)},...) custom-call(f32[8,32,128]{2,1,0:T(8,128)S(1)} %copy-done, ...), custom_call_target="tpu_custom_call" | custom-call | bytes 9000000 | tf_op jit(solution)/shard_map/pallas_call | solution.py:810
  32.2 2.5 %collective-permute-done.5.refs_14_ = f32[16,8,128]{2,1,0:T(8,128)S(1)} collective-permute-done((f32[16,8,128]{2,1,0:T(8,128)S(1)}, f32[16,8,128]{2,1,0:T(8,128)S(1)}, u32[]{:S(2)}, u32[]{:S(2)}) %collective-permute-start.5) | collective-permute-done | bytes 65568 | tf_op jit(solution)/shard_map/ppermute | solution.py:807
  34.8 0.0 collective-permute-start.9
  34.8 0.0 collective-permute-done.8.refs_9_
  34.8 1.2 %collective-permute-done.9.refs_15_ = f32[16,8,128]{2,1,0:T(8,128)S(1)} collective-permute-done((f32[16,8,128]{2,1,0:T(8,128)S(1)}, f32[16,8,128]{2,1,0:T(8,128)S(1)}, u32[]{:S(2)}, u32[]{:S(2)}) %collective-permute-start.9) | collective-permute-done | bytes 65568 | tf_op jit(solution)/shard_map/ppermute | solution.py:740
  36.0 6.0 %shard_map.100 = (f32[8,8,32,128]{3,2,1,0:T(8,128)S(1)}, f32[16,8,128]{2,1,0:T(8,128)S(1)}) custom-call(f32[16,48,128]{2,1,0:T(8,128)S(1)} %get-tuple-element.61.refs_0_, f32[16,48,128]{2,1,0:T(8,128)S(1)} %get-tuple-element.62.refs_1_, f32[16,48,128]{2,1,0:T(8,128)S(1)} %get-tuple-element.63.refs_2_, f32[16,48,128]{2,1,0:T(8,128)S(1)} %get-tuple-element.64.refs_3_, ...), custom_call_target="tpu_custom_call" | custom-call | bytes 30000000 | tf_op jit(solution)/shard_map/pallas_call | solution.py:820
  42.1 12.2 %all_to_all.10.got_ref = f32[16,8,128]{2,1,0:T(8,128)S(1)} all-to-all(f32[16,8,128]{2,1,0:T(8,128)S(1)} %get-tuple-element.72), channel_id=1, replica_groups=mesh['groups'=2,'cols'=4,'rows'=2,'layers'=2] {'cols','rows','layers'}, dimensions={0} | all-to-all | bytes 131072 | tf_op jit(solution)/shard_map/all_to_all | solution.py:834
  54.3 3.0 %shard_map.101 = (f32[8,32,128]{2,1,0:T(8,128)}, f32[4,128]{1,0:T(4,128)}) custom-call(f32[16,8,128]{2,1,0:T(8,128)S(1)} %all_to_all.10.got_ref, f32[8,8,32,128]{3,2,1,0:T(8,128)S(1)} %get-tuple-element.73.own_ref), custom_call_target="tpu_custom_call" | custom-call | bytes 3000000 | tf_op jit(solution)/shard_map/pallas_call | solution.py:835
Async XLA Ops:
  4.5 7.4 %copy-start.2 = (f32[8,32,128]{2,1,0:T(8,128)S(1)}, f32[8,32,128]{2,1,0:T(8,128)}, u32[]{:S(2)}) copy-start(f32[8,32,128]{2,1,0:T(8,128)} %refs_2_.3) | copy-start | bytes 393220
  4.5 7.5 %copy-start = (f32[8,32,128]{2,1,0:T(8,128)S(1)}, f32[8,32,128]{2,1,0:T(8,128)}, u32[]{:S(2)}) copy-start(f32[8,32,128]{2,1,0:T(8,128)} %refs_0_.3) | copy-start | bytes 393220
  4.6 8.0 %copy-start.1 = (f32[8,32,128]{2,1,0:T(8,128)S(1)}, f32[8,32,128]{2,1,0:T(8,128)}, u32[]{:S(2)}) copy-start(f32[8,32,128]{2,1,0:T(8,128)} %refs_1_.3) | copy-start | bytes 393220
  4.6 15.3 %all-to-all-start = ((f32[8,48,128]{2,1,0:T(8,128)}), f32[8,48,128]{2,1,0:T(8,128)S(1)}, u32[]{:S(2)}, u32[]{:S(2)}) async-start(f32[8,48,128]{2,1,0:T(8,128)} %shard_map.95), calls=%async_computation | async-start | bytes 393216 | tf_op jit(solution)/shard_map/all_to_all | solution.py:779
  12.0 1.9 %collective-permute-start.2 = (f32[8,32,128]{2,1,0:T(8,128)S(1)}, f32[8,32,128]{2,1,0:T(8,128)S(1)}, u32[]{:S(2)}, u32[]{:S(2)}) collective-permute-start(f32[8,32,128]{2,1,0:T(8,128)S(1)} %copy-done.2), channel_id=1, source_target_pairs={{0,1},{1,0},{2,3},{3,2},{4,5},{5,4},{6,7},{7,6},{8,9},{9,8},{10,11... | collective-permute-start | bytes 393224 | tf_op jit(solution)/shard_map/ppermute | solution.py:740
  12.1 1.8 %collective-permute-start = (f32[8,32,128]{2,1,0:T(8,128)S(1)}, f32[8,32,128]{2,1,0:T(8,128)S(1)}, u32[]{:S(2)}, u32[]{:S(2)}) collective-permute-start(f32[8,32,128]{2,1,0:T(8,128)S(1)} %copy-done), channel_id=1, source_target_pairs={{0,1},{1,0},{2,3},{3,2},{4,5},{5,4},{6,7},{7,6},{8,9},{9,8},{10,11... | collective-permute-start | bytes 393224 | tf_op jit(solution)/shard_map/ppermute | solution.py:740
  12.6 1.3 %collective-permute-start.1 = (f32[8,32,128]{2,1,0:T(8,128)S(1)}, f32[8,32,128]{2,1,0:T(8,128)S(1)}, u32[]{:S(2)}, u32[]{:S(2)}) collective-permute-start(f32[8,32,128]{2,1,0:T(8,128)S(1)} %copy-done.1), channel_id=1, source_target_pairs={{0,1},{1,0},{2,3},{3,2},{4,5},{5,4},{6,7},{7,6},{8,9},{9,8},{10,11... | collective-permute-start | bytes 393224 | tf_op jit(solution)/shard_map/ppermute | solution.py:740
  12.6 0.7 %copy-start.3 = (s32[32,128]{1,0:T(8,128)S(1)}, s32[32,128]{1,0:T(8,128)}, u32[]{:S(2)}) copy-start(s32[32,128]{1,0:T(8,128)} %pilot_ref) | copy-start | bytes 49156
  24.9 4.7 %collective-permute-start.3 = (f32[3,8,8,128]{3,2,1,0:T(8,128)S(1)}, f32[3,8,8,128]{3,2,1,0:T(8,128)S(1)}, u32[]{:S(2)}, u32[]{:S(2)}) collective-permute-start(f32[3,8,8,128]{3,2,1,0:T(8,128)S(1)} %get-tuple-element.44), channel_id=1, source_target_pairs={{0,4},{8,12},{4,0},{12,8},{1,5},{9,13},{5,1},{13,9},{2,6},{10,14},... | collective-permute-start | bytes 294920 | tf_op jit(solution)/shard_map/ppermute | solution.py:792
  25.3 4.3 %collective-permute-start.4 = (f32[3,8,8,128]{3,2,1,0:T(8,128)S(1)}, f32[3,8,8,128]{3,2,1,0:T(8,128)S(1)}, u32[]{:S(2)}, u32[]{:S(2)}) collective-permute-start(f32[3,8,8,128]{3,2,1,0:T(8,128)S(1)} %get-tuple-element.45), channel_id=1, source_target_pairs={{4,8},{8,4},{5,9},{9,5},{6,10},{10,6},{7,11},{11,7},{20,24},{24,20... | collective-permute-start | bytes 294920 | tf_op jit(solution)/shard_map/ppermute | solution.py:793
  29.6 2.0 %collective-permute-start.6 = (f32[3,8,8,128]{3,2,1,0:T(8,128)S(1)}, f32[3,8,8,128]{3,2,1,0:T(8,128)S(1)}, u32[]{:S(2)}, u32[]{:S(2)}) collective-permute-start(f32[3,8,8,128]{3,2,1,0:T(8,128)S(1)} %collective-permute-done.3.refs_4_.refs_6_.refs_10_), channel_id=1, source_target_pairs={{0,1},{1,0},{2,3},{3,2},{4,5},{5,4},{6,7},{7,6},{8,9},{9,8},{10,11... | collective-permute-start | bytes 294920 | tf_op jit(solution)/shard_map/ppermute | solution.py:740
  29.6 2.0 %collective-permute-start.7 = (f32[3,8,8,128]{3,2,1,0:T(8,128)S(1)}, f32[3,8,8,128]{3,2,1,0:T(8,128)S(1)}, u32[]{:S(2)}, u32[]{:S(2)}) collective-permute-start(f32[3,8,8,128]{3,2,1,0:T(8,128)S(1)} %collective-permute-done.4.refs_5_.refs_7_.refs_11_), channel_id=1, source_target_pairs={{0,1},{1,0},{2,3},{3,2},{4,5},{5,4},{6,7},{7,6},{8,9},{9,8},{10,11... | collective-permute-start | bytes 294920 | tf_op jit(solution)/shard_map/ppermute | solution.py:740
  30.4 4.3 %collective-permute-start.5 = (f32[16,8,128]{2,1,0:T(8,128)S(1)}, f32[16,8,128]{2,1,0:T(8,128)S(1)}, u32[]{:S(2)}, u32[]{:S(2)}) collective-permute-start(f32[16,8,128]{2,1,0:T(8,128)S(1)} %shard_map.98), channel_id=1, source_target_pairs={{0,2},{2,0},{1,3},{3,1},{4,6},{6,4},{5,7},{7,5},{8,10},{10,8},{9,1... | collective-permute-start | bytes 196616 | tf_op jit(solution)/shard_map/ppermute | solution.py:807
  31.6 3.2 %collective-permute-start.8 = (f32[8,32,128]{2,1,0:T(8,128)S(1)}, f32[8,32,128]{2,1,0:T(8,128)S(1)}, u32[]{:S(2)}, u32[]{:S(2)}) collective-permute-start(f32[8,32,128]{2,1,0:T(8,128)S(1)} %get-tuple-element.43.refs_3_.refs_8_), channel_id=1, source_target_pairs={{0,1},{1,0},{2,3},{3,2},{4,5},{5,4},{6,7},{7,6},{8,9},{9,8},{10,11... | collective-permute-start | bytes 393224 | tf_op jit(solution)/shard_map/ppermute | solution.py:740
  34.8 1.3 %collective-permute-start.9 = (f32[16,8,128]{2,1,0:T(8,128)S(1)}, f32[16,8,128]{2,1,0:T(8,128)S(1)}, u32[]{:S(2)}, u32[]{:S(2)}) collective-permute-start(f32[16,8,128]{2,1,0:T(8,128)S(1)} %collective-permute-done.5.refs_14_), channel_id=1, source_target_pairs={{0,1},{1,0},{2,3},{3,2},{4,5},{5,4},{6,7},{7,6},{8,9},{9,8},{10,11... | collective-permute-start | bytes 196616 | tf_op jit(solution)/shard_map/ppermute | solution.py:740

commit v9 on v7

--- a/solution.py
+++ b/solution.py
@@ -404,6 +404,7 @@
     inner = slice(HALO, span)
     top = HALO
     body = slice(top, top + width)
+    own_rows = slice(top + HALO, top + span)
     for k in range(ITERS):
         for z in range(planes):
             basis[k, z, :top, :] = jnp.zeros((top, LANES), jnp.float32)
@@ -524,12 +525,14 @@
             vf, vr = basis[k, z, top + 1 : top + 1 + width, :], right(v)
             vb = basis[k, z, top - 1 : top - 1 + width, :]
             wyz, wsz = wy[z], ws[z]
-            av = diag[z] * v - wz[z] * above
+            part = inner if final else slice(0, width)
+            av = diag[z, part, :] * v[part] - wz[z, part, :] * above[part]
             if z:
-                av = av - wz[z - 1] * below
-            av = av - wx[z] * vf - wx_back[z] * vb - wyz * vr - left(wyz * v) - wsz * side
+                av = av - wz[z - 1, part, :] * below[part]
+            av = av - wx[z, part, :] * vf[part] - wx_back[z, part, :] * vb[part]
+            av = av - wyz[part] * vr[part] - left(wyz[part] * v[part]) - wsz[part] * side[part]
             if final:
-                basis[ITERS, z, body, :] = av
+                basis[ITERS, z, own_rows, :] = av
             else:
                 image[z] = av
                 edge = wsz * v
@@ -555,11 +558,10 @@
         alphas.append(safe_ratio(all_sum(energy), norm) if not final else norm)
         gammas.append(safe_ratio(norm, norms[-1]) if k else jnp.zeros_like(norm))
         norms.append(norm)
-    own_rows = slice(top + HALO, top + span)
 
     dots = {}
     for i in range(ITERS + 1):
-        for j in range(i + 1):
+        for j in range(min(i + 1, ITERS)):
             acc = basis[i, 0, own_rows, :] * basis[j, 0, own_rows, :]
             for z in range(1, nz):
                 acc = acc + basis[i, z, own_rows, :] * basis[j, z, own_rows, :]

time: 57.8 us -> 57.9 us (level)
  no operation moved by 1% of the time
where the time goes in v9:
time: 57.9 us; the launch traced here: 57.5 us
  Pallas kernels  19.5 us (34%)
  waiting for transfers between devices  13.3 us (23%)
  blocking collectives  12.2 us (21%)
  starting transfers between devices  10.9 us (19%)
  local copies, waits for them, and re-layouts  0.74 us (1%)
  between operations  0.73 us (1%)
    all_to_all x1, blocking collectives, on_device(): parts = lax.all_to_all(send, GRID_AXES, 0, 0, tiled=True)  12.2 us
    all_to_all x1, starting transfers between devices, on_device(): got = lax.all_to_all(payload, PEER_AXES, 0, 0, tiled=True)  7.4 us
    pallas_call x1, Pallas kernels, on_device(): kernel_call(functools.partial(basis_body, peers, len(sides) // 2), (shape...  6.16 us
    all_to_all x1, waiting for transfers between devices, on_device(): got = lax.all_to_all(payload, PEER_AXES, 0, 0, tiled=True)  6.01 us
    pallas_call x1, Pallas kernels, on_device(): kernel_call(functools.partial(source_body, capacity // LANES), (shape(nz,...  4.98 us
    pallas_call x1, Pallas kernels, on_device(): kernel_call(functools.partial(route_body, peers, capacity), shape(peers,...  3.89 us
    ppermute x1, waiting for transfers between devices, on_device(): near = lax.ppermute(near, 'cols', swap_pairs('cols', 0))  3.48 us
    pallas_call x1, Pallas kernels, on_device(): kernel_call(functools.partial(solve_body, devices // peers), (shape(nz, n...  3.03 us
  transfers between devices with their start and end apart: 11, of which 4 were waited for; matrix products, arithmetic and copies ran while one was open for 0% of the time, Pallas kernels for 3%

profile of v9, /device:TPU:0, one launch (start us, length us, event | category | flops | bytes accessed | tf_op | source)
XLA Modules:
  0.0 57.5 jit_solution(11963937142454940065)
XLA Ops:
  0.6 3.9 %shard_map.95 = f32[8,48,128]{2,1,0:T(8,128)} custom-call(s32[32,128]{1,0:T(8,128)} %bitcast.5, s32[32,128]{1,0:T(8,128)} %bitcast.6, f32[32,128]{1,0:T(8,128)} %bitcast.7, f32[32,128]{1,0:T(8,128)} %bitcast.8), custom_call_target="tpu_custom_call" | custom-call | bytes 15000000 | tf_op jit(solution)/shard_map/pallas_call | solution.py:773
  4.5 0.0 copy-start.2
  4.5 0.0 copy-start
  4.6 0.0 copy-start.1
  4.6 7.4 %all-to-all-start = ((f32[8,48,128]{2,1,0:T(8,128)}), f32[8,48,128]{2,1,0:T(8,128)S(1)}, u32[]{:S(2)}, u32[]{:S(2)}) async-start(f32[8,48,128]{2,1,0:T(8,128)} %shard_map.95), calls=%async_computation | async-start | bytes 393216 | tf_op jit(solution)/shard_map/all_to_all | solution.py:783
  12.0 0.0 copy-done.2
  12.0 0.1 collective-permute-start.2
  12.1 0.0 copy-done
  12.1 0.5 collective-permute-start
  12.6 0.0 copy-done.1
  12.6 0.1 collective-permute-start.1
  12.6 0.0 copy-start.3
  12.6 0.7 %copy-done.3 = s32[32,128]{1,0:T(8,128)S(1)} copy-done((s32[32,128]{1,0:T(8,128)S(1)}, s32[32,128]{1,0:T(8,128)}, u32[]{:S(2)}) %copy-start.3) | copy-done | bytes 16408
  13.4 0.5 shard_map.96
  13.8 0.0 collective-permute-done.2.refs_5_
  13.8 0.0 collective-permute-done.refs_3_
  13.9 0.0 collective-permute-done.1.refs_4_
  13.9 6.0 %all-to-all-done.got_ref = f32[8,48,128]{2,1,0:T(8,128)S(1)} async-done(((f32[8,48,128]{2,1,0:T(8,128)}), f32[8,48,128]{2,1,0:T(8,128)S(1)}, u32[]{:S(2)}, u32[]{:S(2)}) %all-to-all-start) | async-done | bytes 196640 | tf_op jit(solution)/shard_map/all_to_all | solution.py:783
  19.9 5.0 %shard_map.97 = (f32[8,32,128]{2,1,0:T(8,128)S(1)}, f32[3,8,8,128]{3,2,1,0:T(8,128)S(1)}, f32[3,8,8,128]{3,2,1,0:T(8,128)S(1)}) custom-call(f32[8,48,128]{2,1,0:T(8,128)S(1)} %all-to-all-done.got_ref, f32[8,32,128]{2,1,0:T(8,128)S(1)} %copy-done, f32[8,32,128]{2,1,0:T(8,128)S(1)} %copy-done.1, f32[8,32,128]{2,1,0:T(8,128)S(1)} %copy-done.2), custom_call_target="tpu_custom_call" | custom-call | bytes 18000000 | tf_op jit(solution)/shard_map/pallas_call | solution.py:791
  24.9 0.4 collective-permute-start.3
  25.3 0.8 %collective-permute-start.4 = (f32[3,8,8,128]{3,2,1,0:T(8,128)S(1)}, f32[3,8,8,128]{3,2,1,0:T(8,128)S(1)}, u32[]{:S(2)}, u32[]{:S(2)}) collective-permute-start(f32[3,8,8,128]{3,2,1,0:T(8,128)S(1)} %get-tuple-element.45), channel_id=1, source_target_pairs={{4,8},{8,4},{5,9},{9,5},{6,10},{10,6},{7,11},{11,7},{20,24},{24,20... | collective-permute-start | bytes 294920 | tf_op jit(solution)/shard_map/ppermute | solution.py:797
  26.1 3.5 %collective-permute-done.3.refs_4_.refs_6_.refs_10_ = f32[3,8,8,128]{3,2,1,0:T(8,128)S(1)} collective-permute-done((f32[3,8,8,128]{3,2,1,0:T(8,128)S(1)}, f32[3,8,8,128]{3,2,1,0:T(8,128)S(1)}, u32[]{:S(2)}, u32[]{:S(2)}) %collective-permute-start.3) | collective-permute-done | bytes 98336 | tf_op jit(solution)/shard_map/ppermute | solution.py:796
  29.6 0.0 collective-permute-start.6
  29.6 0.0 collective-permute-done.4.refs_5_.refs_7_.refs_11_
  29.6 0.5 collective-permute-start.7
  30.1 0.4 shard_map.98
  30.4 1.1 %collective-permute-start.5 = (f32[16,8,128]{2,1,0:T(8,128)S(1)}, f32[16,8,128]{2,1,0:T(8,128)S(1)}, u32[]{:S(2)}, u32[]{:S(2)}) collective-permute-start(f32[16,8,128]{2,1,0:T(8,128)S(1)} %shard_map.98), channel_id=1, source_target_pairs={{0,2},{2,0},{1,3},{3,1},{4,6},{6,4},{5,7},{7,5},{8,10},{10,8},{9,1... | collective-permute-start | bytes 196616 | tf_op jit(solution)/shard_map/ppermute | solution.py:811
  31.6 0.0 collective-permute-start.8
  31.6 0.0 collective-permute-done.6.refs_8_.refs_12_
  31.6 0.0 collective-permute-done.7.refs_9_.refs_13_
  31.6 0.6 %shard_map.99 = (f32[16,48,128]{2,1,0:T(8,128)S(1)}, f32[16,48,128]{2,1,0:T(8,128)S(1)}, f32[16,48,128]{2,1,0:T(8,128)S(1)}, f32[16,48,128]{2,1,0:T(8,128)S(1)},...) custom-call(f32[8,32,128]{2,1,0:T(8,128)S(1)} %copy-done, ...), custom_call_target="tpu_custom_call" | custom-call | bytes 9000000 | tf_op jit(solution)/shard_map/pallas_call | solution.py:814
  32.2 2.5 %collective-permute-done.5.refs_14_ = f32[16,8,128]{2,1,0:T(8,128)S(1)} collective-permute-done((f32[16,8,128]{2,1,0:T(8,128)S(1)}, f32[16,8,128]{2,1,0:T(8,128)S(1)}, u32[]{:S(2)}, u32[]{:S(2)}) %collective-permute-start.5) | collective-permute-done | bytes 65568 | tf_op jit(solution)/shard_map/ppermute | solution.py:811
  34.8 0.0 collective-permute-start.9
  34.8 0.0 collective-permute-done.8.refs_9_
  34.8 1.2 %collective-permute-done.9.refs_15_ = f32[16,8,128]{2,1,0:T(8,128)S(1)} collective-permute-done((f32[16,8,128]{2,1,0:T(8,128)S(1)}, f32[16,8,128]{2,1,0:T(8,128)S(1)}, u32[]{:S(2)}, u32[]{:S(2)}) %collective-permute-start.9) | collective-permute-done | bytes 65568 | tf_op jit(solution)/shard_map/ppermute | solution.py:744
  36.0 6.2 %shard_map.100 = (f32[8,8,32,128]{3,2,1,0:T(8,128)S(1)}, f32[16,8,128]{2,1,0:T(8,128)S(1)}) custom-call(f32[16,48,128]{2,1,0:T(8,128)S(1)} %get-tuple-element.61.refs_0_, f32[16,48,128]{2,1,0:T(8,128)S(1)} %get-tuple-element.62.refs_1_, f32[16,48,128]{2,1,0:T(8,128)S(1)} %get-tuple-element.63.refs_2_, f32[16,48,128]{2,1,0:T(8,128)S(1)} %get-tuple-element.64.refs_3_, ...), custom_call_target="tpu_custom_call" | custom-call | bytes 30000000 | tf_op jit(solution)/shard_map/pallas_call | solution.py:824
  42.2 12.2 %all_to_all.10.got_ref = f32[16,8,128]{2,1,0:T(8,128)S(1)} all-to-all(f32[16,8,128]{2,1,0:T(8,128)S(1)} %get-tuple-element.72), channel_id=1, replica_groups=mesh['groups'=2,'cols'=4,'rows'=2,'layers'=2] {'cols','rows','layers'}, dimensions={0} | all-to-all | bytes 131072 | tf_op jit(solution)/shard_map/all_to_all | solution.py:838
  54.4 3.0 %shard_map.101 = (f32[8,32,128]{2,1,0:T(8,128)}, f32[4,128]{1,0:T(4,128)}) custom-call(f32[16,8,128]{2,1,0:T(8,128)S(1)} %all_to_all.10.got_ref, f32[8,8,32,128]{3,2,1,0:T(8,128)S(1)} %get-tuple-element.73.own_ref), custom_call_target="tpu_custom_call" | custom-call | bytes 3000000 | tf_op jit(solution)/shard_map/pallas_call | solution.py:839
Async XLA Ops:
  4.5 7.4 %copy-start.2 = (f32[8,32,128]{2,1,0:T(8,128)S(1)}, f32[8,32,128]{2,1,0:T(8,128)}, u32[]{:S(2)}) copy-start(f32[8,32,128]{2,1,0:T(8,128)} %refs_2_.3) | copy-start | bytes 393220
  4.5 7.5 %copy-start = (f32[8,32,128]{2,1,0:T(8,128)S(1)}, f32[8,32,128]{2,1,0:T(8,128)}, u32[]{:S(2)}) copy-start(f32[8,32,128]{2,1,0:T(8,128)} %refs_0_.3) | copy-start | bytes 393220
  4.6 8.0 %copy-start.1 = (f32[8,32,128]{2,1,0:T(8,128)S(1)}, f32[8,32,128]{2,1,0:T(8,128)}, u32[]{:S(2)}) copy-start(f32[8,32,128]{2,1,0:T(8,128)} %refs_1_.3) | copy-start | bytes 393220
  4.6 15.3 %all-to-all-start = ((f32[8,48,128]{2,1,0:T(8,128)}), f32[8,48,128]{2,1,0:T(8,128)S(1)}, u32[]{:S(2)}, u32[]{:S(2)}) async-start(f32[8,48,128]{2,1,0:T(8,128)} %shard_map.95), calls=%async_computation | async-start | bytes 393216 | tf_op jit(solution)/shard_map/all_to_all | solution.py:783
  12.0 1.9 %collective-permute-start.2 = (f32[8,32,128]{2,1,0:T(8,128)S(1)}, f32[8,32,128]{2,1,0:T(8,128)S(1)}, u32[]{:S(2)}, u32[]{:S(2)}) collective-permute-start(f32[8,32,128]{2,1,0:T(8,128)S(1)} %copy-done.2), channel_id=1, source_target_pairs={{0,1},{1,0},{2,3},{3,2},{4,5},{5,4},{6,7},{7,6},{8,9},{9,8},{10,11... | collective-permute-start | bytes 393224 | tf_op jit(solution)/shard_map/ppermute | solution.py:744
  12.1 1.8 %collective-permute-start = (f32[8,32,128]{2,1,0:T(8,128)S(1)}, f32[8,32,128]{2,1,0:T(8,128)S(1)}, u32[]{:S(2)}, u32[]{:S(2)}) collective-permute-start(f32[8,32,128]{2,1,0:T(8,128)S(1)} %copy-done), channel_id=1, source_target_pairs={{0,1},{1,0},{2,3},{3,2},{4,5},{5,4},{6,7},{7,6},{8,9},{9,8},{10,11... | collective-permute-start | bytes 393224 | tf_op jit(solution)/shard_map/ppermute | solution.py:744
  12.6 1.3 %collective-permute-start.1 = (f32[8,32,128]{2,1,0:T(8,128)S(1)}, f32[8,32,128]{2,1,0:T(8,128)S(1)}, u32[]{:S(2)}, u32[]{:S(2)}) collective-permute-start(f32[8,32,128]{2,1,0:T(8,128)S(1)} %copy-done.1), channel_id=1, source_target_pairs={{0,1},{1,0},{2,3},{3,2},{4,5},{5,4},{6,7},{7,6},{8,9},{9,8},{10,11... | collective-permute-start | bytes 393224 | tf_op jit(solution)/shard_map/ppermute | solution.py:744
  12.6 0.7 %copy-start.3 = (s32[32,128]{1,0:T(8,128)S(1)}, s32[32,128]{1,0:T(8,128)}, u32[]{:S(2)}) copy-start(s32[32,128]{1,0:T(8,128)} %pilot_ref) | copy-start | bytes 49156
  24.9 4.7 %collective-permute-start.3 = (f32[3,8,8,128]{3,2,1,0:T(8,128)S(1)}, f32[3,8,8,128]{3,2,1,0:T(8,128)S(1)}, u32[]{:S(2)}, u32[]{:S(2)}) collective-permute-start(f32[3,8,8,128]{3,2,1,0:T(8,128)S(1)} %get-tuple-element.44), channel_id=1, source_target_pairs={{0,4},{8,12},{4,0},{12,8},{1,5},{9,13},{5,1},{13,9},{2,6},{10,14},... | collective-permute-start | bytes 294920 | tf_op jit(solution)/shard_map/ppermute | solution.py:796
  25.3 4.3 %collective-permute-start.4 = (f32[3,8,8,128]{3,2,1,0:T(8,128)S(1)}, f32[3,8,8,128]{3,2,1,0:T(8,128)S(1)}, u32[]{:S(2)}, u32[]{:S(2)}) collective-permute-start(f32[3,8,8,128]{3,2,1,0:T(8,128)S(1)} %get-tuple-element.45), channel_id=1, source_target_pairs={{4,8},{8,4},{5,9},{9,5},{6,10},{10,6},{7,11},{11,7},{20,24},{24,20... | collective-permute-start | bytes 294920 | tf_op jit(solution)/shard_map/ppermute | solution.py:797
  29.6 2.0 %collective-permute-start.6 = (f32[3,8,8,128]{3,2,1,0:T(8,128)S(1)}, f32[3,8,8,128]{3,2,1,0:T(8,128)S(1)}, u32[]{:S(2)}, u32[]{:S(2)}) collective-permute-start(f32[3,8,8,128]{3,2,1,0:T(8,128)S(1)} %collective-permute-done.3.refs_4_.refs_6_.refs_10_), channel_id=1, source_target_pairs={{0,1},{1,0},{2,3},{3,2},{4,5},{5,4},{6,7},{7,6},{8,9},{9,8},{10,11... | collective-permute-start | bytes 294920 | tf_op jit(solution)/shard_map/ppermute | solution.py:744
  29.6 2.0 %collective-permute-start.7 = (f32[3,8,8,128]{3,2,1,0:T(8,128)S(1)}, f32[3,8,8,128]{3,2,1,0:T(8,128)S(1)}, u32[]{:S(2)}, u32[]{:S(2)}) collective-permute-start(f32[3,8,8,128]{3,2,1,0:T(8,128)S(1)} %collective-permute-done.4.refs_5_.refs_7_.refs_11_), channel_id=1, source_target_pairs={{0,1},{1,0},{2,3},{3,2},{4,5},{5,4},{6,7},{7,6},{8,9},{9,8},{10,11... | collective-permute-start | bytes 294920 | tf_op jit(solution)/shard_map/ppermute | solution.py:744
  30.4 4.3 %collective-permute-start.5 = (f32[16,8,128]{2,1,0:T(8,128)S(1)}, f32[16,8,128]{2,1,0:T(8,128)S(1)}, u32[]{:S(2)}, u32[]{:S(2)}) collective-permute-start(f32[16,8,128]{2,1,0:T(8,128)S(1)} %shard_map.98), channel_id=1, source_target_pairs={{0,2},{2,0},{1,3},{3,1},{4,6},{6,4},{5,7},{7,5},{8,10},{10,8},{9,1... | collective-permute-start | bytes 196616 | tf_op jit(solution)/shard_map/ppermute | solution.py:811
  31.6 3.2 %collective-permute-start.8 = (f32[8,32,128]{2,1,0:T(8,128)S(1)}, f32[8,32,128]{2,1,0:T(8,128)S(1)}, u32[]{:S(2)}, u32[]{:S(2)}) collective-permute-start(f32[8,32,128]{2,1,0:T(8,128)S(1)} %get-tuple-element.43.refs_3_.refs_8_), channel_id=1, source_target_pairs={{0,1},{1,0},{2,3},{3,2},{4,5},{5,4},{6,7},{7,6},{8,9},{9,8},{10,11... | collective-permute-start | bytes 393224 | tf_op jit(solution)/shard_map/ppermute | solution.py:744
  34.8 1.3 %collective-permute-start.9 = (f32[16,8,128]{2,1,0:T(8,128)S(1)}, f32[16,8,128]{2,1,0:T(8,128)S(1)}, u32[]{:S(2)}, u32[]{:S(2)}) collective-permute-start(f32[16,8,128]{2,1,0:T(8,128)S(1)} %collective-permute-done.5.refs_14_), channel_id=1, source_target_pairs={{0,1},{1,0},{2,3},{3,2},{4,5},{5,4},{6,7},{7,6},{8,9},{9,8},{10,11... | collective-permute-start | bytes 196616 | tf_op jit(solution)/shard_map/ppermute | solution.py:744
